TPU v7x, 32 devices: a whole 2x2x4 slice. The times are simulated.
32 devices in a mesh: fsdp: 8 (over z, core), seq: 4 (over y, x).
Axes of the slice: x: 2, y: 2, z: 4, core: 2. Of those that a mesh axis runs over, the one named last changes fastest.
Arguments:
- tokens: bfloat16 [4096, 1024], P(('fsdp', 'seq')), may hold values from -6 to 6
- segment_ids: int32 [4096], P('fsdp'), may hold values from -1 to 1, as said below
- first_gain: bfloat16 [1024], P('fsdp'), may hold values from 0.25 to 1.75
- first_bias: bfloat16 [1024], P('fsdp'), may hold values from -3 to 3
- input_weight: bfloat16 [1024, 3072], P('fsdp'), may hold values from -0.1875 to 0.1875
- query_bias: bfloat16 [1024], P('fsdp'), may hold values from -3 to 3
- value_bias: bfloat16 [1024], P('fsdp'), may hold values from -3 to 3
- output_weight: bfloat16 [1024, 1024], P('fsdp'), may hold values from -0.75 to 0.75
- output_bias: bfloat16 [1024], P('fsdp'), may hold values from -3 to 3
- scale_one: bfloat16 [1024], P('fsdp'), may hold values from 0.5 to 2
- second_gain: bfloat16 [1024], P('fsdp'), may hold values from 0.25 to 1.75
- second_bias: bfloat16 [1024], P('fsdp'), may hold values from -3 to 3
- up_weight: bfloat16 [1024, 4096], P('fsdp'), may hold values from -0.1875 to 0.1875
- up_bias: bfloat16 [4096], P('fsdp'), may hold values from -3 to 3
- down_weight: bfloat16 [4096, 1024], P('fsdp'), may hold values from -0.09375 to 0.09375
- down_bias: bfloat16 [1024], P('fsdp'), may hold values from -3 to 3
- scale_two: bfloat16 [1024], P('fsdp'), may hold values from 0.5 to 2
- out_grad: bfloat16 [4096, 1024], P(('fsdp', 'seq')), may hold values from -6 to 6
Outputs:
- layer_out: bfloat16 [4096, 1024], P(('fsdp', 'seq'))
- tokens_grad: bfloat16 [4096, 1024], P(('fsdp', 'seq'))
- first_gain_grad: float32 [1024], P('fsdp')
- first_bias_grad: float32 [1024], P('fsdp')
- input_weight_grad: float32 [1024, 3072], P('fsdp')
- query_bias_grad: float32 [1024], P('fsdp')
- value_bias_grad: float32 [1024], P('fsdp')
- output_weight_grad: float32 [1024, 1024], P('fsdp')
- output_bias_grad: float32 [1024], P('fsdp')
- scale_one_grad: float32 [1024], P('fsdp')
- second_gain_grad: float32 [1024], P('fsdp')
- second_bias_grad: float32 [1024], P('fsdp')
- up_weight_grad: float32 [1024, 4096], P('fsdp')
- up_bias_grad: float32 [4096], P('fsdp')
- down_weight_grad: float32 [4096, 1024], P('fsdp')
- down_bias_grad: float32 [1024], P('fsdp')
- scale_two_grad: float32 [1024], P('fsdp')
Inputs may be any that keep to these rules, and one draw needn't show every extreme that they name: `segment_ids`: each group of 512 consecutive slots holds two images and then padding: one image fills all but fewer than 128 of the group's slots, the other has 1 to 64 tokens and stands before or after it; the group ends with 1 to 63 padding slots marked -1; the first image in the group has id 0, the second id 1.
All inputs are finite; a program needn't handle non-finite values.
Results may differ from a plain program's by a relative error of at most 0.018.
Values may be sent and summed in bfloat16 or wider, within the bound.
No kernel may reach another device: no remote copies, remote signals or barrier semaphores. Data moves between devices by JAX's collectives and lax.ppermute only.
A program may use at most 192 MiB of HBM per device.

v0:
```python
import math

import jax
import jax.numpy as jnp
from jax import lax
from jax.sharding import PartitionSpec as P

HEADS = 16
HEAD_DIM = 64


epsilon = 1e-06
masked_value = -1000000000.0


def product(left, right):
    return jnp.dot(left, right, preferred_element_type=jnp.float32)


def product_left(left, right):
    return lax.dot_general(
        left, right, (((0,), (0,)), ((), ())), preferred_element_type=jnp.float32
    )


def product_right(left, right):
    return lax.dot_general(
        left, right, (((1,), (1,)), ((), ())), preferred_element_type=jnp.float32
    )


def normalize(values):
    center = values - jnp.mean(values, axis=1, keepdims=True)
    spread = lax.rsqrt(jnp.mean(center * center, axis=1, keepdims=True) + epsilon)
    return (center * spread, spread)


def normalize_back(grad_normed, normed, spread):
    return spread * (
        grad_normed
        - jnp.mean(grad_normed, axis=1, keepdims=True)
        - normed * jnp.mean(grad_normed * normed, axis=1, keepdims=True)
    )


def gelu_pair(before):
    normal_cdf = 0.5 * (1.0 + lax.erf(before * (1.0 / math.sqrt(2.0))))
    density = jnp.exp(-0.5 * before * before) * (1.0 / math.sqrt(2.0 * math.pi))
    return (before * normal_cdf, normal_cdf + before * density)


def masked_scores(query_rows, key_rows, row_segments, segments):
    products = product_right(query_rows, key_rows) * HEAD_DIM ** (-0.5)
    return jnp.where(row_segments[:, None] == segments[None, :], products, masked_value)


def attend_head(queries, key_rows, value_rows, segments, block_rows):

    def one_block(number):
        first_row = number * block_rows
        query_rows = lax.dynamic_slice_in_dim(queries, first_row, block_rows, 0)
        row_segments = lax.dynamic_slice_in_dim(segments, first_row, block_rows, 0)
        scores = masked_scores(query_rows, key_rows, row_segments, segments)
        highest = jnp.max(scores, axis=1, keepdims=True)
        powers = jnp.exp(scores - highest)
        totals = jnp.sum(powers, axis=1, keepdims=True)
        softmax_weights = (powers / totals).astype(jnp.bfloat16)
        result = product(softmax_weights, value_rows).astype(jnp.bfloat16)
        return (result, (highest + jnp.log(totals))[:, 0])

    outputs, logsums = lax.map(one_block, jnp.arange(queries.shape[0] // block_rows))
    return (outputs.reshape(queries.shape[0], -1), logsums.reshape(-1))


def attend_back(queries, key_rows, value_rows, segments, logsums, grad_out, block_rows):

    def one_block(carry, number):
        grad_keys, grad_values = carry
        first_row = number * block_rows
        query_rows = lax.dynamic_slice_in_dim(queries, first_row, block_rows, 0)
        row_segments = lax.dynamic_slice_in_dim(segments, first_row, block_rows, 0)
        row_logsums = lax.dynamic_slice_in_dim(logsums, first_row, block_rows, 0)
        row_grads = lax.dynamic_slice_in_dim(grad_out, first_row, block_rows, 0)
        scores = masked_scores(query_rows, key_rows, row_segments, segments)
        softmax_weights = jnp.exp(scores - row_logsums[:, None])
        grad_values = grad_values + product_left(softmax_weights.astype(jnp.bfloat16), row_grads)
        grad_weights = product_right(row_grads, value_rows)
        row_dots = jnp.sum(softmax_weights * grad_weights, axis=1, keepdims=True)
        grad_scores = (softmax_weights * (grad_weights - row_dots)).astype(jnp.bfloat16)
        grad_rows = product(grad_scores, key_rows) * HEAD_DIM ** (-0.5)
        grad_keys = grad_keys + product_left(grad_scores, query_rows) * HEAD_DIM ** (-0.5)
        return ((grad_keys, grad_values), grad_rows)

    zeros_block = jnp.zeros(key_rows.shape, jnp.float32)
    (grad_keys, grad_values), grad_queries = lax.scan(
        one_block, (zeros_block, zeros_block), jnp.arange(queries.shape[0] // block_rows)
    )
    return (grad_queries.reshape(queries.shape[0], -1), grad_keys, grad_values)


def unpack_rows(gathered, widths):
    pieces = []
    offset = 0
    for width in widths:
        pieces.append(gathered[:, offset : offset + width].reshape(-1).astype(jnp.float32))
        offset += width
    return pieces


def term_rows(left, right):
    return product_left(left, right)


def body(
    tokens,
    segment_ids,
    first_gain,
    first_bias,
    input_weight,
    query_bias,
    value_bias,
    output_weight,
    output_bias,
    scale_one,
    second_gain,
    second_bias,
    up_weight,
    up_bias,
    down_weight,
    down_bias,
    scale_two,
    out_grad,
):
    fsdp_count = lax.axis_size("fsdp")
    local_vectors = (
        first_gain,
        first_bias,
        query_bias,
        value_bias,
        output_bias,
        scale_one,
        second_gain,
        second_bias,
        up_bias,
        down_bias,
        scale_two,
    )
    local_widths = [member.shape[0] for member in local_vectors]
    gathered = lax.all_gather(jnp.concatenate(local_vectors)[None, :], "fsdp", axis=0, tiled=True)
    (
        gain_one,
        offset_one,
        bias_query,
        bias_value,
        bias_output,
        factor_one,
        gain_two,
        offset_two,
        bias_up,
        bias_down,
        factor_two,
    ) = unpack_rows(gathered, local_widths)
    full_input, full_output, full_up, full_down = (
        lax.all_gather(input_weight, "fsdp", axis=0, tiled=True),
        lax.all_gather(output_weight, "fsdp", axis=0, tiled=True),
        lax.all_gather(up_weight, "fsdp", axis=0, tiled=True),
        lax.all_gather(down_weight, "fsdp", axis=0, tiled=True),
    )
    tok_rows = tokens.shape[0]
    seq_index = lax.axis_index("seq")
    inputs = tokens.astype(jnp.float32)
    normed_one, spread_one = normalize(inputs)
    hidden_one = (normed_one * gain_one + offset_one).astype(jnp.bfloat16)
    zeros_key = jnp.zeros((HEADS, HEAD_DIM), jnp.float32)
    bias_full = jnp.stack(
        [bias_query.reshape(HEADS, HEAD_DIM), zeros_key, bias_value.reshape(HEADS, HEAD_DIM)],
        axis=1,
    ).reshape(-1)
    triple = (product(hidden_one, full_input) + bias_full).astype(jnp.bfloat16)
    by_head = lax.all_to_all(triple, "seq", split_axis=1, concat_axis=0, tiled=True)
    slots = by_head.shape[0]
    block_rows = min(512, slots)
    local_heads = by_head.shape[1] // (3 * HEAD_DIM)
    head_outputs = []
    head_logsums = []
    for head in range(local_heads):
        base = head * 3 * HEAD_DIM
        result, logsum = attend_head(
            by_head[:, base : base + HEAD_DIM],
            by_head[:, base + HEAD_DIM : base + 2 * HEAD_DIM],
            by_head[:, base + 2 * HEAD_DIM : base + 3 * HEAD_DIM],
            segment_ids,
            block_rows,
        )
        head_outputs.append(result)
        head_logsums.append(logsum)
    attended = lax.all_to_all(
        jnp.concatenate(head_outputs, axis=1), "seq", split_axis=0, concat_axis=1, tiled=True
    )
    branch_one = product(attended, full_output) + bias_output
    middle = inputs + factor_one * branch_one
    normed_two, spread_two = normalize(middle)
    hidden_two = (normed_two * gain_two + offset_two).astype(jnp.bfloat16)
    before = product(hidden_two, full_up) + bias_up
    activated_full, slope = gelu_pair(before)
    activated = activated_full.astype(jnp.bfloat16)
    branch_two = product(activated, full_down) + bias_down
    layer_out = (middle + factor_two * branch_two).astype(jnp.bfloat16)
    own_segments = lax.dynamic_slice_in_dim(segment_ids, seq_index * tok_rows, tok_rows, 0)
    grad = out_grad.astype(jnp.float32) * (own_segments >= 0).astype(jnp.float32)[:, None]
    back_input, back_output, back_up, back_down = (full_input, full_output, full_up, full_down)
    grad_factor_two = jnp.sum(grad * branch_two, axis=0)
    grad_two = (grad * factor_two).astype(jnp.bfloat16)
    grad_bias_down = jnp.sum(grad_two.astype(jnp.float32), axis=0)
    grad_before = (product_right(grad_two, back_down) * slope).astype(jnp.bfloat16)
    grad_bias_up = jnp.sum(grad_before.astype(jnp.float32), axis=0)
    grad_hidden_two = product_right(grad_before, back_up)
    grad_gain_two = jnp.sum(grad_hidden_two * normed_two, axis=0)
    grad_offset_two = jnp.sum(grad_hidden_two, axis=0)
    grad_middle = grad + normalize_back(grad_hidden_two * gain_two, normed_two, spread_two)
    grad_factor_one = jnp.sum(grad_middle * branch_one, axis=0)
    grad_one = (grad_middle * factor_one).astype(jnp.bfloat16)
    grad_bias_output = jnp.sum(grad_one.astype(jnp.float32), axis=0)
    grad_attended = product_right(grad_one, back_output).astype(jnp.bfloat16)
    grad_heads = lax.all_to_all(grad_attended, "seq", split_axis=1, concat_axis=0, tiled=True)
    grad_pieces = []
    for head in range(local_heads):
        base = head * 3 * HEAD_DIM
        grad_queries, grad_keys, grad_values = attend_back(
            by_head[:, base : base + HEAD_DIM],
            by_head[:, base + HEAD_DIM : base + 2 * HEAD_DIM],
            by_head[:, base + 2 * HEAD_DIM : base + 3 * HEAD_DIM],
            segment_ids,
            head_logsums[head],
            grad_heads[:, head * HEAD_DIM : (head + 1) * HEAD_DIM],
            block_rows,
        )
        grad_pieces.extend([grad_queries, grad_keys, grad_values])
    grad_by_head = jnp.concatenate(grad_pieces, axis=1).astype(jnp.bfloat16)
    grad_triple = lax.all_to_all(grad_by_head, "seq", split_axis=0, concat_axis=1, tiled=True)
    triple_sums = jnp.sum(grad_triple.astype(jnp.float32), axis=0).reshape(HEADS, 3, HEAD_DIM)
    grad_bias_query = triple_sums[:, 0].reshape(-1)
    grad_bias_value = triple_sums[:, 2].reshape(-1)
    grad_hidden_one = product_right(grad_triple, back_input)
    grad_gain_one = jnp.sum(grad_hidden_one * normed_one, axis=0)
    grad_offset_one = jnp.sum(grad_hidden_one, axis=0)
    tokens_grad = (
        grad_middle + normalize_back(grad_hidden_one * gain_one, normed_one, spread_one)
    ).astype(jnp.bfloat16)
    pairs = (
        (hidden_one, grad_triple),
        (attended, grad_one),
        (hidden_two, grad_before),
        (activated, grad_two),
    )
    vector_grads = (
        grad_gain_one,
        grad_offset_one,
        grad_bias_query,
        grad_bias_value,
        grad_bias_output,
        grad_factor_one,
        grad_gain_two,
        grad_offset_two,
        grad_bias_up,
        grad_bias_down,
        grad_factor_two,
    )
    packed_grads = jnp.concatenate(
        [member.reshape(fsdp_count, -1) for member in vector_grads], axis=1
    )
    shards = []
    for left, right in pairs:
        shards.append(
            lax.psum_scatter(
                term_rows(left, right).astype(jnp.bfloat16), "fsdp", scatter_dimension=0, tiled=True
            ).astype(jnp.float32)
        )
    vector_share = lax.psum_scatter(
        packed_grads.astype(jnp.bfloat16), "fsdp", scatter_dimension=0, tiled=True
    )
    totals = (
        lax.psum(shards[0].astype(jnp.bfloat16), "seq").astype(jnp.float32),
        lax.psum(shards[1].astype(jnp.bfloat16), "seq").astype(jnp.float32),
        lax.psum(shards[2].astype(jnp.bfloat16), "seq").astype(jnp.float32),
        lax.psum(shards[3].astype(jnp.bfloat16), "seq").astype(jnp.float32),
        lax.psum(vector_share, "seq").astype(jnp.float32),
    )
    vector_out = unpack_rows(totals[4], local_widths)
    return (
        layer_out,
        tokens_grad,
        vector_out[0],
        vector_out[1],
        totals[0],
        vector_out[2],
        vector_out[3],
        totals[1],
        vector_out[4],
        vector_out[5],
        vector_out[6],
        vector_out[7],
        totals[2],
        vector_out[8],
        totals[3],
        vector_out[9],
        vector_out[10],
    )


def solution(mesh):
    placed = (
        P(("fsdp", "seq"), None),
        P("fsdp"),
        P("fsdp"),
        P("fsdp"),
        P("fsdp", None),
        P("fsdp"),
        P("fsdp"),
        P("fsdp", None),
        P("fsdp"),
        P("fsdp"),
        P("fsdp"),
        P("fsdp"),
        P("fsdp", None),
        P("fsdp"),
        P("fsdp", None),
        P("fsdp"),
        P("fsdp"),
        P(("fsdp", "seq"), None),
    )
    return jax.shard_map(
        body,
        mesh=mesh,
        in_specs=placed,
        out_specs=(
            P(("fsdp", "seq"), None),
            P(("fsdp", "seq"), None),
            P("fsdp"),
            P("fsdp"),
            P("fsdp", None),
            P("fsdp"),
            P("fsdp"),
            P("fsdp", None),
            P("fsdp"),
            P("fsdp"),
            P("fsdp"),
            P("fsdp"),
            P("fsdp", None),
            P("fsdp"),
            P("fsdp", None),
            P("fsdp"),
            P("fsdp"),
        ),
        check_vma=False,
    )
```

profile of v0, /device:TPU:0, one launch (start us, length us, event | category | flops | bytes accessed | tf_op | source)
XLA Modules:
  0.0 683.4 jit_solution(12038587939500006447)
XLA Ops:
  7.4 0.7 all-gather.7.cloned.1.call-update
  8.1 0.7 all-gather.9.cloned.1.call-update
  8.8 0.7 all-gather.11.cloned.1.call-update
  12.5 15.8 %all-gather.1 = bf16[8,1,1792]{2,1,0:T(2,128)(2,1)S(1)} all-gather(bf16[1,1,1792]{2,1,0:T(2,128)(2,1)S(1)} %reshape.408), channel_id=2, replica_groups=mesh['fsdp'=8,'seq'=4] {'fsdp'}, dimensions={0}, use_global_device_ids=true | all-gather | bytes 32256 | tf_op jit(solution)/shard_map/all_gather | solution.py:149
  29.1 48.3 %all-gather.7.cloned.1.call-done = bf16[1024,3072]{1,0:T(8,128)(2,1)} async-done(((bf16[128,3072]{1,0:T(8,128)(2,1)}), bf16[1024,3072]{1,0:T(8,128)(2,1)}) %all-gather.7.cloned.1.call-update) | async-done | bytes 6291472 | tf_op jit(solution)/shard_map/all_gather | solution.py:164
  77.4 3.9 fusion.1
  81.3 0.9 copy.134
  82.2 3.7 all-to-all-start
  86.0 11.2 %all-to-all-done = bf16[128,4,768]{2,0,1:T(8,128)(2,1)S(1)} async-done(((bf16[128,4,768]{2,0,1:T(8,128)(2,1)}), bf16[128,4,768]{2,0,1:T(8,128)(2,1)S(1)}, u32[]{:S(2)}, u32[]{:S(2)}) %all-to-all-start) | async-done | bytes 786464 | tf_op jit(solution)/shard_map/all_to_all | solution.py:180
  98.3 1.4 fusion.111
  102.5 0.7 pad_maximum_fusion
  103.2 3.6 all-to-all-start.1
  106.9 5.1 all-to-all-done.1
  112.0 3.0 fusion.109
  115.2 74.9 %all-gather.11.cloned.1.call-done = bf16[1024,4096]{1,0:T(8,128)(2,1)} async-done(((bf16[128,4096]{1,0:T(8,128)(2,1)}), bf16[1024,4096]{1,0:T(8,128)(2,1)}) %all-gather.11.cloned.1.call-update) | async-done | bytes 8388624 | tf_op jit(solution)/shard_map/all_gather | solution.py:166
  190.0 4.8 convolution_add_fusion
  194.8 77.3 %all-gather.13.cloned.1.call-done = bf16[4096,1024]{1,0:T(8,128)(2,1)} async-done(((bf16[512,1024]{1,0:T(8,128)(2,1)}), bf16[4096,1024]{1,0:T(8,128)(2,1)}) %all-gather.13.cloned.1.call-update) | async-done | bytes 8388624 | tf_op jit(solution)/shard_map/all_gather | solution.py:167
  272.1 6.6 fusion.114
  278.8 3.0 multiply_reduce_fusion.5
  281.9 0.7 copy-done.1
  282.6 2.4 multiply_reduce_fusion.4
  285.1 0.8 convolution_convert_fusion.4
  286.0 0.7 copy.135
  286.7 3.7 all-to-all-start.2
  290.4 3.0 convolution_convert_fusion.3
  293.7 2.4 all-to-all-done.2
  296.2 1.8 multiply_reduce_fusion
  305.3 13.1 %all_to_all.70 = bf16[4,128,768]{1,2,0:T(8,128)(2,1)S(1)} all-to-all(bf16[4,128,768]{1,2,0:T(8,128)(2,1)S(1)} %bitcast_dynamic-update-slice_fusion), channel_id=1, replica_groups=mesh['fsdp'=8,'seq'=4] {'seq'}, dimensions={0} | all-to-all | bytes 1572864 | tf_op jit(solution)/shard_map/all_to_all | solution.py:240
  318.4 0.9 copy-done.11
  319.2 4.6 convolution_convert_fusion.2
  323.9 4.7 convolution_convert_fusion
  328.7 1.1 copy-done.20
  329.9 5.8 convolution_convert_fusion.1
  336.3 0.6 dynamic-slice
  337.5 5.1 fusion.51
  342.7 56.6 %reduce-scatter.5.cloned.1.call-done = bf16[128,3072]{1,0:T(8,128)(2,1)} async-done(((bf16[1024,3072]{1,0:T(8,128)(2,1)}), bf16[128,3072]{1,0:T(8,128)(2,1)}) %reduce-scatter.5.cloned.1.call-update) | async-done | bytes 786448 | tf_op jit(solution)/shard_map/reduce_scatter | solution.py:275
  399.3 90.3 %reduce-scatter.11.cloned.1.call-done = bf16[512,1024]{1,0:T(8,128)(2,1)} async-done(((bf16[4096,1024]{1,0:T(8,128)(2,1)}), bf16[512,1024]{1,0:T(8,128)(2,1)}) %reduce-scatter.11.cloned.1.call-update) | async-done | bytes 1048592 | tf_op jit(solution)/shard_map/reduce_scatter | solution.py:275
  489.6 90.3 %reduce-scatter.9.cloned.1.call-done = bf16[128,4096]{1,0:T(8,128)(2,1)} async-done(((bf16[1024,4096]{1,0:T(8,128)(2,1)}), bf16[128,4096]{1,0:T(8,128)(2,1)}) %reduce-scatter.9.cloned.1.call-update) | async-done | bytes 1048592 | tf_op jit(solution)/shard_map/reduce_scatter | solution.py:275
  580.3 26.0 %all-reduce = bf16[8,1792]{1,0:T(8,128)(2,1)S(1)} all-reduce(bf16[8,1792]{1,0:T(8,128)(2,1)S(1)} %constant_dynamic-update-slice_fusion), channel_id=3, replica_groups=mesh['fsdp'=8,'seq'=4] {'fsdp'}, use_global_device_ids=true, to_apply=%region_30.31.clone | all-reduce | flops 14336 | bytes 57344
  606.3 0.7 constant_dynamic-slice_fusion
  606.9 10.1 %psum.35 = bf16[1,1792]{1,0:T(2,128)(2,1)S(1)} all-reduce(bf16[1,1792]{1,0:T(2,128)(2,1)S(1)} %constant_dynamic-slice_fusion), channel_id=1, replica_groups=mesh['fsdp'=8,'seq'=4] {'seq'}, use_global_device_ids=true, to_apply=%region_31.32 | all-reduce | flops 1792 | bytes 7168 | tf_op jit(solution)/shard_map/psum | solution.py:287
  617.0 0.6 slice.211
  618.2 1.0 fusion.50
  619.2 50.3 %all-reduce.4.cloned.1.call-done = (bf16[128,3072]{1,0:T(8,128)(2,1)}, bf16[128,1024]{1,0:T(8,128)(2,1)}, bf16[128,4096]{1,0:T(8,128)(2,1)}, bf16[512,1024]{1,0:T(8,128)(2,1)}) async-done(((bf16[128,3072]{1,0:T(8,128)(2,1)}, bf16[128,1024]{1,0:T(8,128)(2,1)}, bf16[128,4096]{1,0:T(8,128)(2,1)}, bf16[512,1024]{1,0:T(8,128)(2,1)}), (bf16[128,3072]{1,0:T(8,128)(2,1)}, bf16[128,1024]{1,0:T(8,128)(2,1)}, ...) | async-done | bytes 3145744 | tf_op jit(solution)/shard_map/psum | solution.py:283
  669.4 1.9 convert_element_type.329
  671.3 2.4 convert_element_type.327
  673.7 1.5 convert_element_type.331
  675.3 1.6 convert_element_type.333
  (197 shorter events, 17.8 us)
Async XLA Ops:
  7.2 2.9 copy-start.28
  7.2 3.2 copy-start.29
  7.2 3.4 copy-start.30
  7.2 3.6 copy-start.31
  7.2 3.8 copy-start.32
  7.2 4.0 copy-start.33
  7.3 4.2 copy-start.34
  7.3 4.4 copy-start.35
  7.3 4.6 copy-start.27
  7.3 4.8 copy-start.36
  7.3 5.0 copy-start.37
  7.3 21.4 %copy-start.2 = (bf16[128,1024]{1,0:T(8,128)(2,1)S(1)}, bf16[128,1024]{1,0:T(8,128)(2,1)}, u32[]{:S(2)}) copy-start(bf16[128,1024]{1,0:T(8,128)(2,1)} %param.18) | copy-start | bytes 786436
  7.3 70.1 %all-gather.7.cloned.1.call-start = ((), (), s32[]{:S(2)}) async-start(), calls=%async_computation.8 | async-start | bytes 7077888 | tf_op jit(solution)/shard_map/all_gather | solution.py:164
  8.0 98.8 %all-gather.9.cloned.1.call-start = ((), (), s32[]{:S(2)}) async-start(), calls=%async_computation.9 | async-start | bytes 2359296 | tf_op jit(solution)/shard_map/all_gather | solution.py:165
  8.8 181.2 %all-gather.11.cloned.1.call-start = ((), (), s32[]{:S(2)}) async-start(), calls=%async_computation.10 | async-start | bytes 9437184 | tf_op jit(solution)/shard_map/all_gather | solution.py:166
  9.5 262.6 %all-gather.13.cloned.1.call-start = ((), (), s32[]{:S(2)}) async-start(), calls=%async_computation.11 | async-start | bytes 9437184 | tf_op jit(solution)/shard_map/all_gather | solution.py:167
  81.3 4.6 copy-start.38
  82.2 15.0 %all-to-all-start = ((bf16[128,4,768]{2,0,1:T(8,128)(2,1)}), bf16[128,4,768]{2,0,1:T(8,128)(2,1)S(1)}, u32[]{:S(2)}, u32[]{:S(2)}) async-start(bf16[128,4,768]{2,0,1:T(8,128)(2,1)} %bitcast.193), calls=%async_computation | async-start | bytes 1572864 | tf_op jit(solution)/shard_map/all_to_all | solution.py:180
  97.6 3.5 copy-start.3
  98.3 1.6 copy-start.15
  99.7 1.7 copy-start.5
  100.3 1.5 copy-start.9
  100.9 1.3 copy-start.7
  103.2 8.8 %all-to-all-start.1 = ((bf16[4,128,256]{1,2,0:T(8,128)(2,1)}), bf16[4,128,256]{1,2,0:T(8,128)(2,1)S(1)}, u32[]{:S(2)}, u32[]{:S(2)}) async-start(bf16[4,128,256]{1,2,0:T(8,128)(2,1)} %pad_maximum_fusion), calls=%async_computation.1 | async-start | bytes 524288 | tf_op jit(solution)/shard_map/all_to_all | solution.py:197
  112.0 3.2 copy-start.23
  190.0 82.1 %copy-start.21 = (bf16[128,1024]{1,0:T(8,128)(2,1)S(1)}, bf16[128,1024]{1,0:T(8,128)(2,1)}, u32[]{:S(2)}) copy-start(bf16[128,1024]{1,0:T(8,128)(2,1)} %param.35) | copy-start | bytes 786436
  272.1 6.6 copy-start
  278.7 3.1 copy-start.19
  278.8 3.8 copy-start.1
  278.8 3.8 copy-start.24
  282.6 2.5 copy-start.13
  285.0 0.9 copy-start.17
  286.7 9.5 %all-to-all-start.2 = ((bf16[128,4,256]{2,0,1:T(8,128)(2,1)}), bf16[128,4,256]{2,0,1:T(8,128)(2,1)S(1)}, u32[]{:S(2)}, u32[]{:S(2)}) async-start(bf16[128,4,256]{2,0,1:T(8,128)(2,1)} %bitcast.230), calls=%async_computation.2 | async-start | bytes 524288 | tf_op jit(solution)/shard_map/all_to_all | solution.py:225
  290.4 52.3 %reduce-scatter.7.cloned.1.call-start = ((), (), s32[]{:S(2)}) async-start(), calls=%async_computation.13 | async-start | bytes 2359296 | tf_op jit(solution)/shard_map/reduce_scatter | solution.py:275
  293.4 105.9 %reduce-scatter.5.cloned.1.call-start = ((), (), s32[]{:S(2)}) async-start(), calls=%async_computation.12 | async-start | bytes 7077888 | tf_op jit(solution)/shard_map/reduce_scatter | solution.py:275
  296.2 1.8 copy-start.4
  296.2 2.1 copy-start.16
  298.0 1.3 copy-start.6
  299.6 1.2 copy-start.10
  301.6 1.2 copy-start.8
  323.9 165.7 %reduce-scatter.11.cloned.1.call-start = ((), (), s32[]{:S(2)}) async-start(), calls=%async_computation.15 | async-start | bytes 9437184 | tf_op jit(solution)/shard_map/reduce_scatter | solution.py:275
  328.7 1.2 copy-start.20
  328.7 251.2 %reduce-scatter.9.cloned.1.call-start = ((), (), s32[]{:S(2)}) async-start(), calls=%async_computation.14 | async-start | bytes 9437184 | tf_op jit(solution)/shard_map/reduce_scatter | solution.py:275
  335.7 1.4 copy-start.12
  335.7 333.7 %all-reduce.4.cloned.1.call-start = ((), (), s32[]{:S(2)}) async-start(), calls=%async_computation.16 | async-start | bytes 6291456 | tf_op jit(solution)/shard_map/psum | solution.py:283
  342.6 275.6 %copy-start.18 = (f32[128,1024]{1,0:T(8,128)S(1)}, f32[128,1024]{1,0:T(8,128)}, u32[]{:S(2)}) copy-start(f32[128,1024]{1,0:T(8,128)} %copy-done.17) | copy-start | bytes 1572868
  669.4 4.3 copy-start.26
  673.7 1.5 copy-start.25
  (4 other events, 3.3 us)
Sparse Core Ops, SparseCore 0:
  9.8 67.5 all-gather.6
  79.0 27.7 all-gather.8
  108.4 81.5 all-gather.10
  191.5 80.5 all-gather.12
  293.8 34.8 reduce-scatter.6
  330.9 68.4 reduce-scatter.4
  401.6 87.9 reduce-scatter.10
  491.9 87.9 reduce-scatter.8
  583.3 86.1 all-reduce.3
where the time goes:
time: 684 us; the launch traced here: 683 us
  waiting for transfers between devices  509 us (74%)
  blocking collectives  64.9 us (9%)
  matrix products  58.2 us (9%)
  between operations  14.6 us (2%)
  local copies, waits for them, and re-layouts  12.2 us (2%)
  other arithmetic  12.2 us (2%)
  starting transfers between devices  11.7 us (2%)
    reduce_scatter x4, waiting for transfers between devices, body(): lax.psum_scatter(term_rows(left, right).astype(jnp.bfloat16), 'fsdp', sca...  237 us
    all_gather x1, waiting for transfers between devices, body(): lax.all_gather(down_weight, 'fsdp', axis=0, tiled=True)  77.3 us
    all_gather x1, waiting for transfers between devices, body(): lax.all_gather(up_weight, 'fsdp', axis=0, tiled=True)  74.9 us
    psum x1, waiting for transfers between devices, body(): lax.psum(shards[0].astype(jnp.bfloat16), 'seq').astype(jnp.float32)  50.3 us
    all_gather x1, waiting for transfers between devices, body(): lax.all_gather(input_weight, 'fsdp', axis=0, tiled=True)  48.3 us
    unnamed x1, blocking collectives  26 us
    dot_general x12, matrix products, product_right(): lax.dot_general(left, right, (((1,), (1,)), ((), ())), preferred_element_...  21 us
    dot_general x12, matrix products, product_left(): lax.dot_general(left, right, (((0,), (0,)), ((), ())), preferred_element_...  20.8 us
  transfers between devices with their start and end apart: 12, of which 10 were waited for; matrix products, arithmetic and copies ran while one was open for 8% of the time, Pallas kernels for 0%

commit v1 on v0

v1 whole, which is shorter than its diff:
```python
import math

import jax
import jax.numpy as jnp
from jax import lax
from jax.sharding import PartitionSpec as P

HEADS = 16
HEAD_DIM = 64
epsilon = 1e-06
masked_value = -1000000000.0
bf16 = jnp.bfloat16
f32 = jnp.float32


def product(left, right):
    return jnp.dot(left, right, preferred_element_type=f32)


def product_left(left, right):
    return lax.dot_general(left, right, (((0,), (0,)), ((), ())), preferred_element_type=f32)


def product_right(left, right):
    return lax.dot_general(left, right, (((1,), (1,)), ((), ())), preferred_element_type=f32)


def normalize(values):
    center = values - jnp.mean(values, axis=1, keepdims=True)
    spread = lax.rsqrt(jnp.mean(center * center, axis=1, keepdims=True) + epsilon)
    return (center * spread, spread)


def normalize_back(grad_normed, normed, spread):
    return spread * (
        grad_normed
        - jnp.mean(grad_normed, axis=1, keepdims=True)
        - normed * jnp.mean(grad_normed * normed, axis=1, keepdims=True)
    )


def gelu_pair(before):
    normal_cdf = 0.5 * (1.0 + lax.erf(before * (1.0 / math.sqrt(2.0))))
    density = jnp.exp(-0.5 * before * before) * (1.0 / math.sqrt(2.0 * math.pi))
    return (before * normal_cdf, normal_cdf + before * density)


def swap(x, axis, k):
    count = lax.axis_size(axis)
    return lax.ppermute(x, axis, [(i, i ^ k) for i in range(count)])


def from_others(x):
    return [x] + [swap(x, "seq", k) for k in range(1, lax.axis_size("seq"))]


def exchange(blocks):
    return [blocks[0]] + [swap(blocks[k], "seq", k) for k in range(1, len(blocks))]


def gather_fsdp(x):
    count = lax.axis_size("fsdp")
    f = lax.axis_index("fsdp")
    same = [x] + [swap(x, "fsdp", 2 * k) for k in range(1, count // 2)]
    other = swap(jnp.stack(same), "fsdp", 1)
    out = jnp.zeros((count,) + x.shape, x.dtype)
    for k in range(count // 2):
        out = lax.dynamic_update_index_in_dim(out, same[k], f ^ (2 * k), 0)
        out = lax.dynamic_update_index_in_dim(out, other[k], f ^ (2 * k + 1), 0)
    return out


def scatter_fsdp(g):
    count = g.shape[0]
    f = lax.axis_index("fsdp")
    z, core = f // 2, f % 2
    pairs = g.reshape((count // 2, 2) + g.shape[1:])
    mine = lax.dynamic_index_in_dim(pairs, core, 1, keepdims=False)
    theirs = lax.dynamic_index_in_dim(pairs, 1 - core, 1, keepdims=False)
    sums = (mine.astype(f32) + swap(theirs, "fsdp", 1).astype(f32)).astype(bf16)
    total = lax.dynamic_index_in_dim(sums, z, 0, keepdims=False).astype(f32)
    for k in range(1, count // 2):
        block = lax.dynamic_index_in_dim(sums, z ^ k, 0, keepdims=False)
        total = total + swap(block, "fsdp", 2 * k).astype(f32)
    return total


def attend(triple, segments, heads):
    rows = triple.shape[0]
    parts = triple.reshape(rows, heads, 3, HEAD_DIM)
    outs = []
    logsums = []
    same = segments[:, None] == segments[None, :]
    for h in range(heads):
        q, k, v = parts[:, h, 0], parts[:, h, 1], parts[:, h, 2]
        scores = jnp.where(same, product_right(q, k) * HEAD_DIM**-0.5, masked_value)
        highest = jnp.max(scores, axis=1, keepdims=True)
        powers = jnp.exp(scores - highest)
        totals = jnp.sum(powers, axis=1, keepdims=True)
        outs.append(product((powers / totals).astype(bf16), v).astype(bf16))
        logsums.append(highest + jnp.log(totals))
    return jnp.concatenate(outs, axis=1), logsums


def attend_back(triple, segments, logsums, grad, heads):
    rows = triple.shape[0]
    parts = triple.reshape(rows, heads, 3, HEAD_DIM)
    same = segments[:, None] == segments[None, :]
    outs = []
    for h in range(heads):
        q, k, v = parts[:, h, 0], parts[:, h, 1], parts[:, h, 2]
        g = grad[:, h * HEAD_DIM : (h + 1) * HEAD_DIM]
        scores = jnp.where(same, product_right(q, k) * HEAD_DIM**-0.5, masked_value)
        weights = jnp.exp(scores - logsums[h])
        grad_v = product_left(weights.astype(bf16), g)
        grad_weights = product_right(g, v)
        dots = jnp.sum(weights * grad_weights, axis=1, keepdims=True)
        grad_scores = (weights * (grad_weights - dots)).astype(bf16)
        grad_q = product(grad_scores, k) * HEAD_DIM**-0.5
        grad_k = product_left(grad_scores, q) * HEAD_DIM**-0.5
        outs.extend([grad_q, grad_k, grad_v])
    return jnp.concatenate(outs, axis=1).astype(bf16)


def body(
    tokens,
    segment_ids,
    first_gain,
    first_bias,
    input_weight,
    query_bias,
    value_bias,
    output_weight,
    output_bias,
    scale_one,
    second_gain,
    second_bias,
    up_weight,
    up_bias,
    down_weight,
    down_bias,
    scale_two,
    out_grad,
):
    members = lax.axis_size("seq")
    fsdp = lax.axis_size("fsdp")
    s = lax.axis_index("seq")
    rows, width = tokens.shape
    heads = HEADS // members
    own_cols = 3 * HEAD_DIM * heads
    part = width // members
    shard = input_weight.shape[0]
    ff_shard = down_weight.shape[0]
    ff_part = ff_shard // members

    local_vectors = (
        first_gain,
        first_bias,
        query_bias,
        value_bias,
        output_bias,
        scale_one,
        second_gain,
        second_bias,
        up_bias,
        down_bias,
        scale_two,
    )
    widths = [v.shape[0] for v in local_vectors]
    packed_width = sum(widths)

    own_in = lax.dynamic_slice_in_dim(input_weight, s * own_cols, own_cols, 1)
    own_out = lax.dynamic_slice_in_dim(output_weight, s * part, part, 1)
    own_up = lax.dynamic_slice_in_dim(
        up_weight.reshape(shard, fsdp, ff_shard), s * ff_part, ff_part, 2
    ).reshape(shard, fsdp * ff_part)
    own_down = lax.dynamic_slice_in_dim(down_weight, s * ff_part, ff_part, 0)

    vectors = gather_fsdp(jnp.concatenate(local_vectors)[None, :])[:, 0]
    w_in = gather_fsdp(own_in).reshape(width, own_cols)
    w_out_part = gather_fsdp(own_out).reshape(width, part)
    w_up = gather_fsdp(own_up).reshape(width, fsdp * ff_part)
    w_down = gather_fsdp(own_down).reshape(fsdp * ff_part, width)
    w_out = jnp.zeros((width, width), bf16)
    for k, block in enumerate(from_others(w_out_part)):
        w_out = lax.dynamic_update_slice_in_dim(w_out, block, (s ^ k) * part, 1)

    pieces = []
    offset = 0
    for size in widths:
        pieces.append(vectors[:, offset : offset + size].reshape(-1).astype(f32))
        offset += size
    (
        gain_one,
        offset_one,
        bias_query,
        bias_value,
        bias_output,
        factor_one,
        gain_two,
        offset_two,
        bias_up,
        bias_down,
        factor_two,
    ) = pieces
    own_bias_up = lax.dynamic_slice_in_dim(
        bias_up.reshape(fsdp, ff_shard), s * ff_part, ff_part, 1
    ).reshape(-1)
    own_query = lax.dynamic_slice_in_dim(bias_query, s * part, part, 0)
    own_value = lax.dynamic_slice_in_dim(bias_value, s * part, part, 0)

    inputs = jnp.concatenate(from_others(tokens), axis=0).astype(f32)
    out_grads = jnp.concatenate(from_others(out_grad), axis=0).astype(f32)
    segments = jnp.concatenate(
        [lax.dynamic_slice_in_dim(segment_ids, (s ^ k) * rows, rows, 0) for k in range(members)]
    )

    normed_one, spread_one = normalize(inputs)
    hidden_one = (normed_one * gain_one + offset_one).astype(bf16)
    bias_own = jnp.stack(
        [
            own_query.reshape(heads, HEAD_DIM),
            jnp.zeros((heads, HEAD_DIM), f32),
            own_value.reshape(heads, HEAD_DIM),
        ],
        axis=1,
    ).reshape(-1)
    triple = (product(hidden_one, w_in) + bias_own).astype(bf16)
    attended_own, logsums = attend(triple, segments, heads)

    attended = jnp.zeros((members * rows, width), bf16)
    for k, block in enumerate(from_others(attended_own)):
        block = block.reshape(members, rows, part)
        block = jnp.concatenate([block[j ^ k] for j in range(members)], axis=0)
        attended = lax.dynamic_update_slice_in_dim(attended, block, (s ^ k) * part, 1)

    branch_one = product(attended, w_out) + bias_output
    middle = inputs + factor_one * branch_one
    normed_two, spread_two = normalize(middle)
    hidden_two = (normed_two * gain_two + offset_two).astype(bf16)
    before = product(hidden_two, w_up) + own_bias_up
    activated_full, slope = gelu_pair(before)
    activated = activated_full.astype(bf16)

    grads = out_grads * (segments >= 0).astype(f32)[:, None]
    grad_two = (grads * factor_two).astype(bf16)
    grad_before = (product_right(grad_two, w_down) * slope).astype(bf16)
    partial_hidden_two = product_right(grad_before, w_up)
    grad_hidden_two = sum(
        block.astype(f32)
        for block in exchange(
            [partial_hidden_two[:rows]]
            + [partial_hidden_two[k * rows : (k + 1) * rows].astype(bf16) for k in range(1, members)]
        )
    )

    partial_two = product(activated, w_down)
    branch_two = bias_down + sum(
        block.astype(f32)
        for block in exchange(
            [partial_two[:rows]]
            + [partial_two[k * rows : (k + 1) * rows].astype(bf16) for k in range(1, members)]
        )
    )
    own_middle, own_grad = middle[:rows], grads[:rows]
    layer_out = (own_middle + factor_two * branch_two).astype(bf16)
    grad_factor_two = jnp.sum(own_grad * branch_two, axis=0)
    grad_bias_down = jnp.sum(grad_two[:rows].astype(f32), axis=0)
    grad_bias_up = jnp.sum(grad_before.astype(f32), axis=0)

    own_normed_two = normed_two[:rows]
    grad_gain_two = jnp.sum(grad_hidden_two * own_normed_two, axis=0)
    grad_offset_two = jnp.sum(grad_hidden_two, axis=0)
    grad_middle = own_grad + normalize_back(
        grad_hidden_two * gain_two, own_normed_two, spread_two[:rows]
    )
    grad_factor_one = jnp.sum(grad_middle * branch_one[:rows], axis=0)
    grad_one = (grad_middle * factor_one).astype(bf16)
    grad_bias_output = jnp.sum(grad_one.astype(f32), axis=0)
    grad_attended = product_right(grad_one, w_out).astype(bf16)

    def columns(x, k):
        return lax.dynamic_slice_in_dim(x, (s ^ k) * part, part, 1)

    grad_heads = jnp.concatenate(
        exchange([columns(grad_attended, k) for k in range(members)]), axis=0
    )
    grad_one_cols = jnp.concatenate(exchange([columns(grad_one, k) for k in range(members)]), axis=0)
    grad_triple = attend_back(triple, segments, logsums, grad_heads, heads)
    partial_hidden_one = product_right(grad_triple, w_in)
    grad_hidden_one = sum(
        block.astype(f32)
        for block in exchange(
            [partial_hidden_one[:rows]]
            + [partial_hidden_one[k * rows : (k + 1) * rows].astype(bf16) for k in range(1, members)]
        )
    )
    own_normed_one = normed_one[:rows]
    grad_gain_one = jnp.sum(grad_hidden_one * own_normed_one, axis=0)
    grad_offset_one = jnp.sum(grad_hidden_one, axis=0)
    tokens_grad = (
        grad_middle
        + normalize_back(grad_hidden_one * gain_one, own_normed_one, spread_one[:rows])
    ).astype(bf16)

    def own_share(left, right, lead):
        full = product_left(left, right).astype(bf16)
        return scatter_fsdp(full.reshape(fsdp, lead, full.shape[1])).astype(bf16)

    share_down = own_share(activated, grad_two, ff_part)
    share_up = own_share(hidden_two, grad_before, shard)
    share_out = own_share(attended, grad_one_cols, shard)
    share_in = own_share(hidden_one, grad_triple, shard)

    grad_down = jnp.zeros(down_weight.shape, f32)
    for k, block in enumerate(from_others(share_down)):
        grad_down = lax.dynamic_update_slice_in_dim(
            grad_down, block.astype(f32), (s ^ k) * ff_part, 0
        )
    grad_up = jnp.zeros((shard, fsdp, ff_shard), f32)
    for k, block in enumerate(from_others(share_up)):
        grad_up = lax.dynamic_update_slice_in_dim(
            grad_up, block.astype(f32).reshape(shard, fsdp, ff_part), (s ^ k) * ff_part, 2
        )
    grad_up = grad_up.reshape(up_weight.shape)
    grad_out = jnp.zeros(output_weight.shape, f32)
    for k, block in enumerate(from_others(share_out)):
        grad_out = lax.dynamic_update_slice_in_dim(
            grad_out, block.astype(f32), (s ^ k) * part, 1
        )
    grad_in = jnp.zeros(input_weight.shape, f32)
    for k, block in enumerate(from_others(share_in)):
        grad_in = lax.dynamic_update_slice_in_dim(
            grad_in, block.astype(f32), (s ^ k) * own_cols, 1
        )

    triple_sums = jnp.sum(grad_triple.astype(f32), axis=0).reshape(heads, 3, HEAD_DIM)

    def placed(x, total):
        return lax.dynamic_update_slice_in_dim(
            jnp.zeros((total,), f32), x.reshape(-1), s * x.size, 0
        )

    grad_bias_up_full = lax.dynamic_update_slice_in_dim(
        jnp.zeros((fsdp, ff_shard), f32), grad_bias_up.reshape(fsdp, ff_part), s * ff_part, 1
    )
    vector_grads = (
        grad_gain_one,
        grad_offset_one,
        placed(triple_sums[:, 0], width),
        placed(triple_sums[:, 2], width),
        grad_bias_output,
        grad_factor_one,
        grad_gain_two,
        grad_offset_two,
        grad_bias_up_full,
        grad_bias_down,
        grad_factor_two,
    )
    packed = jnp.concatenate([v.reshape(fsdp, -1) for v in vector_grads], axis=1)
    packed = sum(from_others(packed))
    vector_total = scatter_fsdp(packed.astype(bf16)[:, None, :])[0]
    outs = []
    offset = 0
    for size in widths:
        outs.append(vector_total[offset : offset + size])
        offset += size
    return (
        layer_out,
        tokens_grad,
        outs[0],
        outs[1],
        grad_in,
        outs[2],
        outs[3],
        grad_out,
        outs[4],
        outs[5],
        outs[6],
        outs[7],
        grad_up,
        outs[8],
        grad_down,
        outs[9],
        outs[10],
    )


def solution(mesh):
    rows, vec, mat = P(("fsdp", "seq"), None), P("fsdp"), P("fsdp", None)
    return jax.shard_map(
        body,
        mesh=mesh,
        in_specs=(
            rows, vec, vec, vec, mat, vec, vec, mat, vec,
            vec, vec, vec, mat, vec, mat, vec, vec, rows,
        ),
        out_specs=(
            rows, rows, vec, vec, mat, vec, vec, mat, vec,
            vec, vec, vec, mat, vec, mat, vec, vec,
        ),
        check_vma=False,
    )
```

time: 684 us -> 397 us (0.58)
  waiting for transfers between devices: 509 us -> 136 us
  starting transfers between devices: 11.7 us -> 127 us
  blocking collectives: 64.9 us -> 0 us
  local copies, waits for them, and re-layouts: 12.2 us -> 64.8 us
  matrix products: 58.2 us -> 38.1 us
  between operations: 14.6 us -> 2.61 us
  other arithmetic: 12.2 us -> 22.7 us
    reduce_scatter x4 -> x0, waiting for transfers between devices: 237 us -> none  [body(): lax.psum_scatter(term_rows(left, right).astype(jnp.bfloat16), 'fsdp', sca...]
    all_gather x4 -> x0, waiting for transfers between devices: 201 us -> none  [the longest x1 77.3 us: body(): lax.all_gather(down_weight, 'fsdp', axis=0, tiled=True)]
    ppermute x0 -> x82, waiting for transfers between devices: none -> 136 us  [swap(): return lax.ppermute(x, axis, [(i, i ^ k) for i in range(count)])]
    ppermute x0 -> x82, starting transfers between devices: none -> 127 us  [swap(): return lax.ppermute(x, axis, [(i, i ^ k) for i in range(count)])]
    psum x1 -> x0, waiting for transfers between devices: 50.3 us -> none  [body(): lax.psum(shards[0].astype(jnp.bfloat16), 'seq').astype(jnp.float32)]
    dynamic_update_slice x0 -> x50, local copies, waits for them, and re-layouts: none -> 31.3 us  [the longest x20 17 us: gather_fsdp(): out = lax.dynamic_update_index_in_dim(out, other[k], f ^ 2 * k + 1, 0)]
    unnamed x1 -> x0, blocking collectives: 26 us -> none
    all_to_all x3 -> x0, waiting for transfers between devices: 18.7 us -> none  [the longest x1 11.2 us: body(): lax.all_to_all(triple, 'seq', split_axis=1, concat_axis=0, tiled=True)]
  transfers between devices with their start and end apart: 12 -> 82, of which waited for: 10 -> 27; matrix products, arithmetic and copies ran while one was open for 8% -> 21% of each run, Pallas kernels for 0% -> 0%
where the time goes in v1:
time: 397 us; the launch traced here: 391 us
  waiting for transfers between devices  136 us (34%)
  starting transfers between devices  127 us (32%)
  local copies, waits for them, and re-layouts  64.8 us (16%)
  matrix products  38.1 us (10%)
  other arithmetic  22.7 us (6%)
    ppermute x82, waiting for transfers between devices, swap(): return lax.ppermute(x, axis, [(i, i ^ k) for i in range(count)])  136 us
    ppermute x82, starting transfers between devices, swap(): return lax.ppermute(x, axis, [(i, i ^ k) for i in range(count)])  127 us
    dynamic_update_slice x20, local copies, waits for them, and re-layouts, gather_fsdp(): out = lax.dynamic_update_index_in_dim(out, other[k], f ^ 2 * k + 1, 0)  17 us
    unnamed x151, local copies, waits for them, and re-layouts  15.8 us
    dot_general x12, matrix products, product(): return jnp.dot(left, right, preferred_element_type=f32)  15.2 us
    dot_general x12, matrix products, product_right(): lax.dot_general(left, right, (((1,), (1,)), ((), ())), preferred_element_...  13.7 us
    dynamic_update_slice x19, local copies, waits for them, and re-layouts, gather_fsdp(): out = lax.dynamic_update_index_in_dim(out, same[k], f ^ 2 * k, 0)  13.5 us
    dot_general x12, matrix products, product_left(): lax.dot_general(left, right, (((0,), (0,)), ((), ())), preferred_element_...  9.18 us
  transfers between devices with their start and end apart: 82, of which 27 were waited for; matrix products, arithmetic and copies ran while one was open for 21% of the time, Pallas kernels for 0%

profile of v1, /device:TPU:0, one launch (start us, length us, event | category | flops | bytes accessed | tf_op | source)
XLA Modules:
  0.0 391.5 jit_solution(7938891020562071414)
XLA Ops:
  9.9 5.1 %collective-permute-start.5 = (bf16[1,1792]{1,0:T(2,128)(2,1)S(1)}, bf16[1,1792]{1,0:T(2,128)(2,1)S(1)}, u32[]{:S(2)}, u32[]{:S(2)}) collective-permute-start(bf16[1,1792]{1,0:T(2,128)(2,1)S(1)} %squeeze.177), channel_id=1, source_target_pairs={{0,24},{4,28},{8,16},{12,20},{16,8},{20,12},{24,0},{28,4},{1,25},{... | collective-permute-start | bytes 10760 | tf_op jit(solution)/shard_map/ppermute | solution.py:50
  16.5 3.8 collective-permute-start.16
  31.5 2.6 collective-permute-start.2
  35.4 3.6 collective-permute-start.9
  44.4 8.3 %collective-permute-start.7 = (bf16[128,768]{1,0:T(8,128)(2,1)S(1)}, bf16[128,768]{1,0:T(8,128)(2,1)S(1)}, u32[]{:S(2)}, u32[]{:S(2)}) collective-permute-start(bf16[128,768]{1,0:T(8,128)(2,1)S(1)} %get-tuple-element.50), channel_id=1, source_target_pairs={{0,8},{4,12},{8,0},{12,4},{16,24},{20,28},{24,16},{28,20},{1,9},{5... | collective-permute-start | bytes 589832 | tf_op jit(solution)/shard_map/ppermute | solution.py:50
  56.4 3.6 collective-permute-done.7
  60.7 2.5 collective-permute-start.27
  65.5 4.5 %collective-permute-done.33 = bf16[128,1024]{1,0:T(8,128)(2,1)S(1)} collective-permute-done((bf16[128,1024]{1,0:T(8,128)(2,1)S(1)}, bf16[128,1024]{1,0:T(8,128)(2,1)S(1)}, u32[]{:S(2)}, u32[]{:S(2)}) %collective-permute-start.33) | collective-permute-done | bytes 262176 | tf_op jit(solution)/shard_map/ppermute | solution.py:50
  70.0 2.5 collective-permute-start.23
  76.5 4.3 %collective-permute-start.21 = (bf16[128,1024]{1,0:T(8,128)(2,1)S(1)}, bf16[128,1024]{1,0:T(8,128)(2,1)S(1)}, u32[]{:S(2)}, u32[]{:S(2)}) collective-permute-start(bf16[128,1024]{1,0:T(8,128)(2,1)S(1)} %bitcast.407), channel_id=1, source_target_pairs={{0,8},{4,12},{8,0},{12,4},{16,24},{20,28},{24,16},{28,20},{1,9},{5... | collective-permute-start | bytes 786440 | tf_op jit(solution)/shard_map/ppermute | solution.py:50
  80.8 16.3 %collective-permute-done.26 = bf16[128,1024]{1,0:T(8,128)(2,1)S(1)} collective-permute-done((bf16[128,1024]{1,0:T(8,128)(2,1)S(1)}, bf16[128,1024]{1,0:T(8,128)(2,1)S(1)}, u32[]{:S(2)}, u32[]{:S(2)}) %collective-permute-start.26) | collective-permute-done | bytes 262176 | tf_op jit(solution)/shard_map/ppermute | solution.py:50
  97.1 2.1 collective-permute-start.18
  101.9 5.4 %collective-permute-done.22 = bf16[128,1024]{1,0:T(8,128)(2,1)S(1)} collective-permute-done((bf16[128,1024]{1,0:T(8,128)(2,1)S(1)}, bf16[128,1024]{1,0:T(8,128)(2,1)S(1)}, u32[]{:S(2)}, u32[]{:S(2)}) %collective-permute-start.22) | collective-permute-done | bytes 262176 | tf_op jit(solution)/shard_map/ppermute | solution.py:50
  107.3 2.5 collective-permute-start.20
  112.1 12.3 %collective-permute-done.19 = bf16[1024,256]{1,0:T(8,128)(2,1)S(1)} collective-permute-done((bf16[1024,256]{1,0:T(8,128)(2,1)S(1)}, bf16[1024,256]{1,0:T(8,128)(2,1)S(1)}, u32[]{:S(2)}, u32[]{:S(2)}) %collective-permute-start.19) | collective-permute-done | bytes 524320 | tf_op jit(solution)/shard_map/ppermute | solution.py:50
  129.5 3.4 add_convert_fusion.2
  141.6 10.8 %collective-permute-done.12 = bf16[512,256]{0,1:T(8,128)(2,1)S(1)} collective-permute-done((bf16[512,256]{0,1:T(8,128)(2,1)S(1)}, bf16[512,256]{0,1:T(8,128)(2,1)S(1)}, u32[]{:S(2)}, u32[]{:S(2)}) %collective-permute-start.12) | collective-permute-done | bytes 262176 | tf_op jit(solution)/shard_map/ppermute | solution.py:50
  152.8 2.9 fusion.118
  167.4 3.1 multiply_convert_fusion.1
  177.1 4.2 %convert_reduce_fusion.1 = (f32[1024]{0:T(1024)S(1)}, bf16[512,1024]{1,0:T(8,128)(2,1)S(1)}) fusion(f32[512,1024]{1,0:T(8,128)S(1)} %get-tuple-element.140, f32[1024]{0:T(1024)S(1)} %copy-done.50, bf16[512,1024]{1,0:T(8,128)(2,1)S(1)} %copy-done.6, bf16[1024,1024]{1,0:T(8,128)(2,1)} %bitcast.49), kind=kOutput, calls=%fused_computation.17 | convolution fusion | flops 1080556544 | bytes 6299648 | tf_op jit(solution)/shard_map/dot_general | solution.py:25
  181.4 2.9 fusion.131
  185.6 3.6 fusion.130
  198.5 7.9 %collective-permute-done.37 = bf16[128,1024]{1,0:T(8,128)(2,1)S(1)} collective-permute-done((bf16[128,1024]{1,0:T(8,128)(2,1)S(1)}, bf16[128,1024]{1,0:T(8,128)(2,1)S(1)}, u32[]{:S(2)}, u32[]{:S(2)}) %collective-permute-start.37) | collective-permute-done | bytes 262176 | tf_op jit(solution)/shard_map/ppermute | solution.py:50
  207.0 7.7 %collective-permute-done.36 = bf16[128,1024]{1,0:T(8,128)(2,1)S(1)} collective-permute-done((bf16[128,1024]{1,0:T(8,128)(2,1)S(1)}, bf16[128,1024]{1,0:T(8,128)(2,1)S(1)}, u32[]{:S(2)}, u32[]{:S(2)}) %collective-permute-start.36) | collective-permute-done | bytes 262176 | tf_op jit(solution)/shard_map/ppermute | solution.py:50
  215.6 2.2 multiply_reduce_fusion.5
  224.0 2.1 collective-permute-start.60
  233.6 2.7 fusion.132
  237.2 2.5 convolution_convert_fusion.2
  239.9 2.1 collective-permute-start.43
  245.8 2.1 dynamic-slice_bitcast_fusion.2
  247.8 2.5 collective-permute-done.43
  250.3 3.8 collective-permute-done.42
  261.2 2.4 collective-permute-start.64
  267.9 2.5 collective-permute-start.50
  280.2 4.2 %collective-permute-done.67 = bf16[128,256]{1,0:T(8,128)(2,1)S(1)} collective-permute-done((bf16[128,256]{1,0:T(8,128)(2,1)S(1)}, bf16[128,256]{1,0:T(8,128)(2,1)S(1)}, u32[]{:S(2)}, u32[]{:S(2)}) %collective-permute-start.67) | collective-permute-done | bytes 65568 | tf_op jit(solution)/shard_map/ppermute | solution.py:50
  287.8 3.0 collective-permute-start.69
  294.3 2.5 collective-permute-start.78
  297.5 21.4 %collective-permute-start.77 = (bf16[128,1024]{1,0:T(8,128)(2,1)S(1)}, bf16[128,1024]{1,0:T(8,128)(2,1)S(1)}, u32[]{:S(2)}, u32[]{:S(2)}) collective-permute-start(bf16[128,1024]{1,0:T(8,128)(2,1)S(1)} %get-tuple-element.59), channel_id=1, source_target_pairs={{0,16},{4,20},{8,24},{12,28},{16,0},{20,4},{24,8},{28,12},{1,17},{... | collective-permute-start | bytes 786440 | tf_op jit(solution)/shard_map/ppermute | solution.py:50
  318.9 5.1 %collective-permute-done.70 = bf16[128,1024]{1,0:T(8,128)(2,1)S(1)} collective-permute-done((bf16[128,1024]{1,0:T(8,128)(2,1)S(1)}, bf16[128,1024]{1,0:T(8,128)(2,1)S(1)}, u32[]{:S(2)}, u32[]{:S(2)}) %collective-permute-start.70) | collective-permute-done | bytes 262176 | tf_op jit(solution)/shard_map/ppermute | solution.py:50
  324.0 3.1 collective-permute-start.53
  327.1 5.4 %collective-permute-start.52 = (bf16[128,768]{1,0:T(8,128)(2,1)S(1)}, bf16[128,768]{1,0:T(8,128)(2,1)S(1)}, u32[]{:S(2)}, u32[]{:S(2)}) collective-permute-start(bf16[128,768]{1,0:T(8,128)(2,1)S(1)} %get-tuple-element.73), channel_id=1, source_target_pairs={{0,8},{4,12},{8,0},{12,4},{16,24},{20,28},{24,16},{28,20},{1,9},{5... | collective-permute-start | bytes 589832 | tf_op jit(solution)/shard_map/ppermute | solution.py:50
  332.7 14.5 %collective-permute-done.53 = bf16[128,768]{1,0:T(8,128)(2,1)S(1)} collective-permute-done((bf16[128,768]{1,0:T(8,128)(2,1)S(1)}, bf16[128,768]{1,0:T(8,128)(2,1)S(1)}, u32[]{:S(2)}, u32[]{:S(2)}) %collective-permute-start.53) | collective-permute-done | bytes 196640 | tf_op jit(solution)/shard_map/ppermute | solution.py:50
  349.1 2.0 collective-permute-start.74
  354.1 11.9 %collective-permute-done.55 = bf16[128,768]{1,0:T(8,128)(2,1)S(1)} collective-permute-done((bf16[128,768]{1,0:T(8,128)(2,1)S(1)}, bf16[128,768]{1,0:T(8,128)(2,1)S(1)}, u32[]{:S(2)}, u32[]{:S(2)}) %collective-permute-start.55) | collective-permute-done | bytes 196640 | tf_op jit(solution)/shard_map/ppermute | solution.py:50
  366.7 6.4 %collective-permute-done.56 = bf16[128,768]{1,0:T(8,128)(2,1)S(1)} collective-permute-done((bf16[128,768]{1,0:T(8,128)(2,1)S(1)}, bf16[128,768]{1,0:T(8,128)(2,1)S(1)}, u32[]{:S(2)}, u32[]{:S(2)}) %collective-permute-start.56) | collective-permute-done | bytes 196640 | tf_op jit(solution)/shard_map/ppermute | solution.py:50
  374.2 6.4 %collective-permute-done.57 = bf16[128,768]{1,0:T(8,128)(2,1)S(1)} collective-permute-done((bf16[128,768]{1,0:T(8,128)(2,1)S(1)}, bf16[128,768]{1,0:T(8,128)(2,1)S(1)}, u32[]{:S(2)}, u32[]{:S(2)}) %collective-permute-start.57) | collective-permute-done | bytes 196640 | tf_op jit(solution)/shard_map/ppermute | solution.py:50
  384.0 3.0 copy.51
  386.9 2.9 collective-permute-done.80
  (482 shorter events, 146.1 us)
Async XLA Ops:
  9.9 20.9 %collective-permute-start.5 = (bf16[1,1792]{1,0:T(2,128)(2,1)S(1)}, bf16[1,1792]{1,0:T(2,128)(2,1)S(1)}, u32[]{:S(2)}, u32[]{:S(2)}) collective-permute-start(bf16[1,1792]{1,0:T(2,128)(2,1)S(1)} %squeeze.177), channel_id=1, source_target_pairs={{0,24},{4,28},{8,16},{12,20},{16,8},{20,12},{24,0},{28,4},{1,25},{... | collective-permute-start | bytes 10760 | tf_op jit(solution)/shard_map/ppermute | solution.py:50
  15.0 16.5 %collective-permute-start.4 = (bf16[1,1792]{1,0:T(2,128)(2,1)S(1)}, bf16[1,1792]{1,0:T(2,128)(2,1)S(1)}, u32[]{:S(2)}, u32[]{:S(2)}) collective-permute-start(bf16[1,1792]{1,0:T(2,128)(2,1)S(1)} %squeeze.177), channel_id=1, source_target_pairs={{0,16},{4,20},{8,24},{12,28},{16,0},{20,4},{24,8},{28,12},{1,17},{... | collective-permute-start | bytes 10760 | tf_op jit(solution)/shard_map/ppermute | solution.py:50
  15.0 19.1 %collective-permute-start.3 = (bf16[1,1792]{1,0:T(2,128)(2,1)S(1)}, bf16[1,1792]{1,0:T(2,128)(2,1)S(1)}, u32[]{:S(2)}, u32[]{:S(2)}) collective-permute-start(bf16[1,1792]{1,0:T(2,128)(2,1)S(1)} %squeeze.177), channel_id=1, source_target_pairs={{0,8},{4,12},{8,0},{12,4},{16,24},{20,28},{24,16},{28,20},{1,9},{5... | collective-permute-start | bytes 10760 | tf_op jit(solution)/shard_map/ppermute | solution.py:50
  16.5 25.8 %collective-permute-start.16 = (bf16[128,256]{1,0:T(8,128)(2,1)S(1)}, bf16[128,256]{1,0:T(8,128)(2,1)S(1)}, u32[]{:S(2)}, u32[]{:S(2)}) collective-permute-start(bf16[128,256]{1,0:T(8,128)(2,1)S(1)} %get-tuple-element.48), channel_id=1, source_target_pairs={{0,24},{4,28},{8,16},{12,20},{16,8},{20,12},{24,0},{28,4},{1,25},{... | collective-permute-start | bytes 196616 | tf_op jit(solution)/shard_map/ppermute | solution.py:50
  20.3 22.5 %collective-permute-start.15 = (bf16[128,256]{1,0:T(8,128)(2,1)S(1)}, bf16[128,256]{1,0:T(8,128)(2,1)}, u32[]{:S(2)}, u32[]{:S(2)}) collective-permute-start(bf16[128,256]{1,0:T(8,128)(2,1)S(1)} %get-tuple-element.48), channel_id=1, source_target_pairs={{0,16},{4,20},{8,24},{12,28},{16,0},{20,4},{24,8},{28,12},{1,17},{... | collective-permute-start | bytes 196616 | tf_op jit(solution)/shard_map/ppermute | solution.py:50
  30.8 12.6 %collective-permute-start.14 = (bf16[128,256]{1,0:T(8,128)(2,1)S(1)}, bf16[128,256]{1,0:T(8,128)(2,1)}, u32[]{:S(2)}, u32[]{:S(2)}) collective-permute-start(bf16[128,256]{1,0:T(8,128)(2,1)S(1)} %get-tuple-element.48), channel_id=1, source_target_pairs={{0,8},{4,12},{8,0},{12,4},{16,24},{20,28},{24,16},{28,20},{1,9},{5... | collective-permute-start | bytes 196616 | tf_op jit(solution)/shard_map/ppermute | solution.py:50
  31.5 29.1 %collective-permute-start.2 = (bf16[128,1024]{1,0:T(8,128)(2,1)S(1)}, bf16[128,1024]{1,0:T(8,128)(2,1)S(1)}, u32[]{:S(2)}, u32[]{:S(2)}) collective-permute-start(bf16[128,1024]{1,0:T(8,128)(2,1)S(1)} %copy-done.10), channel_id=1, source_target_pairs={{0,3},{1,2},{2,1},{3,0},{4,7},{5,6},{6,5},{7,4},{8,11},{9,10},{10,... | collective-permute-start | bytes 786440 | tf_op jit(solution)/shard_map/ppermute | solution.py:50
  42.3 18.4 %collective-permute-start.1 = (bf16[128,1024]{1,0:T(8,128)(2,1)S(1)}, bf16[128,1024]{1,0:T(8,128)(2,1)S(1)}, u32[]{:S(2)}, u32[]{:S(2)}) collective-permute-start(bf16[128,1024]{1,0:T(8,128)(2,1)S(1)} %copy-done.10), channel_id=1, source_target_pairs={{0,2},{1,3},{2,0},{3,1},{4,6},{5,7},{6,4},{7,5},{8,10},{9,11},{10,... | collective-permute-start | bytes 786440 | tf_op jit(solution)/shard_map/ppermute | solution.py:50
  42.8 20.4 %collective-permute-start = (bf16[128,1024]{1,0:T(8,128)(2,1)S(1)}, bf16[128,1024]{1,0:T(8,128)(2,1)S(1)}, u32[]{:S(2)}, u32[]{:S(2)}) collective-permute-start(bf16[128,1024]{1,0:T(8,128)(2,1)S(1)} %copy-done.10), channel_id=1, source_target_pairs={{0,1},{1,0},{2,3},{3,2},{4,5},{5,4},{6,7},{7,6},{8,9},{9,8},{10,11... | collective-permute-start | bytes 786440 | tf_op jit(solution)/shard_map/ppermute | solution.py:50
  44.4 15.6 %collective-permute-start.7 = (bf16[128,768]{1,0:T(8,128)(2,1)S(1)}, bf16[128,768]{1,0:T(8,128)(2,1)S(1)}, u32[]{:S(2)}, u32[]{:S(2)}) collective-permute-start(bf16[128,768]{1,0:T(8,128)(2,1)S(1)} %get-tuple-element.50), channel_id=1, source_target_pairs={{0,8},{4,12},{8,0},{12,4},{16,24},{20,28},{24,16},{28,20},{1,9},{5... | collective-permute-start | bytes 589832 | tf_op jit(solution)/shard_map/ppermute | solution.py:50
  60.7 15.7 %collective-permute-start.27 = (bf16[128,1024]{1,0:T(8,128)(2,1)S(1)}, bf16[128,1024]{1,0:T(8,128)(2,1)S(1)}, u32[]{:S(2)}, u32[]{:S(2)}) collective-permute-start(bf16[128,1024]{1,0:T(8,128)(2,1)S(1)} %get-tuple-element.44), channel_id=1, source_target_pairs={{0,24},{4,28},{8,16},{12,20},{16,8},{20,12},{24,0},{28,4},{1,25},{... | collective-permute-start | bytes 786440 | tf_op jit(solution)/shard_map/ppermute | solution.py:50
  63.3 33.8 %collective-permute-start.26 = (bf16[128,1024]{1,0:T(8,128)(2,1)S(1)}, bf16[128,1024]{1,0:T(8,128)(2,1)S(1)}, u32[]{:S(2)}, u32[]{:S(2)}) collective-permute-start(bf16[128,1024]{1,0:T(8,128)(2,1)S(1)} %get-tuple-element.44), channel_id=1, source_target_pairs={{0,16},{4,20},{8,24},{12,28},{16,0},{20,4},{24,8},{28,12},{1,17},{... | collective-permute-start | bytes 786440 | tf_op jit(solution)/shard_map/ppermute | solution.py:50
  64.7 32.4 %collective-permute-start.25 = (bf16[128,1024]{1,0:T(8,128)(2,1)S(1)}, bf16[128,1024]{1,0:T(8,128)(2,1)S(1)}, u32[]{:S(2)}, u32[]{:S(2)}) collective-permute-start(bf16[128,1024]{1,0:T(8,128)(2,1)S(1)} %get-tuple-element.44), channel_id=1, source_target_pairs={{0,8},{4,12},{8,0},{12,4},{16,24},{20,28},{24,16},{28,20},{1,9},{5... | collective-permute-start | bytes 786440 | tf_op jit(solution)/shard_map/ppermute | solution.py:50
  70.0 29.2 %collective-permute-start.23 = (bf16[128,1024]{1,0:T(8,128)(2,1)S(1)}, bf16[128,1024]{1,0:T(8,128)(2,1)S(1)}, u32[]{:S(2)}, u32[]{:S(2)}) collective-permute-start(bf16[128,1024]{1,0:T(8,128)(2,1)S(1)} %bitcast.405), channel_id=1, source_target_pairs={{0,24},{4,28},{8,16},{12,20},{16,8},{20,12},{24,0},{28,4},{1,25},{... | collective-permute-start | bytes 786440 | tf_op jit(solution)/shard_map/ppermute | solution.py:50
  74.6 32.7 %collective-permute-start.22 = (bf16[128,1024]{1,0:T(8,128)(2,1)S(1)}, bf16[128,1024]{1,0:T(8,128)(2,1)S(1)}, u32[]{:S(2)}, u32[]{:S(2)}) collective-permute-start(bf16[128,1024]{1,0:T(8,128)(2,1)S(1)} %bitcast.406), channel_id=1, source_target_pairs={{0,16},{4,20},{8,24},{12,28},{16,0},{20,4},{24,8},{28,12},{1,17},{... | collective-permute-start | bytes 786440 | tf_op jit(solution)/shard_map/ppermute | solution.py:50
  76.5 33.3 %collective-permute-start.21 = (bf16[128,1024]{1,0:T(8,128)(2,1)S(1)}, bf16[128,1024]{1,0:T(8,128)(2,1)S(1)}, u32[]{:S(2)}, u32[]{:S(2)}) collective-permute-start(bf16[128,1024]{1,0:T(8,128)(2,1)S(1)} %bitcast.407), channel_id=1, source_target_pairs={{0,8},{4,12},{8,0},{12,4},{16,24},{20,28},{24,16},{28,20},{1,9},{5... | collective-permute-start | bytes 786440 | tf_op jit(solution)/shard_map/ppermute | solution.py:50
  97.1 27.5 %collective-permute-start.10 = (bf16[4,128,768]{2,1,0:T(8,128)(2,1)S(1)}, bf16[4,128,768]{2,1,0:T(8,128)(2,1)S(1)}, u32[]{:S(2)}, u32[]{:S(2)}) collective-permute-start(bf16[4,128,768]{2,1,0:T(8,128)(2,1)S(1)} %pad_maximum_fusion.3), channel_id=1, source_target_pairs={{0,4},{4,0},{8,12},{12,8},{16,20},{20,16},{24,28},{28,24},{1,5},{5... | collective-permute-start | bytes 2359304 | tf_op jit(solution)/shard_map/ppermute | solution.py:50
  97.1 14.9 %collective-permute-start.18 = (bf16[1024,256]{1,0:T(8,128)(2,1)S(1)}, bf16[1024,256]{1,0:T(8,128)(2,1)S(1)}, u32[]{:S(2)}, u32[]{:S(2)}) collective-permute-start(bf16[1024,256]{1,0:T(8,128)(2,1)S(1)} %bitcast.384), channel_id=1, source_target_pairs={{0,1},{1,0},{2,3},{3,2},{4,5},{5,4},{6,7},{7,6},{8,9},{9,8},{10,11... | collective-permute-start | bytes 1572872 | tf_op jit(solution)/shard_map/ppermute | solution.py:50
  99.2 25.2 %collective-permute-start.19 = (bf16[1024,256]{1,0:T(8,128)(2,1)S(1)}, bf16[1024,256]{1,0:T(8,128)(2,1)S(1)}, u32[]{:S(2)}, u32[]{:S(2)}) collective-permute-start(bf16[1024,256]{1,0:T(8,128)(2,1)S(1)} %bitcast.385), channel_id=1, source_target_pairs={{0,2},{1,3},{2,0},{3,1},{4,6},{5,7},{6,4},{7,5},{8,10},{9,11},{10,... | collective-permute-start | bytes 1572872 | tf_op jit(solution)/shard_map/ppermute | solution.py:50
  107.3 17.3 %collective-permute-start.20 = (bf16[1024,256]{1,0:T(8,128)(2,1)S(1)}, bf16[1024,256]{1,0:T(8,128)(2,1)S(1)}, u32[]{:S(2)}, u32[]{:S(2)}) collective-permute-start(bf16[1024,256]{1,0:T(8,128)(2,1)S(1)} %bitcast.386), channel_id=1, source_target_pairs={{0,3},{1,2},{2,1},{3,0},{4,7},{5,6},{6,5},{7,4},{8,11},{9,10},{10,... | collective-permute-start | bytes 1572872 | tf_op jit(solution)/shard_map/ppermute | solution.py:50
  109.8 46.9 %collective-permute-start.28 = (bf16[4,128,1024]{2,1,0:T(8,128)(2,1)}, bf16[4,128,1024]{2,1,0:T(8,128)(2,1)}, u32[]{:S(2)}, u32[]{:S(2)}) collective-permute-start(bf16[4,128,1024]{2,1,0:T(8,128)(2,1)} %pad_maximum_fusion.2), channel_id=1, source_target_pairs={{0,4},{4,0},{8,12},{12,8},{16,20},{20,16},{24,28},{28,24},{1,5},{5... | collective-permute-start | bytes 3145736 | tf_op jit(solution)/shard_map/ppermute | solution.py:50
  112.0 46.4 %collective-permute-start.24 = (bf16[4,128,1024]{2,1,0:T(8,128)(2,1)}, bf16[4,128,1024]{2,1,0:T(8,128)(2,1)}, u32[]{:S(2)}, u32[]{:S(2)}) collective-permute-start(bf16[4,128,1024]{2,1,0:T(8,128)(2,1)} %pad_maximum_fusion.1), channel_id=1, source_target_pairs={{0,4},{4,0},{8,12},{12,8},{16,20},{20,16},{24,28},{28,24},{1,5},{5... | collective-permute-start | bytes 3145736 | tf_op jit(solution)/shard_map/ppermute | solution.py:50
  138.0 14.4 %collective-permute-start.11 = (bf16[512,256]{0,1:T(8,128)(2,1)S(1)}, bf16[512,256]{0,1:T(8,128)(2,1)S(1)}, u32[]{:S(2)}, u32[]{:S(2)}) collective-permute-start(bf16[512,256]{0,1:T(8,128)(2,1)S(1)} %get-tuple-element.97), channel_id=1, source_target_pairs={{0,1},{1,0},{2,3},{3,2},{4,5},{5,4},{6,7},{7,6},{8,9},{9,8},{10,11... | collective-permute-start | bytes 786440 | tf_op jit(solution)/shard_map/ppermute | solution.py:50
  139.2 13.2 %collective-permute-start.12 = (bf16[512,256]{0,1:T(8,128)(2,1)S(1)}, bf16[512,256]{0,1:T(8,128)(2,1)S(1)}, u32[]{:S(2)}, u32[]{:S(2)}) collective-permute-start(bf16[512,256]{0,1:T(8,128)(2,1)S(1)} %get-tuple-element.97), channel_id=1, source_target_pairs={{0,2},{1,3},{2,0},{3,1},{4,6},{5,7},{6,4},{7,5},{8,10},{9,11},{10,... | collective-permute-start | bytes 786440 | tf_op jit(solution)/shard_map/ppermute | solution.py:50
  190.6 24.9 %collective-permute-start.31 = (bf16[128,1024]{1,0:T(8,128)(2,1)S(1)}, bf16[128,1024]{1,0:T(8,128)(2,1)S(1)}, u32[]{:S(2)}, u32[]{:S(2)}) collective-permute-start(bf16[128,1024]{1,0:T(8,128)(2,1)S(1)} %get-tuple-element.71), channel_id=1, source_target_pairs={{0,3},{1,2},{2,1},{3,0},{4,7},{5,6},{6,5},{7,4},{8,11},{9,10},{10,... | collective-permute-start | bytes 786440 | tf_op jit(solution)/shard_map/ppermute | solution.py:50
  192.2 23.3 %collective-permute-start.30 = (bf16[128,1024]{1,0:T(8,128)(2,1)S(1)}, bf16[128,1024]{1,0:T(8,128)(2,1)S(1)}, u32[]{:S(2)}, u32[]{:S(2)}) collective-permute-start(bf16[128,1024]{1,0:T(8,128)(2,1)S(1)} %get-tuple-element.72), channel_id=1, source_target_pairs={{0,2},{1,3},{2,0},{3,1},{4,6},{5,7},{6,4},{7,5},{8,10},{9,11},{10,... | collective-permute-start | bytes 786440 | tf_op jit(solution)/shard_map/ppermute | solution.py:50
  192.8 13.7 %collective-permute-start.37 = (bf16[128,1024]{1,0:T(8,128)(2,1)S(1)}, bf16[128,1024]{1,0:T(8,128)(2,1)S(1)}, u32[]{:S(2)}, u32[]{:S(2)}) collective-permute-start(bf16[128,1024]{1,0:T(8,128)(2,1)S(1)} %get-tuple-element.68), channel_id=1, source_target_pairs={{0,3},{1,2},{2,1},{3,0},{4,7},{5,6},{6,5},{7,4},{8,11},{9,10},{10,... | collective-permute-start | bytes 786440 | tf_op jit(solution)/shard_map/ppermute | solution.py:50
  194.3 20.4 %collective-permute-start.36 = (bf16[128,1024]{1,0:T(8,128)(2,1)S(1)}, bf16[128,1024]{1,0:T(8,128)(2,1)S(1)}, u32[]{:S(2)}, u32[]{:S(2)}) collective-permute-start(bf16[128,1024]{1,0:T(8,128)(2,1)S(1)} %get-tuple-element.69), channel_id=1, source_target_pairs={{0,2},{1,3},{2,0},{3,1},{4,6},{5,7},{6,4},{7,5},{8,10},{9,11},{10,... | collective-permute-start | bytes 786440 | tf_op jit(solution)/shard_map/ppermute | solution.py:50
  195.7 19.0 %collective-permute-start.35 = (bf16[128,1024]{1,0:T(8,128)(2,1)S(1)}, bf16[128,1024]{1,0:T(8,128)(2,1)S(1)}, u32[]{:S(2)}, u32[]{:S(2)}) collective-permute-start(bf16[128,1024]{1,0:T(8,128)(2,1)S(1)} %get-tuple-element.67), channel_id=1, source_target_pairs={{0,1},{1,0},{2,3},{3,2},{4,5},{5,4},{6,7},{7,6},{8,9},{9,8},{10,11... | collective-permute-start | bytes 786440 | tf_op jit(solution)/shard_map/ppermute | solution.py:50
  214.7 69.7 %collective-permute-start.68 = (bf16[4,128,1024]{2,1,0:T(8,128)(2,1)}, bf16[4,128,1024]{2,1,0:T(8,128)(2,1)}, u32[]{:S(2)}, u32[]{:S(2)}) collective-permute-start(bf16[4,128,1024]{2,1,0:T(8,128)(2,1)} %dynamic-slice_bitcast_fusion.1), channel_id=1, source_target_pairs={{0,4},{4,0},{8,12},{12,8},{16,20},{20,16},{24,28},{28,24},{1,5},{5... | collective-permute-start | bytes 3145736 | tf_op jit(solution)/shard_map/ppermute | solution.py:50
  214.7 77.8 %collective-permute-start.75 = (bf16[4,128,1024]{2,1,0:T(8,128)(2,1)}, bf16[4,128,1024]{2,1,0:T(8,128)(2,1)}, u32[]{:S(2)}, u32[]{:S(2)}) collective-permute-start(bf16[4,128,1024]{2,1,0:T(8,128)(2,1)} %dynamic-slice_bitcast_fusion), channel_id=1, source_target_pairs={{0,4},{4,0},{8,12},{12,8},{16,20},{20,16},{24,28},{28,24},{1,5},{5... | collective-permute-start | bytes 3145736 | tf_op jit(solution)/shard_map/ppermute | solution.py:50
  224.0 15.9 %collective-permute-start.60 = (bf16[128,256]{1,0:T(8,128)(2,1)S(1)}, bf16[128,256]{1,0:T(8,128)(2,1)S(1)}, u32[]{:S(2)}, u32[]{:S(2)}) collective-permute-start(bf16[128,256]{1,0:T(8,128)(2,1)S(1)} %get-tuple-element.82), channel_id=1, source_target_pairs={{0,3},{1,2},{2,1},{3,0},{4,7},{5,6},{6,5},{7,4},{8,11},{9,10},{10,... | collective-permute-start | bytes 196616 | tf_op jit(solution)/shard_map/ppermute | solution.py:50
  226.1 16.0 %collective-permute-start.59 = (bf16[128,256]{1,0:T(8,128)(2,1)S(1)}, bf16[128,256]{1,0:T(8,128)(2,1)S(1)}, u32[]{:S(2)}, u32[]{:S(2)}) collective-permute-start(bf16[128,256]{1,0:T(8,128)(2,1)S(1)} %get-tuple-element.80), channel_id=1, source_target_pairs={{0,2},{1,3},{2,0},{3,1},{4,6},{5,7},{6,4},{7,5},{8,10},{9,11},{10,... | collective-permute-start | bytes 196616 | tf_op jit(solution)/shard_map/ppermute | solution.py:50
  226.1 16.0 %collective-permute-start.58 = (bf16[128,256]{1,0:T(8,128)(2,1)S(1)}, bf16[128,256]{1,0:T(8,128)(2,1)S(1)}, u32[]{:S(2)}, u32[]{:S(2)}) collective-permute-start(bf16[128,256]{1,0:T(8,128)(2,1)S(1)} %get-tuple-element.81), channel_id=1, source_target_pairs={{0,1},{1,0},{2,3},{3,2},{4,5},{5,4},{6,7},{7,6},{8,9},{9,8},{10,11... | collective-permute-start | bytes 196616 | tf_op jit(solution)/shard_map/ppermute | solution.py:50
  273.4 17.4 %collective-permute-start.51 = (bf16[4,128,768]{2,1,0:T(8,128)(2,1)S(1)}, bf16[4,128,768]{2,1,0:T(8,128)(2,1)S(1)}, u32[]{:S(2)}, u32[]{:S(2)}) collective-permute-start(bf16[4,128,768]{2,1,0:T(8,128)(2,1)S(1)} %copy-done.38), channel_id=1, source_target_pairs={{0,4},{4,0},{8,12},{12,8},{16,20},{20,16},{24,28},{28,24},{1,5},{5... | collective-permute-start | bytes 2359304 | tf_op jit(solution)/shard_map/ppermute | solution.py:50
  287.8 36.2 %collective-permute-start.70 = (bf16[128,1024]{1,0:T(8,128)(2,1)S(1)}, bf16[128,1024]{1,0:T(8,128)(2,1)S(1)}, u32[]{:S(2)}, u32[]{:S(2)}) collective-permute-start(bf16[128,1024]{1,0:T(8,128)(2,1)S(1)} %get-tuple-element.62), channel_id=1, source_target_pairs={{0,16},{4,20},{8,24},{12,28},{16,0},{20,4},{24,8},{28,12},{1,17},{... | collective-permute-start | bytes 786440 | tf_op jit(solution)/shard_map/ppermute | solution.py:50
  287.8 36.2 %collective-permute-start.69 = (bf16[128,1024]{1,0:T(8,128)(2,1)S(1)}, bf16[128,1024]{1,0:T(8,128)(2,1)S(1)}, u32[]{:S(2)}, u32[]{:S(2)}) collective-permute-start(bf16[128,1024]{1,0:T(8,128)(2,1)S(1)} %get-tuple-element.60), channel_id=1, source_target_pairs={{0,8},{4,12},{8,0},{12,4},{16,24},{20,28},{24,16},{28,20},{1,9},{5... | collective-permute-start | bytes 786440 | tf_op jit(solution)/shard_map/ppermute | solution.py:50
  291.1 36.0 %collective-permute-start.54 = (bf16[128,768]{1,0:T(8,128)(2,1)S(1)}, bf16[128,768]{1,0:T(8,128)(2,1)S(1)}, u32[]{:S(2)}, u32[]{:S(2)}) collective-permute-start(bf16[128,768]{1,0:T(8,128)(2,1)S(1)} %get-tuple-element.74), channel_id=1, source_target_pairs={{0,24},{4,28},{8,16},{12,20},{16,8},{20,12},{24,0},{28,4},{1,25},{... | collective-permute-start | bytes 589832 | tf_op jit(solution)/shard_map/ppermute | solution.py:50
  294.3 54.8 %collective-permute-start.78 = (bf16[128,1024]{1,0:T(8,128)(2,1)S(1)}, bf16[128,1024]{1,0:T(8,128)(2,1)S(1)}, u32[]{:S(2)}, u32[]{:S(2)}) collective-permute-start(bf16[128,1024]{1,0:T(8,128)(2,1)S(1)} %get-tuple-element.58), channel_id=1, source_target_pairs={{0,24},{4,28},{8,16},{12,20},{16,8},{20,12},{24,0},{28,4},{1,25},{... | collective-permute-start | bytes 786440 | tf_op jit(solution)/shard_map/ppermute | solution.py:50
  297.5 53.6 %collective-permute-start.77 = (bf16[128,1024]{1,0:T(8,128)(2,1)S(1)}, bf16[128,1024]{1,0:T(8,128)(2,1)S(1)}, u32[]{:S(2)}, u32[]{:S(2)}) collective-permute-start(bf16[128,1024]{1,0:T(8,128)(2,1)S(1)} %get-tuple-element.59), channel_id=1, source_target_pairs={{0,16},{4,20},{8,24},{12,28},{16,0},{20,4},{24,8},{28,12},{1,17},{... | collective-permute-start | bytes 786440 | tf_op jit(solution)/shard_map/ppermute | solution.py:50
  324.0 27.8 %collective-permute-start.76 = (bf16[128,1024]{1,0:T(8,128)(2,1)S(1)}, bf16[128,1024]{1,0:T(8,128)(2,1)S(1)}, u32[]{:S(2)}, u32[]{:S(2)}) collective-permute-start(bf16[128,1024]{1,0:T(8,128)(2,1)S(1)} %get-tuple-element.57), channel_id=1, source_target_pairs={{0,8},{4,12},{8,0},{12,4},{16,24},{20,28},{24,16},{28,20},{1,9},{5... | collective-permute-start | bytes 786440 | tf_op jit(solution)/shard_map/ppermute | solution.py:50
  324.0 23.3 %collective-permute-start.53 = (bf16[128,768]{1,0:T(8,128)(2,1)S(1)}, bf16[128,768]{1,0:T(8,128)(2,1)S(1)}, u32[]{:S(2)}, u32[]{:S(2)}) collective-permute-start(bf16[128,768]{1,0:T(8,128)(2,1)S(1)} %get-tuple-element.75), channel_id=1, source_target_pairs={{0,16},{4,20},{8,24},{12,28},{16,0},{20,4},{24,8},{28,12},{1,17},{... | collective-permute-start | bytes 589832 | tf_op jit(solution)/shard_map/ppermute | solution.py:50
  327.1 20.8 %collective-permute-start.52 = (bf16[128,768]{1,0:T(8,128)(2,1)S(1)}, bf16[128,768]{1,0:T(8,128)(2,1)S(1)}, u32[]{:S(2)}, u32[]{:S(2)}) collective-permute-start(bf16[128,768]{1,0:T(8,128)(2,1)S(1)} %get-tuple-element.73), channel_id=1, source_target_pairs={{0,8},{4,12},{8,0},{12,4},{16,24},{20,28},{24,16},{28,20},{1,9},{5... | collective-permute-start | bytes 589832 | tf_op jit(solution)/shard_map/ppermute | solution.py:50
  347.3 34.1 %collective-permute-start.72 = (bf16[128,1024]{1,0:T(8,128)(2,1)S(1)}, bf16[128,1024]{1,0:T(8,128)(2,1)S(1)}, u32[]{:S(2)}, u32[]{:S(2)}) collective-permute-start(bf16[128,1024]{1,0:T(8,128)(2,1)S(1)} %get-tuple-element.30), channel_id=1, source_target_pairs={{0,1},{1,0},{2,3},{3,2},{4,5},{5,4},{6,7},{7,6},{8,9},{9,8},{10,11... | collective-permute-start | bytes 786440 | tf_op jit(solution)/shard_map/ppermute | solution.py:50
  348.0 35.3 %collective-permute-start.73 = (bf16[128,1024]{1,0:T(8,128)(2,1)S(1)}, bf16[128,1024]{1,0:T(8,128)(2,1)S(1)}, u32[]{:S(2)}, u32[]{:S(2)}) collective-permute-start(bf16[128,1024]{1,0:T(8,128)(2,1)S(1)} %get-tuple-element.30), channel_id=1, source_target_pairs={{0,2},{1,3},{2,0},{3,1},{4,6},{5,7},{6,4},{7,5},{8,10},{9,11},{10,... | collective-permute-start | bytes 786440 | tf_op jit(solution)/shard_map/ppermute | solution.py:50
  349.1 34.3 %collective-permute-start.74 = (bf16[128,1024]{1,0:T(8,128)(2,1)S(1)}, bf16[128,1024]{1,0:T(8,128)(2,1)S(1)}, u32[]{:S(2)}, u32[]{:S(2)}) collective-permute-start(bf16[128,1024]{1,0:T(8,128)(2,1)S(1)} %get-tuple-element.30), channel_id=1, source_target_pairs={{0,3},{1,2},{2,1},{3,0},{4,7},{5,6},{6,5},{7,4},{8,11},{9,10},{10,... | collective-permute-start | bytes 786440 | tf_op jit(solution)/shard_map/ppermute | solution.py:50
  351.1 14.9 %collective-permute-start.55 = (bf16[128,768]{1,0:T(8,128)(2,1)S(1)}, bf16[128,768]{1,0:T(8,128)(2,1)S(1)}, u32[]{:S(2)}, u32[]{:S(2)}) collective-permute-start(bf16[128,768]{1,0:T(8,128)(2,1)S(1)} %get-tuple-element.34), channel_id=1, source_target_pairs={{0,1},{1,0},{2,3},{3,2},{4,5},{5,4},{6,7},{7,6},{8,9},{9,8},{10,11... | collective-permute-start | bytes 589832 | tf_op jit(solution)/shard_map/ppermute | solution.py:50
  352.3 31.1 %collective-permute-start.79 = (bf16[128,1024]{1,0:T(8,128)(2,1)S(1)}, bf16[128,1024]{1,0:T(8,128)(2,1)S(1)}, u32[]{:S(2)}, u32[]{:S(2)}) collective-permute-start(bf16[128,1024]{1,0:T(8,128)(2,1)S(1)} %get-tuple-element.28), channel_id=1, source_target_pairs={{0,1},{1,0},{2,3},{3,2},{4,5},{5,4},{6,7},{7,6},{8,9},{9,8},{10,11... | collective-permute-start | bytes 786440 | tf_op jit(solution)/shard_map/ppermute | solution.py:50
  (98 other events, 1061.9 us)

commit v2 on v1

--- a/solution.py
+++ b/solution.py
@@ -3,6 +3,8 @@
 import jax
 import jax.numpy as jnp
 from jax import lax
+from jax.experimental import pallas as pl
+from jax.experimental.pallas import tpu as pltpu
 from jax.sharding import PartitionSpec as P
 
 HEADS = 16
@@ -122,7 +124,7 @@
     return jnp.concatenate(outs, axis=1).astype(bf16)
 
 
-def body(
+def body_any(
     tokens,
     segment_ids,
     first_gain,
@@ -358,7 +360,7 @@
         grad_factor_two,
     )
     packed = jnp.concatenate([v.reshape(fsdp, -1) for v in vector_grads], axis=1)
-    packed = sum(from_others(packed))
+    packed = lax.psum(packed, "seq")
     vector_total = scatter_fsdp(packed.astype(bf16)[:, None, :])[0]
     outs = []
     offset = 0
@@ -386,6 +388,487 @@
     )
 
 
+def spec(kind=pltpu.VMEM):
+    return pl.BlockSpec(memory_space=kind)
+
+
+def shape(dims, kind):
+    return jax.ShapeDtypeStruct(dims, kind)
+
+
+def call(kernel, where, ins, outs, flops=0, name=None, scratch=(), in_hbm=(), out_hbm=False):
+    moved = sum(x.size * x.dtype.itemsize for x in ins) + sum(
+        math.prod(o.shape) * o.dtype.itemsize for o in outs
+    )
+    in_specs = [spec(pl.ANY) if i in in_hbm else spec() for i in range(len(ins))]
+    return pl.pallas_call(
+        kernel,
+        out_shape=outs,
+        in_specs=[spec(pltpu.SMEM)] + in_specs,
+        out_specs=[spec(pl.ANY) if out_hbm else spec() for _ in outs],
+        scratch_shapes=list(scratch),
+        compiler_params=pltpu.CompilerParams(vmem_limit_bytes=50 * 1024 * 1024),
+        cost_estimate=pl.CostEstimate(flops=flops, bytes_accessed=moved, transcendentals=0),
+        name=name,
+    )(where, *ins)
+
+
+def at(index, size):
+    return pl.ds(pl.multiple_of(index * size, size), size)
+
+
+def prepare(where, w_in, w_out, w_up, w_down, tokens, grad, vec, first, second, rows, sems):
+    s = where[1]
+    shard, parts = w_in.shape[0], first.shape[1]
+    cols, out_cols = w_in.shape[1] // 4, w_out.shape[1] // 4
+    lane, wide = 128, w_up.shape[1] // 8
+    pairs = [
+        (w_in.at[:, at(s, cols)], first.at[0:shard, 0:cols]),
+        (w_out.at[:, at(s, out_cols)], first.at[0:shard, cols:parts]),
+        (vec, first.at[shard : shard + 16]),
+        (tokens, rows.at[0:shard]),
+        (grad, rows.at[shard : 2 * shard]),
+        (w_down.at[at(s, lane)], second.at[shard : 2 * shard]),
+    ]
+    for i in range(8):
+        lanes = pl.ds(pl.multiple_of(i * wide + s * lane, lane), lane)
+        pairs.append((w_up.at[:, lanes], second.at[0:shard, i * lane : (i + 1) * lane]))
+    copies = [pltpu.make_async_copy(a, b, sems.at[i]) for i, (a, b) in enumerate(pairs)]
+    for copy in copies:
+        copy.start()
+    for copy in copies:
+        copy.wait()
+
+
+def place_first(where, *refs):
+    blocks, (w_in, w_out, vecs) = refs[:8], refs[8:]
+    for j in range(8):
+        n = where[0] ^ j
+        w_in[at(n, 128)] = blocks[j][0:128, 0:768]
+        w_out[at(n, 128)] = blocks[j][0:128, 768:1024]
+        vecs[:, at(n, 128)] = blocks[j][128:144, 0:128].astype(f32)
+
+
+def column_segments(where, seg):
+    return jnp.concatenate([seg[at(where[1] ^ k, 128)] for k in range(4)], axis=0)
+
+
+def row_segments(where, seg):
+    return jnp.concatenate([seg[:, at(where[1] ^ k, 128)] for k in range(4)], axis=1)
+
+
+def attention(where, t0, t1, t2, t3, w_in, vecs, seg_col, seg_row, triple, attended, logsum, hidden):
+    gain, offset = vecs[0:1], vecs[1:2]
+    for k, ref in enumerate((t0, t1, t2, t3)):
+        normed, _ = normalize(ref[0:128].astype(f32))
+        hidden[k * 128 : (k + 1) * 128] = (normed * gain + offset).astype(bf16)
+    own = at(where[1], 256)
+    query, value = vecs[2:3, own], vecs[3:4, own]
+    zero = jnp.zeros((1, 64), f32)
+    pieces = []
+    for h in range(4):
+        pieces += [query[:, h * 64 : (h + 1) * 64], zero, value[:, h * 64 : (h + 1) * 64]]
+    triple[...] = (product(hidden[...], w_in[...]) + jnp.concatenate(pieces, axis=1)).astype(bf16)
+    same = column_segments(where, seg_col) == row_segments(where, seg_row)
+    outs = []
+    for h in range(4):
+        q, k, v = (triple[:, h * 192 + c * 64 : h * 192 + (c + 1) * 64] for c in range(3))
+        scores = jnp.where(same, product_right(q, k) * HEAD_DIM**-0.5, masked_value)
+        highest = jnp.max(scores, axis=1, keepdims=True)
+        powers = jnp.exp(scores - highest)
+        totals = jnp.sum(powers, axis=1, keepdims=True)
+        probs = (powers * (1.0 / totals)).astype(bf16)
+        outs.append(product(probs, v).astype(bf16))
+        logsum[:, h : h + 1] = highest + jnp.log(totals)
+    attended[...] = jnp.concatenate(outs, axis=1)
+
+
+def project(
+    where, a0, a1, a2, a3, w0, w1, w2, w3, t0, t1, t2, t3, vecs, full, hidden, own_middle, own_branch, branch
+):
+    for k, ref in enumerate((a0, a1, a2, a3)):
+        cols = at(where[1] ^ k, 256)
+        for j in range(4):
+            full[j * 128 : (j + 1) * 128, cols] = ref[(j ^ k) * 128 : ((j ^ k) + 1) * 128]
+    for k, ref in enumerate((w0, w1, w2, w3)):
+        branch[:, at(where[1] ^ k, 256)] = product(full[...], ref[...])
+    for r, ref in enumerate((t0, t1, t2, t3)):
+        rows = slice(r * 128, (r + 1) * 128)
+        piece = branch[rows] + vecs[4:5]
+        middle = ref[0:128].astype(f32) + vecs[5:6] * piece
+        normed, _ = normalize(middle)
+        hidden[rows] = (normed * vecs[6:7] + vecs[7:8]).astype(bf16)
+        if r == 0:
+            own_middle[...] = middle
+            own_branch[...] = piece
+
+
+def feed(where, *refs):
+    hidden, blocks, tokens, (vecs, seg_col) = refs[0], refs[1:9], refs[9:13], refs[13:15]
+    w_down, act, grad_two, grad_before, sums, p0, p1, p2, p3, w_up = refs[15:]
+    for j in range(8):
+        rows = at(where[0] ^ j, 128)
+        w_up[rows] = blocks[j][0:128]
+        w_down[rows] = blocks[j][128:256]
+    valid = (column_segments(where, seg_col) >= 0).astype(f32)
+    for k in range(4):
+        rows = slice(k * 128, (k + 1) * 128)
+        grad = tokens[k][128:256].astype(f32) * valid[rows]
+        grad_two[rows] = (grad * vecs[9:10]).astype(bf16)
+    bias = vecs[pl.ds(10 + where[1], 1)]
+    for c in range(4):
+        cols = slice(c * 256, (c + 1) * 256)
+        before = product(hidden[...], w_up[:, cols]) + bias[:, cols]
+        value, slope = gelu_pair(before)
+        act[:, cols] = value.astype(bf16)
+        back = (product_right(grad_two[...], w_down[cols]) * slope).astype(bf16)
+        grad_before[:, cols] = back
+        sums[:, cols] = jnp.sum(back.astype(f32), axis=0, keepdims=True)
+    p0[...] = product_right(grad_before[0:128], w_up[...])
+    for k, ref in ((1, p1), (2, p2), (3, p3)):
+        ref[...] = product_right(grad_before[k * 128 : (k + 1) * 128], w_up[...]).astype(bf16)
+
+
+def halves(where, mine, theirs, k, first_row, result):
+    rows = pl.ds(first_row, 128)
+
+    @pl.when(where[0] % 2 == 0)
+    def _():
+        mine[k, rows] = result[0:128]
+        theirs[k, rows] = result[128:256]
+
+    @pl.when(where[0] % 2 == 1)
+    def _():
+        mine[k, rows] = result[128:256]
+        theirs[k, rows] = result[0:128]
+
+
+def feed_weights(where, *refs):
+    hidden, grad_before, act, grad_two, w_down, t0, t1, t2, t3, vecs, seg_col = refs[:11]
+    mine, theirs, sums, o0, o1, o2, o3 = refs[11:]
+    for k in range(4):
+        cols = at((where[0] // 2) ^ k, 256)
+        up = product_left(hidden[:, cols], grad_before[...]).astype(bf16)
+        halves(where, mine, theirs, k, 0, up)
+        down = product_left(act[:, cols], grad_two[...]).astype(bf16)
+        halves(where, mine, theirs, k, 128, down)
+    valid = (column_segments(where, seg_col) >= 0).astype(f32)
+    scale = jnp.zeros((1, 1024), f32)
+    for k, (ref, out) in enumerate(((t0, o0), (t1, o1), (t2, o2), (t3, o3))):
+        rows = slice(k * 128, (k + 1) * 128)
+        part = product(act[rows], w_down[...])
+        grad = ref[128:256].astype(f32) * valid[rows]
+        out[...] = part.astype(out.dtype)
+        if k == 0:
+            part = part + vecs[8:9]
+        scale = scale + jnp.sum(grad * part, axis=0, keepdims=True)
+    sums[0:1] = jnp.sum(grad_two[0:128].astype(f32), axis=0, keepdims=True)
+    sums[1:2] = scale
+
+
+def middle_back(
+    where, p0, p1, p2, p3, own_middle, own_branch, t0, seg_col, vecs, w0, w1, w2, w3,
+    grad_middle, sums, m0, m1, m2, m3, attended, one,
+):
+    total = p0[...] + p1[...].astype(f32) + p2[...].astype(f32) + p3[...].astype(f32)
+    normed, spread = normalize(own_middle[...])
+    valid = (seg_col[at(where[1], 128)] >= 0).astype(f32)
+    back = t0[128:256].astype(f32) * valid + normalize_back(total * vecs[6:7], normed, spread)
+    grad_middle[...] = back
+    grad_one = (back * vecs[5:6]).astype(bf16)
+    one[...] = grad_one
+    sums[0:1] = jnp.sum(total * normed, axis=0, keepdims=True)
+    sums[1:2] = jnp.sum(total, axis=0, keepdims=True)
+    sums[2:3] = jnp.sum(back * own_branch[...], axis=0, keepdims=True)
+    sums[3:4] = jnp.sum(grad_one.astype(f32), axis=0, keepdims=True)
+    result = jnp.zeros((128, 1024), f32)
+    for k, ref in enumerate((w0, w1, w2, w3)):
+        result = result + product_right(one[:, at(where[1] ^ k, 256)], ref[...])
+    attended[...] = result.astype(bf16)
+    for k, ref in enumerate((m0, m1, m2, m3)):
+        cols = at(where[1] ^ k, 256)
+        ref[0:128] = attended[:, cols]
+        ref[128:256] = one[:, cols]
+
+
+def attention_back(
+    where, triple, logsum, m0, m1, m2, m3, seg_col, seg_row, w_in, t0, t1, t2, t3, o1, o2, o3,
+    grad_triple, sums, own, n1, n2, n3,
+):
+    same = column_segments(where, seg_col) == row_segments(where, seg_row)
+    grads = jnp.concatenate([m[0:128] for m in (m0, m1, m2, m3)], axis=0)
+    pieces = []
+    for h in range(4):
+        q, k, v = (triple[:, h * 192 + c * 64 : h * 192 + (c + 1) * 64] for c in range(3))
+        g = grads[:, h * 64 : (h + 1) * 64]
+        scores = jnp.where(same, product_right(q, k) * HEAD_DIM**-0.5, masked_value)
+        weights = jnp.exp(scores - logsum[:, h : h + 1])
+        grad_v = product_left(weights.astype(bf16), g)
+        grad_weights = product_right(g, v)
+        dots = jnp.sum(weights * grad_weights, axis=1, keepdims=True)
+        grad_scores = (weights * (grad_weights - dots)).astype(bf16)
+        grad_q = product(grad_scores, k) * HEAD_DIM**-0.5
+        grad_k = product_left(grad_scores, q) * HEAD_DIM**-0.5
+        pieces += [grad_q.astype(bf16), grad_k.astype(bf16), grad_v.astype(bf16)]
+    whole = jnp.concatenate(pieces, axis=1)
+    grad_triple[...] = whole
+    columns = jnp.sum(whole.astype(f32), axis=0, keepdims=True)
+    sums[...] = jnp.zeros(sums.shape, f32)
+    lanes = at(where[1], 256)
+    for row, c in ((2, 0), (3, 2)):
+        sums[row : row + 1, lanes] = jnp.concatenate(
+            [columns[:, h * 192 + c * 64 : h * 192 + (c + 1) * 64] for h in range(4)], axis=1
+        )
+    gain = jnp.zeros((1, 1024), f32)
+    offset = jnp.zeros((1, 1024), f32)
+    sent = ((t0, own, None), (t1, n1, o1), (t2, n2, o2), (t3, n3, o3))
+    for k, (ref, out, other) in enumerate(sent):
+        part = product_right(grad_triple[k * 128 : (k + 1) * 128], w_in[...])
+        normed, _ = normalize(ref[0:128].astype(f32))
+        gain = gain + jnp.sum(part * normed, axis=0, keepdims=True)
+        offset = offset + jnp.sum(part, axis=0, keepdims=True)
+        if k == 0:
+            out[...] = part
+        else:
+            out[0:128] = part.astype(bf16)
+            out[128:256] = other[...]
+    sums[0:1] = gain
+    sums[1:2] = offset
+
+
+def attention_weights(
+    where, hidden, grad_triple, attended, m0, m1, m2, m3, up_sums, two_sums, mid_sums, one_sums,
+    mine, theirs, vecs,
+):
+    ones = jnp.concatenate([m[128:256] for m in (m0, m1, m2, m3)], axis=0)
+    vecs[...] = jnp.zeros(vecs.shape, f32)
+    vecs[0:4] = one_sums[...]
+    vecs[4:5] = mid_sums[3:4]
+    vecs[5:6] = mid_sums[2:3]
+    vecs[6:8] = mid_sums[0:2]
+    vecs[8:10] = two_sums[0:2]
+    vecs[pl.ds(10 + where[1], 1)] = up_sums[...]
+    blank = jnp.zeros((16, 896), bf16)
+    core = where[0] % 2
+    for k in range(4):
+        pair = (where[0] // 2) ^ k
+        cols = at(pair, 256)
+        left = product_left(hidden[:, cols], grad_triple[...]).astype(bf16)
+        right = product_left(attended[:, cols], ones).astype(bf16)
+        halves(where, mine, theirs, k, 0, jnp.concatenate([left, right], axis=1))
+        for ref, half in ((mine, core), (theirs, 1 - core)):
+            block = vecs[:, at(2 * pair + half, 128)].astype(bf16)
+            ref[k, 128:144] = jnp.concatenate([block, blank], axis=1)
+
+
+def finish_rows(where, own, n1, n2, n3, own_two, own_middle, grad_middle, t0, vecs, out, grad):
+    total = own[...] + sum(n[0:128].astype(f32) for n in (n1, n2, n3))
+    two = own_two[...] + sum(n[128:256].astype(f32) for n in (n1, n2, n3)) + vecs[8:9]
+    out[...] = (own_middle[...] + vecs[9:10] * two).astype(bf16)
+    normed, spread = normalize(t0[0:128].astype(f32))
+    grad[...] = (grad_middle[...] + normalize_back(total * vecs[0:1], normed, spread)).astype(bf16)
+
+
+def finish_feed(where, s0, s1, s2, s3, up, down):
+    for k, ref in enumerate((s0, s1, s2, s3)):
+        m = where[1] ^ k
+        down[at(m, 128)] = ref[128:256].astype(f32)
+        for n in range(8):
+            lanes = pl.ds(pl.multiple_of(n * 512 + m * 128, 128), 128)
+            up[:, lanes] = ref[0:128, n * 128 : (n + 1) * 128].astype(f32)
+
+
+def finish_attention(where, s0, s1, s2, s3, w_in, w_out, *refs):
+    outs, held = refs[:-1], refs[-1]
+    for k, ref in enumerate((s0, s1, s2, s3)):
+        m = where[1] ^ k
+        w_in[:, at(m, 768)] = ref[0:128, 0:768].astype(f32)
+        w_out[:, at(m, 256)] = ref[0:128, 768:1024].astype(f32)
+        held[m] = ref[128:144, 0:128].astype(f32)
+    total = held[0] + held[1] + held[2] + held[3]
+    for i in range(10):
+        outs[i][...] = total[i : i + 1]
+    outs[10][...] = jnp.concatenate([total[i : i + 1] for i in range(10, 14)], axis=1)
+
+
+def gather_blocks(x):
+    out = []
+    for k in range(4):
+        block = swap(x, "fsdp", 2 * k) if k else x
+        out += [block, swap(block, "fsdp", 1)]
+    return out
+
+
+def scatter_blocks(mine, theirs):
+    other = swap(theirs, "fsdp", 1)
+    sums = [(mine[k].astype(f32) + other[k].astype(f32)).astype(bf16) for k in range(4)]
+    total = sums[0].astype(f32)
+    for k in range(1, 4):
+        total = total + swap(sums[k], "fsdp", 2 * k).astype(f32)
+    return total.astype(bf16)
+
+
+def body(*args):
+    tokens, input_weight, up_weight = args[0], args[4], args[12]
+    fits = (
+        lax.axis_size("seq") == 4
+        and lax.axis_size("fsdp") == 8
+        and tokens.shape == (128, 1024)
+        and input_weight.shape == (128, 3072)
+        and up_weight.shape == (128, 4096)
+    )
+    return body_fast(*args) if fits else body_any(*args)
+
+
+def body_fast(
+    tokens,
+    segment_ids,
+    first_gain,
+    first_bias,
+    input_weight,
+    query_bias,
+    value_bias,
+    output_weight,
+    output_bias,
+    scale_one,
+    second_gain,
+    second_bias,
+    up_weight,
+    up_bias,
+    down_weight,
+    down_bias,
+    scale_two,
+    out_grad,
+):
+    where = jnp.stack([lax.axis_index("fsdp"), lax.axis_index("seq")]).astype(jnp.int32)
+    vectors = (
+        first_gain, first_bias, query_bias, value_bias, output_bias,
+        scale_one, second_gain, second_bias, down_bias, scale_two,
+    )
+    packed = jnp.pad(up_bias.reshape(4, 128), ((10, 2), (0, 896)))
+    for i, v in enumerate(vectors):
+        packed = packed + jnp.pad(v.reshape(1, 128), ((i, 15 - i), (0, 896)))
+    seg_col, seg_row = segment_ids.reshape(512, 1), segment_ids.reshape(1, 512)
+    mat = shape((512, 1024), bf16)
+    rows_f, rows_b = shape((128, 1024), f32), shape((128, 1024), bf16)
+
+    first, second, rows = call(
+        prepare,
+        where,
+        [input_weight, output_weight, up_weight, down_weight, tokens, out_grad, packed],
+        [shape((144, 1024), bf16), shape((256, 1024), bf16), shape((256, 1024), bf16)],
+        name="prepare",
+        scratch=[pltpu.SemaphoreType.DMA((14,))],
+        in_hbm=range(7),
+        out_hbm=True,
+    )
+    shared = from_others(rows)
+    first_blocks = gather_blocks(first)
+    w_in, w_out_own, vecs = call(
+        place_first,
+        where,
+        first_blocks,
+        [shape((1024, 768), bf16), shape((1024, 256), bf16), shape((16, 1024), f32)],
+        name="place_first",
+    )
+    second, _ = lax.optimization_barrier((second, vecs))
+    second_blocks = gather_blocks(second)
+    w_out = from_others(w_out_own)
+    triple, attended_own, logsum, hidden_one = call(
+        attention,
+        where,
+        shared + [w_in, vecs, seg_col, seg_row],
+        [shape((512, 768), bf16), shape((512, 256), bf16), shape((512, 128), f32), mat],
+        flops=2 * 512 * (1024 * 768 + 4 * 512 * 128),
+        name="attention",
+    )
+    attended, hidden_two, own_middle, own_branch = call(
+        project,
+        where,
+        from_others(attended_own) + w_out + shared + [vecs],
+        [mat, mat, rows_f, rows_f],
+        flops=2 * 512 * 1024 * 1024,
+        name="project",
+        scratch=[pltpu.VMEM((512, 1024), f32)],
+    )
+    w_down, act, grad_two, grad_before, up_sums, *partial = call(
+        feed,
+        where,
+        [hidden_two] + second_blocks + shared + [vecs, seg_col],
+        [shape((1024, 1024), bf16), mat, mat, mat, shape((1, 1024), f32), rows_f, rows_b, rows_b, rows_b],
+        flops=3 * 2 * 512 * 1024 * 1024,
+        name="feed",
+        scratch=[pltpu.VMEM((1024, 1024), bf16)],
+    )
+    second_mine, second_theirs, two_sums, *two = call(
+        feed_weights,
+        where,
+        [hidden_two, grad_before, act, grad_two, w_down] + shared + [vecs, seg_col],
+        [shape((4, 256, 1024), bf16)] * 2 + [shape((2, 1024), f32), rows_f, rows_b, rows_b, rows_b],
+        flops=3 * 2 * 512 * 1024 * 1024,
+        name="feed_weights",
+    )
+    grad_middle, mid_sums, *messages = call(
+        middle_back,
+        where,
+        exchange(partial) + [own_middle, own_branch, shared[0], seg_col, vecs] + w_out,
+        [rows_f, shape((4, 1024), f32)] + [shape((256, 256), bf16)] * 4,
+        flops=2 * 128 * 1024 * 1024,
+        name="middle_back",
+        scratch=[pltpu.VMEM((128, 1024), bf16), pltpu.VMEM((128, 1024), bf16)],
+    )
+    second_mine, second_theirs, messages = lax.optimization_barrier(
+        (second_mine, second_theirs, messages)
+    )
+    got = exchange(messages)
+    grad_triple, one_sums, own_one, *last = call(
+        attention_back,
+        where,
+        [triple, logsum] + got + [seg_col, seg_row, w_in] + shared + two[1:],
+        [shape((512, 768), bf16), shape((4, 1024), f32), rows_f] + [shape((256, 1024), bf16)] * 3,
+        flops=2 * 512 * (1024 * 768 + 4 * 512 * 64 * 5),
+        name="attention_back",
+    )
+    first_mine, first_theirs = call(
+        attention_weights,
+        where,
+        [hidden_one, grad_triple, attended] + got + [up_sums, two_sums, mid_sums, one_sums],
+        [shape((4, 144, 1024), bf16)] * 2,
+        flops=2 * 512 * 1024 * 1024,
+        name="attention_weights",
+        scratch=[pltpu.VMEM((16, 1024), f32)],
+    )
+    layer_out, tokens_grad = call(
+        finish_rows,
+        where,
+        exchange([own_one] + last) + [two[0], own_middle, grad_middle, shared[0], vecs],
+        [rows_b, rows_b],
+        name="finish_rows",
+    )
+    second_share = scatter_blocks(second_mine, second_theirs)
+    grad_up, grad_down = call(
+        finish_feed,
+        where,
+        from_others(second_share),
+        [shape((128, 4096), f32), shape((512, 1024), f32)],
+        name="finish_feed",
+    )
+    first_share = scatter_blocks(first_mine, first_theirs)
+    grad_in, grad_out, *small = call(
+        finish_attention,
+        where,
+        from_others(first_share),
+        [shape((128, 3072), f32), rows_f] + [shape((1, 128), f32)] * 10 + [shape((1, 512), f32)],
+        name="finish_attention",
+        scratch=[pltpu.VMEM((4, 16, 128), f32)],
+    )
+    g = [v.reshape(-1) for v in small]
+    return (
+        layer_out, tokens_grad, g[0], g[1], grad_in, g[2], g[3], grad_out, g[4],
+        g[5], g[6], g[7], grad_up, g[10], grad_down, g[8], g[9],
+    )
+
+
 def solution(mesh):
     rows, vec, mat = P(("fsdp", "seq"), None), P("fsdp"), P("fsdp", None)
     return jax.shard_map(

time: 397 us -> 294 us (0.74)
  the two profiles are of different devices: /device:TPU:0 before, /device:TPU:8 now
where the time goes in v2:
time: 294 us; the launch traced here: 293 us
  waiting for transfers between devices  164 us (56%)
  Pallas kernels  57.4 us (20%)
  starting transfers between devices  50.9 us (17%)
  local copies, waits for them, and re-layouts  13.3 us (5%)
  other arithmetic  7.11 us (2%)
    ppermute x46, waiting for transfers between devices, swap(): return lax.ppermute(x, axis, [(i, i ^ k) for i in range(count)])  164 us
    pallas_call x12, Pallas kernels, call(): pl.pallas_call(kernel, out_shape=outs, in_specs=[spec(pltpu.SMEM)] + in_s...  57.4 us
    ppermute x46, starting transfers between devices, swap(): return lax.ppermute(x, axis, [(i, i ^ k) for i in range(count)])  50.9 us
    unnamed x66, local copies, waits for them, and re-layouts  13.2 us
  transfers between devices with their start and end apart: 46, of which 24 were waited for; matrix products, arithmetic and copies ran while one was open for 2% of the time, Pallas kernels for 12%

profile of v2, /device:TPU:8, one launch (start us, length us, event | category | flops | bytes accessed | tf_op | source)
XLA Modules:
  0.0 293.5 jit_solution(11513332294837947327)
XLA Ops:
  6.8 1.8 prepare.1
  9.4 3.0 %collective-permute-start.6 = (bf16[144,1024]{1,0:T(8,128)(2,1)S(1)}, bf16[144,1024]{1,0:T(8,128)(2,1)S(1)}, u32[]{:S(2)}, u32[]{:S(2)}) collective-permute-start(bf16[144,1024]{1,0:T(8,128)(2,1)S(1)} %get-tuple-element.86.refs_0_), channel_id=1, source_target_pairs={{0,16},{4,20},{8,24},{12,28},{16,0},{20,4},{24,8},{28,12},{1,17},{... | collective-permute-start | bytes 884744 | tf_op jit(solution)/shard_map/ppermute | solution.py:52
  12.8 8.6 %collective-permute-done.4.refs_2_ = bf16[144,1024]{1,0:T(8,128)(2,1)S(1)} collective-permute-done((bf16[144,1024]{1,0:T(8,128)(2,1)S(1)}, bf16[144,1024]{1,0:T(8,128)(2,1)S(1)}, u32[]{:S(2)}, u32[]{:S(2)}) %collective-permute-start.4) | collective-permute-done | bytes 294944 | tf_op jit(solution)/shard_map/ppermute | solution.py:52
  21.5 1.7 collective-permute-start
  23.1 9.4 %collective-permute-done.6.refs_4_ = bf16[144,1024]{1,0:T(8,128)(2,1)S(1)} collective-permute-done((bf16[144,1024]{1,0:T(8,128)(2,1)S(1)}, bf16[144,1024]{1,0:T(8,128)(2,1)S(1)}, u32[]{:S(2)}, u32[]{:S(2)}) %collective-permute-start.6) | collective-permute-done | bytes 294944 | tf_op jit(solution)/shard_map/ppermute | solution.py:52
  34.0 4.3 %collective-permute-done.8.refs_6_ = bf16[144,1024]{1,0:T(8,128)(2,1)S(1)} collective-permute-done((bf16[144,1024]{1,0:T(8,128)(2,1)S(1)}, bf16[144,1024]{1,0:T(8,128)(2,1)S(1)}, u32[]{:S(2)}, u32[]{:S(2)}) %collective-permute-start.8) | collective-permute-done | bytes 294944 | tf_op jit(solution)/shard_map/ppermute | solution.py:52
  38.3 2.4 collective-permute-start.2
  46.0 2.4 place_first.1
  48.3 4.6 %collective-permute-done.1.t2.refs_11_.refs_7_ = bf16[256,1024]{1,0:T(8,128)(2,1)S(1)} collective-permute-done((bf16[256,1024]{1,0:T(8,128)(2,1)S(1)}, bf16[256,1024]{1,0:T(8,128)(2,1)S(1)}, u32[]{:S(2)}, u32[]{:S(2)}) %collective-permute-start.1) | collective-permute-done | bytes 524320 | tf_op jit(solution)/shard_map/ppermute | solution.py:52
  52.9 5.8 %attention.1 = (bf16[512,768]{1,0:T(8,128)(2,1)S(1)}, bf16[512,256]{1,0:T(8,128)(2,1)S(1)}, f32[512,128]{1,0:T(8,128)S(1)}, bf16[512,1024]{1,0:T(8,128)(2,1)}) custom-call(s32[2]{0:T(128)S(1)} %pad_add_fusion.1.where, bf16[256,1024]{1,0:T(8,128)(2,1)S(1)} %get-tuple-element.85.t0.refs_9_.refs_5_, ...), custom_call_target="tpu_custom_call" | custom-call | flops 1073741824 | bytes 6098944 | tf_op jit(solution)/shard_map/attention/pallas_call | solution.py:404
  66.1 2.7 collective-permute-done.10.a1
  68.9 2.4 collective-permute-start.17
  72.6 1.7 collective-permute-start.19
  75.4 1.6 collective-permute-start.21
  77.0 5.0 %collective-permute-done.13.w1 = bf16[1024,256]{1,0:T(8,128)(2,1)S(1)} collective-permute-done((bf16[1024,256]{1,0:T(8,128)(2,1)S(1)}, bf16[1024,256]{1,0:T(8,128)(2,1)S(1)}, u32[]{:S(2)}, u32[]{:S(2)}) %collective-permute-start.13) | collective-permute-done | bytes 524320 | tf_op jit(solution)/shard_map/ppermute | solution.py:52
  82.0 3.5 %collective-permute-start.15 = (bf16[1024,256]{1,0:T(8,128)(2,1)S(1)}, bf16[1024,256]{1,0:T(8,128)(2,1)S(1)}, u32[]{:S(2)}, u32[]{:S(2)}) collective-permute-start(bf16[1024,256]{1,0:T(8,128)(2,1)S(1)} %get-tuple-element.92.w0), channel_id=1, source_target_pairs={{0,3},{1,2},{2,1},{3,0},{4,7},{5,6},{6,5},{7,4},{8,11},{9,10},{10,... | collective-permute-start | bytes 1572872 | tf_op jit(solution)/shard_map/ppermute | solution.py:52
  85.4 8.1 %collective-permute-done.14.w2 = bf16[1024,256]{1,0:T(8,128)(2,1)S(1)} collective-permute-done((bf16[1024,256]{1,0:T(8,128)(2,1)S(1)}, bf16[1024,256]{1,0:T(8,128)(2,1)S(1)}, u32[]{:S(2)}, u32[]{:S(2)}) %collective-permute-start.14) | collective-permute-done | bytes 524320 | tf_op jit(solution)/shard_map/ppermute | solution.py:52
  94.1 10.0 %collective-permute-done.19.refs_5_ = bf16[256,1024]{1,0:T(8,128)(2,1)S(1)} collective-permute-done((bf16[256,1024]{1,0:T(8,128)(2,1)S(1)}, bf16[256,1024]{1,0:T(8,128)(2,1)S(1)}, u32[]{:S(2)}, u32[]{:S(2)}) %collective-permute-start.19) | collective-permute-done | bytes 524320 | tf_op jit(solution)/shard_map/ppermute | solution.py:52
  104.1 8.5 %collective-permute-done.21.refs_7_ = bf16[256,1024]{1,0:T(8,128)(2,1)S(1)} collective-permute-done((bf16[256,1024]{1,0:T(8,128)(2,1)S(1)}, bf16[256,1024]{1,0:T(8,128)(2,1)S(1)}, u32[]{:S(2)}, u32[]{:S(2)}) %collective-permute-start.21) | collective-permute-done | bytes 524320 | tf_op jit(solution)/shard_map/ppermute | solution.py:52
  113.5 5.2 %project.1 = (bf16[512,1024]{1,0:T(8,128)(2,1)}, bf16[512,1024]{1,0:T(8,128)(2,1)}, f32[128,1024]{1,0:T(8,128)S(1)}, f32[128,1024]{1,0:T(8,128)S(1)}) custom-call(s32[2]{0:T(128)S(1)} %pad_add_fusion.1.where, bf16[512,256]{1,0:T(8,128)(2,1)S(1)} %get-tuple-element.91.a0, bf16[512,256]{1,0:T(8,128)(2,1)S(1)} %collective-permute-done.10.a1, ...), custom_call_target="tpu_custom_call" | custom-call | flops 1073741824 | bytes 8454144 | tf_op jit(solution)/shard_map/project/pallas_call | solution.py:404
  119.7 8.5 %feed.1 = (bf16[1024,1024]{1,0:T(8,128)(2,1)}, bf16[512,1024]{1,0:T(8,128)(2,1)}, bf16[512,1024]{1,0:T(8,128)(2,1)}, bf16[512,1024]{1,0:T(8,128)(2,1)}, f32[1,10...) custom-call(s32[2]{0:T(128)S(1)} %pad_add_fusion.1.where, ...), custom_call_target="tpu_custom_call" | custom-call | flops 3221225472 | bytes 13965312 | tf_op jit(solution)/shard_map/feed/pallas_call | solution.py:404
  128.6 1.7 collective-permute-start.24
  130.3 1.5 collective-permute-start.25
  131.8 10.2 %feed_weights.1 = (bf16[4,256,1024]{2,1,0:T(8,128)(2,1)}, bf16[4,256,1024]{2,1,0:T(8,128)(2,1)}, f32[2,1024]{1,0:T(2,128)S(1)}, f32[128,1024]{1,0:T(8,128)S(1)},...) custom-call(s32[2]{0:T(128)S(1)} %pad_add_fusion.1.where, ...), custom_call_target="tpu_custom_call" | custom-call | flops 3221225472 | bytes 13969408 | tf_op jit(solution)/shard_map/feed_weights/pallas_call | solution.py:404
  142.1 1.8 collective-permute-done.25.p3
  143.9 3.2 %middle_back.1 = (f32[128,1024]{1,0:T(8,128)S(1)}, f32[4,1024]{1,0:T(4,128)S(1)}, bf16[256,256]{1,0:T(8,128)(2,1)S(1)}, bf16[256,256]{1,0:T(8,128)(2,1)S(1)}, bf...) custom-call(s32[2]{0:T(128)S(1)} %pad_add_fusion.1.where, f32[128,1024]{1,0:T(8,128)S(1)} %get-tuple-element.102.p0, ...), custom_call_target="tpu_custom_call" | custom-call | flops 268435456 | bytes 6113280 | tf_op jit(solution)/shard_map/middle_back/pallas_call | solution.py:404
  147.8 1.7 collective-permute-start.27
  150.7 2.8 collective-permute-done.26.m1
  153.5 2.6 collective-permute-done.27.m2
  156.2 8.4 %attention_back.1 = (bf16[512,768]{1,0:T(8,128)(2,1)}, f32[4,1024]{1,0:T(4,128)S(1)}, f32[128,1024]{1,0:T(8,128)S(1)}, bf16[256,1024]{1,0:T(8,128)(2,1)S(1)}, bf...) custom-call(s32[2]{0:T(128)S(1)} %pad_add_fusion.1.where, bf16[512,768]{1,0:T(8,128)(2,1)} %copy-done.12, ...), custom_call_target="tpu_custom_call" | custom-call | flops 1476395008 | bytes 8933376 | tf_op jit(solution)/shard_map/attention_back/pallas_call | solution.py:404
  165.8 4.4 %attention_weights.1 = (bf16[4,144,1024]{2,1,0:T(8,128)(2,1)}, bf16[4,144,1024]{2,1,0:T(8,128)(2,1)}) custom-call(s32[2]{0:T(128)S(1)} %pad_add_fusion.1.where, bf16[512,1024]{1,0:T(8,128)(2,1)S(1)} %copy-done.22, bf16[512,768]{1,0:T(8,128)(2,1)S(1)} %copy-done.24, bf16[512,1024]{1,0:T(8,128)(2,1)S(1)} %copy-done.23, ...), custom_call_target="tpu_custom_call" | custom-call | flops 1073741824 | bytes 5812224 | tf_op jit(solution)/shard_map/attention_weights/pallas_call | solution.py:404
  170.2 3.1 %collective-permute-done.32 = bf16[4,144,1024]{2,1,0:T(8,128)(2,1)S(1)} collective-permute-done((bf16[4,144,1024]{2,1,0:T(8,128)(2,1)}, bf16[4,144,1024]{2,1,0:T(8,128)(2,1)S(1)}, u32[]{:S(2)}, u32[]{:S(2)}) %collective-permute-start.32) | collective-permute-done | bytes 1179680 | tf_op jit(solution)/shard_map/ppermute | solution.py:52
  174.8 3.8 %collective-permute-start.34 = (bf16[144,1024]{1,0:T(8,128)(2,1)S(1)}, bf16[144,1024]{1,0:T(8,128)(2,1)S(1)}, u32[]{:S(2)}, u32[]{:S(2)}) collective-permute-start(bf16[144,1024]{1,0:T(8,128)(2,1)S(1)} %get-tuple-element.158), channel_id=1, source_target_pairs={{0,16},{4,20},{8,24},{12,28},{16,0},{20,4},{24,8},{28,12},{1,17},{... | collective-permute-start | bytes 884744 | tf_op jit(solution)/shard_map/ppermute | solution.py:52
  178.6 2.0 fusion.7
  180.6 1.5 collective-permute-start.40
  182.1 2.0 collective-permute-start.41
  184.2 4.0 %collective-permute-done.33 = bf16[144,1024]{1,0:T(8,128)(2,1)S(1)} collective-permute-done((bf16[144,1024]{1,0:T(8,128)(2,1)S(1)}, bf16[144,1024]{1,0:T(8,128)(2,1)S(1)}, u32[]{:S(2)}, u32[]{:S(2)}) %collective-permute-start.33) | collective-permute-done | bytes 294944 | tf_op jit(solution)/shard_map/ppermute | solution.py:52
  188.8 9.9 %collective-permute-done.34 = bf16[144,1024]{1,0:T(8,128)(2,1)S(1)} collective-permute-done((bf16[144,1024]{1,0:T(8,128)(2,1)S(1)}, bf16[144,1024]{1,0:T(8,128)(2,1)S(1)}, u32[]{:S(2)}, u32[]{:S(2)}) %collective-permute-start.34) | collective-permute-done | bytes 294944 | tf_op jit(solution)/shard_map/ppermute | solution.py:52
  199.0 6.1 %collective-permute-done.35 = bf16[144,1024]{1,0:T(8,128)(2,1)S(1)} collective-permute-done((bf16[144,1024]{1,0:T(8,128)(2,1)S(1)}, bf16[144,1024]{1,0:T(8,128)(2,1)S(1)}, u32[]{:S(2)}, u32[]{:S(2)}) %collective-permute-start.35) | collective-permute-done | bytes 294944 | tf_op jit(solution)/shard_map/ppermute | solution.py:52
  205.1 1.7 collective-permute-start.30
  208.1 3.0 %collective-permute-done.40 = bf16[256,1024]{1,0:T(8,128)(2,1)S(1)} collective-permute-done((bf16[256,1024]{1,0:T(8,128)(2,1)S(1)}, bf16[256,1024]{1,0:T(8,128)(2,1)S(1)}, u32[]{:S(2)}, u32[]{:S(2)}) %collective-permute-start.40) | collective-permute-done | bytes 524320 | tf_op jit(solution)/shard_map/ppermute | solution.py:52
  212.2 26.5 %collective-permute-done.41 = bf16[256,1024]{1,0:T(8,128)(2,1)S(1)} collective-permute-done((bf16[256,1024]{1,0:T(8,128)(2,1)S(1)}, bf16[256,1024]{1,0:T(8,128)(2,1)S(1)}, u32[]{:S(2)}, u32[]{:S(2)}) %collective-permute-start.41) | collective-permute-done | bytes 524320 | tf_op jit(solution)/shard_map/ppermute | solution.py:52
  239.1 9.9 %collective-permute-done.42 = bf16[256,1024]{1,0:T(8,128)(2,1)S(1)} collective-permute-done((bf16[256,1024]{1,0:T(8,128)(2,1)S(1)}, bf16[256,1024]{1,0:T(8,128)(2,1)S(1)}, u32[]{:S(2)}, u32[]{:S(2)}) %collective-permute-start.42) | collective-permute-done | bytes 524320 | tf_op jit(solution)/shard_map/ppermute | solution.py:52
  254.1 1.7 collective-permute-start.37
  257.0 2.6 finish_rows.1
  259.6 28.9 %collective-permute-done.37.s2 = bf16[144,1024]{1,0:T(8,128)(2,1)S(1)} collective-permute-done((bf16[144,1024]{1,0:T(8,128)(2,1)S(1)}, bf16[144,1024]{1,0:T(8,128)(2,1)S(1)}, u32[]{:S(2)}, u32[]{:S(2)}) %collective-permute-start.37) | collective-permute-done | bytes 294944 | tf_op jit(solution)/shard_map/ppermute | solution.py:52
  288.5 1.9 finish_attention.1
  290.5 3.0 %finish_feed.1 = (f32[128,4096]{1,0:T(8,128)}, f32[512,1024]{1,0:T(8,128)}) custom-call(s32[2]{0:T(128)S(1)} %pad_add_fusion.1.where, bf16[256,1024]{1,0:T(8,128)(2,1)S(1)} %fusion.2.s0, bf16[256,1024]{1,0:T(8,128)(2,1)S(1)} %collective-permute-done.43.s1, bf16[256,1024]{1,0:T(8,128)(2,1)S(1)} %collective-permute-done.44.s2, ...), custom_call_target="tpu_custom_call" | custom-call | bytes 6291456 | tf_op jit(solution)/shard_map/finish_feed/pallas_call | solution.py:404
  (129 shorter events, 41.2 us)
Async XLA Ops:
  9.4 12.1 %collective-permute-start.4 = (bf16[144,1024]{1,0:T(8,128)(2,1)S(1)}, bf16[144,1024]{1,0:T(8,128)(2,1)S(1)}, u32[]{:S(2)}, u32[]{:S(2)}) collective-permute-start(bf16[144,1024]{1,0:T(8,128)(2,1)S(1)} %get-tuple-element.86.refs_0_), channel_id=1, source_target_pairs={{0,8},{4,12},{8,0},{12,4},{16,24},{20,28},{24,16},{28,20},{1,9},{5... | collective-permute-start | bytes 884744 | tf_op jit(solution)/shard_map/ppermute | solution.py:52
  9.4 23.1 %collective-permute-start.6 = (bf16[144,1024]{1,0:T(8,128)(2,1)S(1)}, bf16[144,1024]{1,0:T(8,128)(2,1)S(1)}, u32[]{:S(2)}, u32[]{:S(2)}) collective-permute-start(bf16[144,1024]{1,0:T(8,128)(2,1)S(1)} %get-tuple-element.86.refs_0_), channel_id=1, source_target_pairs={{0,16},{4,20},{8,24},{12,28},{16,0},{20,4},{24,8},{28,12},{1,17},{... | collective-permute-start | bytes 884744 | tf_op jit(solution)/shard_map/ppermute | solution.py:52
  12.4 25.9 %collective-permute-start.8 = (bf16[144,1024]{1,0:T(8,128)(2,1)S(1)}, bf16[144,1024]{1,0:T(8,128)(2,1)S(1)}, u32[]{:S(2)}, u32[]{:S(2)}) collective-permute-start(bf16[144,1024]{1,0:T(8,128)(2,1)S(1)} %get-tuple-element.86.refs_0_), channel_id=1, source_target_pairs={{0,24},{4,28},{8,16},{12,20},{16,8},{20,12},{24,0},{28,4},{1,25},{... | collective-permute-start | bytes 884744 | tf_op jit(solution)/shard_map/ppermute | solution.py:52
  12.8 27.9 %collective-permute-start.3 = (bf16[144,1024]{1,0:T(8,128)(2,1)S(1)}, bf16[144,1024]{1,0:T(8,128)(2,1)S(1)}, u32[]{:S(2)}, u32[]{:S(2)}) collective-permute-start(bf16[144,1024]{1,0:T(8,128)(2,1)S(1)} %get-tuple-element.86.refs_0_), channel_id=1, source_target_pairs={{0,4},{4,0},{8,12},{12,8},{16,20},{20,16},{24,28},{28,24},{1,5},{5... | collective-permute-start | bytes 884744 | tf_op jit(solution)/shard_map/ppermute | solution.py:52
  21.5 20.0 %collective-permute-start.5 = (bf16[144,1024]{1,0:T(8,128)(2,1)S(1)}, bf16[144,1024]{1,0:T(8,128)(2,1)S(1)}, u32[]{:S(2)}, u32[]{:S(2)}) collective-permute-start(bf16[144,1024]{1,0:T(8,128)(2,1)S(1)} %collective-permute-done.4.refs_2_), channel_id=1, source_target_pairs={{0,4},{4,0},{8,12},{12,8},{16,20},{20,16},{24,28},{28,24},{1,5},{5... | collective-permute-start | bytes 884744 | tf_op jit(solution)/shard_map/ppermute | solution.py:52
  21.5 26.9 %collective-permute-start = (bf16[256,1024]{1,0:T(8,128)(2,1)S(1)}, bf16[256,1024]{1,0:T(8,128)(2,1)S(1)}, u32[]{:S(2)}, u32[]{:S(2)}) collective-permute-start(bf16[256,1024]{1,0:T(8,128)(2,1)S(1)} %get-tuple-element.85.t0.refs_9_.refs_5_), channel_id=1, source_target_pairs={{0,1},{1,0},{2,3},{3,2},{4,5},{5,4},{6,7},{7,6},{8,9},{9,8},{10,11... | collective-permute-start | bytes 1572872 | tf_op jit(solution)/shard_map/ppermute | solution.py:52
  32.5 20.4 %collective-permute-start.1 = (bf16[256,1024]{1,0:T(8,128)(2,1)S(1)}, bf16[256,1024]{1,0:T(8,128)(2,1)S(1)}, u32[]{:S(2)}, u32[]{:S(2)}) collective-permute-start(bf16[256,1024]{1,0:T(8,128)(2,1)S(1)} %get-tuple-element.85.t0.refs_9_.refs_5_), channel_id=1, source_target_pairs={{0,2},{1,3},{2,0},{3,1},{4,6},{5,7},{6,4},{7,5},{8,10},{9,11},{10,... | collective-permute-start | bytes 1572872 | tf_op jit(solution)/shard_map/ppermute | solution.py:52
  38.3 14.6 %collective-permute-start.2 = (bf16[256,1024]{1,0:T(8,128)(2,1)S(1)}, bf16[256,1024]{1,0:T(8,128)(2,1)S(1)}, u32[]{:S(2)}, u32[]{:S(2)}) collective-permute-start(bf16[256,1024]{1,0:T(8,128)(2,1)S(1)} %get-tuple-element.85.t0.refs_9_.refs_5_), channel_id=1, source_target_pairs={{0,3},{1,2},{2,1},{3,0},{4,7},{5,6},{6,5},{7,4},{8,11},{9,10},{10,... | collective-permute-start | bytes 1572872 | tf_op jit(solution)/shard_map/ppermute | solution.py:52
  41.5 1.7 collective-permute-start.7
  42.2 1.8 collective-permute-start.9
  48.3 70.4 %copy-start.8 = (bf16[1024,256]{1,0:T(8,128)(2,1)}, bf16[1024,256]{1,0:T(8,128)(2,1)S(1)}, u32[]{:S(2)}) copy-start(bf16[1024,256]{1,0:T(8,128)(2,1)S(1)} %get-tuple-element.92.w0) | copy-start | bytes 1572868
  48.3 64.3 %copy-start.2 = (bf16[256,1024]{1,0:T(8,128)(2,1)}, bf16[256,1024]{1,0:T(8,128)(2,1)S(1)}, u32[]{:S(2)}) copy-start(bf16[256,1024]{1,0:T(8,128)(2,1)S(1)} %collective-permute-done.t1.refs_10_.refs_6_) | copy-start | bytes 1572868
  59.6 9.2 %collective-permute-start.10 = (bf16[512,256]{1,0:T(8,128)(2,1)S(1)}, bf16[512,256]{1,0:T(8,128)(2,1)S(1)}, u32[]{:S(2)}, u32[]{:S(2)}) collective-permute-start(bf16[512,256]{1,0:T(8,128)(2,1)S(1)} %get-tuple-element.91.a0), channel_id=1, source_target_pairs={{0,1},{1,0},{2,3},{3,2},{4,5},{5,4},{6,7},{7,6},{8,9},{9,8},{10,11... | collective-permute-start | bytes 786440 | tf_op jit(solution)/shard_map/ppermute | solution.py:52
  61.1 11.5 %collective-permute-start.11 = (bf16[512,256]{1,0:T(8,128)(2,1)S(1)}, bf16[512,256]{1,0:T(8,128)(2,1)S(1)}, u32[]{:S(2)}, u32[]{:S(2)}) collective-permute-start(bf16[512,256]{1,0:T(8,128)(2,1)S(1)} %get-tuple-element.91.a0), channel_id=1, source_target_pairs={{0,2},{1,3},{2,0},{3,1},{4,6},{5,7},{6,4},{7,5},{8,10},{9,11},{10,... | collective-permute-start | bytes 786440 | tf_op jit(solution)/shard_map/ppermute | solution.py:52
  62.6 12.8 %collective-permute-start.12 = (bf16[512,256]{1,0:T(8,128)(2,1)S(1)}, bf16[512,256]{1,0:T(8,128)(2,1)S(1)}, u32[]{:S(2)}, u32[]{:S(2)}) collective-permute-start(bf16[512,256]{1,0:T(8,128)(2,1)S(1)} %get-tuple-element.91.a0), channel_id=1, source_target_pairs={{0,3},{1,2},{2,1},{3,0},{4,7},{5,6},{6,5},{7,4},{8,11},{9,10},{10,... | collective-permute-start | bytes 786440 | tf_op jit(solution)/shard_map/ppermute | solution.py:52
  63.1 18.9 %collective-permute-start.13 = (bf16[1024,256]{1,0:T(8,128)(2,1)S(1)}, bf16[1024,256]{1,0:T(8,128)(2,1)S(1)}, u32[]{:S(2)}, u32[]{:S(2)}) collective-permute-start(bf16[1024,256]{1,0:T(8,128)(2,1)S(1)} %get-tuple-element.92.w0), channel_id=1, source_target_pairs={{0,1},{1,0},{2,3},{3,2},{4,5},{5,4},{6,7},{7,6},{8,9},{9,8},{10,11... | collective-permute-start | bytes 1572872 | tf_op jit(solution)/shard_map/ppermute | solution.py:52
  64.6 29.0 %collective-permute-start.14 = (bf16[1024,256]{1,0:T(8,128)(2,1)S(1)}, bf16[1024,256]{1,0:T(8,128)(2,1)S(1)}, u32[]{:S(2)}, u32[]{:S(2)}) collective-permute-start(bf16[1024,256]{1,0:T(8,128)(2,1)S(1)} %get-tuple-element.92.w0), channel_id=1, source_target_pairs={{0,2},{1,3},{2,0},{3,1},{4,6},{5,7},{6,4},{7,5},{8,10},{9,11},{10,... | collective-permute-start | bytes 1572872 | tf_op jit(solution)/shard_map/ppermute | solution.py:52
  68.9 24.7 %collective-permute-start.17 = (bf16[256,1024]{1,0:T(8,128)(2,1)S(1)}, bf16[256,1024]{1,0:T(8,128)(2,1)S(1)}, u32[]{:S(2)}, u32[]{:S(2)}) collective-permute-start(bf16[256,1024]{1,0:T(8,128)(2,1)S(1)} %copy-done.26), channel_id=1, source_target_pairs={{0,8},{4,12},{8,0},{12,4},{16,24},{20,28},{24,16},{28,20},{1,9},{5... | collective-permute-start | bytes 1572872 | tf_op jit(solution)/shard_map/ppermute | solution.py:52
  72.6 31.5 %collective-permute-start.19 = (bf16[256,1024]{1,0:T(8,128)(2,1)S(1)}, bf16[256,1024]{1,0:T(8,128)(2,1)S(1)}, u32[]{:S(2)}, u32[]{:S(2)}) collective-permute-start(bf16[256,1024]{1,0:T(8,128)(2,1)S(1)} %copy-done.26), channel_id=1, source_target_pairs={{0,16},{4,20},{8,24},{12,28},{16,0},{20,4},{24,8},{28,12},{1,17},{... | collective-permute-start | bytes 1572872 | tf_op jit(solution)/shard_map/ppermute | solution.py:52
  75.4 37.1 %collective-permute-start.21 = (bf16[256,1024]{1,0:T(8,128)(2,1)S(1)}, bf16[256,1024]{1,0:T(8,128)(2,1)S(1)}, u32[]{:S(2)}, u32[]{:S(2)}) collective-permute-start(bf16[256,1024]{1,0:T(8,128)(2,1)S(1)} %copy-done.26), channel_id=1, source_target_pairs={{0,24},{4,28},{8,16},{12,20},{16,8},{20,12},{24,0},{28,4},{1,25},{... | collective-permute-start | bytes 1572872 | tf_op jit(solution)/shard_map/ppermute | solution.py:52
  82.0 30.6 %collective-permute-start.15 = (bf16[1024,256]{1,0:T(8,128)(2,1)S(1)}, bf16[1024,256]{1,0:T(8,128)(2,1)S(1)}, u32[]{:S(2)}, u32[]{:S(2)}) collective-permute-start(bf16[1024,256]{1,0:T(8,128)(2,1)S(1)} %get-tuple-element.92.w0), channel_id=1, source_target_pairs={{0,3},{1,2},{2,1},{3,0},{4,7},{5,6},{6,5},{7,4},{8,11},{9,10},{10,... | collective-permute-start | bytes 1572872 | tf_op jit(solution)/shard_map/ppermute | solution.py:52
  93.6 25.1 %collective-permute-start.16 = (bf16[256,1024]{1,0:T(8,128)(2,1)S(1)}, bf16[256,1024]{1,0:T(8,128)(2,1)S(1)}, u32[]{:S(2)}, u32[]{:S(2)}) collective-permute-start(bf16[256,1024]{1,0:T(8,128)(2,1)S(1)} %copy-done.26), channel_id=1, source_target_pairs={{0,4},{4,0},{8,12},{12,8},{16,20},{20,16},{24,28},{28,24},{1,5},{5... | collective-permute-start | bytes 1572872 | tf_op jit(solution)/shard_map/ppermute | solution.py:52
  93.6 25.1 %collective-permute-start.18 = (bf16[256,1024]{1,0:T(8,128)(2,1)S(1)}, bf16[256,1024]{1,0:T(8,128)(2,1)S(1)}, u32[]{:S(2)}, u32[]{:S(2)}) collective-permute-start(bf16[256,1024]{1,0:T(8,128)(2,1)S(1)} %collective-permute-done.17.refs_3_), channel_id=1, source_target_pairs={{0,4},{4,0},{8,12},{12,8},{16,20},{20,16},{24,28},{28,24},{1,5},{5... | collective-permute-start | bytes 1572872 | tf_op jit(solution)/shard_map/ppermute | solution.py:52
  104.1 14.6 %collective-permute-start.20 = (bf16[256,1024]{1,0:T(8,128)(2,1)S(1)}, bf16[256,1024]{1,0:T(8,128)(2,1)S(1)}, u32[]{:S(2)}, u32[]{:S(2)}) collective-permute-start(bf16[256,1024]{1,0:T(8,128)(2,1)S(1)} %collective-permute-done.19.refs_5_), channel_id=1, source_target_pairs={{0,4},{4,0},{8,12},{12,8},{16,20},{20,16},{24,28},{28,24},{1,5},{5... | collective-permute-start | bytes 1572872 | tf_op jit(solution)/shard_map/ppermute | solution.py:52
  112.6 6.2 %collective-permute-start.22 = (bf16[256,1024]{1,0:T(8,128)(2,1)S(1)}, bf16[256,1024]{1,0:T(8,128)(2,1)S(1)}, u32[]{:S(2)}, u32[]{:S(2)}) collective-permute-start(bf16[256,1024]{1,0:T(8,128)(2,1)S(1)} %collective-permute-done.21.refs_7_), channel_id=1, source_target_pairs={{0,4},{4,0},{8,12},{12,8},{16,20},{20,16},{24,28},{28,24},{1,5},{5... | collective-permute-start | bytes 1572872 | tf_op jit(solution)/shard_map/ppermute | solution.py:52
  128.2 13.8 %collective-permute-start.23 = (bf16[128,1024]{1,0:T(8,128)(2,1)S(1)}, bf16[128,1024]{1,0:T(8,128)(2,1)S(1)}, u32[]{:S(2)}, u32[]{:S(2)}) collective-permute-start(bf16[128,1024]{1,0:T(8,128)(2,1)S(1)} %get-tuple-element.103), channel_id=1, source_target_pairs={{0,1},{1,0},{2,3},{3,2},{4,5},{5,4},{6,7},{7,6},{8,9},{9,8},{10,11... | collective-permute-start | bytes 786440 | tf_op jit(solution)/shard_map/ppermute | solution.py:52
  128.6 13.5 %collective-permute-start.24 = (bf16[128,1024]{1,0:T(8,128)(2,1)S(1)}, bf16[128,1024]{1,0:T(8,128)(2,1)S(1)}, u32[]{:S(2)}, u32[]{:S(2)}) collective-permute-start(bf16[128,1024]{1,0:T(8,128)(2,1)S(1)} %get-tuple-element.104), channel_id=1, source_target_pairs={{0,2},{1,3},{2,0},{3,1},{4,6},{5,7},{6,4},{7,5},{8,10},{9,11},{10,... | collective-permute-start | bytes 786440 | tf_op jit(solution)/shard_map/ppermute | solution.py:52
  130.3 13.6 %collective-permute-start.25 = (bf16[128,1024]{1,0:T(8,128)(2,1)S(1)}, bf16[128,1024]{1,0:T(8,128)(2,1)S(1)}, u32[]{:S(2)}, u32[]{:S(2)}) collective-permute-start(bf16[128,1024]{1,0:T(8,128)(2,1)S(1)} %get-tuple-element.105), channel_id=1, source_target_pairs={{0,3},{1,2},{2,1},{3,0},{4,7},{5,6},{6,5},{7,4},{8,11},{9,10},{10,... | collective-permute-start | bytes 786440 | tf_op jit(solution)/shard_map/ppermute | solution.py:52
  147.1 31.5 %collective-permute-start.39 = (bf16[4,256,1024]{2,1,0:T(8,128)(2,1)}, bf16[4,256,1024]{2,1,0:T(8,128)(2,1)}, u32[]{:S(2)}, u32[]{:S(2)}) collective-permute-start(bf16[4,256,1024]{2,1,0:T(8,128)(2,1)} %get-tuple-element.147), channel_id=1, source_target_pairs={{0,4},{4,0},{8,12},{12,8},{16,20},{20,16},{24,28},{28,24},{1,5},{5... | collective-permute-start | bytes 6291464 | tf_op jit(solution)/shard_map/ppermute | solution.py:52
  147.2 6.4 %collective-permute-start.26 = (bf16[256,256]{1,0:T(8,128)(2,1)S(1)}, bf16[256,256]{1,0:T(8,128)(2,1)S(1)}, u32[]{:S(2)}, u32[]{:S(2)}) collective-permute-start(bf16[256,256]{1,0:T(8,128)(2,1)S(1)} %get-tuple-element.113), channel_id=1, source_target_pairs={{0,1},{1,0},{2,3},{3,2},{4,5},{5,4},{6,7},{7,6},{8,9},{9,8},{10,11... | collective-permute-start | bytes 393224 | tf_op jit(solution)/shard_map/ppermute | solution.py:52
  147.8 8.4 %collective-permute-start.27 = (bf16[256,256]{1,0:T(8,128)(2,1)S(1)}, bf16[256,256]{1,0:T(8,128)(2,1)S(1)}, u32[]{:S(2)}, u32[]{:S(2)}) collective-permute-start(bf16[256,256]{1,0:T(8,128)(2,1)S(1)} %get-tuple-element.114), channel_id=1, source_target_pairs={{0,2},{1,3},{2,0},{3,1},{4,6},{5,7},{6,4},{7,5},{8,10},{9,11},{10,... | collective-permute-start | bytes 393224 | tf_op jit(solution)/shard_map/ppermute | solution.py:52
  149.6 6.6 %collective-permute-start.28 = (bf16[256,256]{1,0:T(8,128)(2,1)S(1)}, bf16[256,256]{1,0:T(8,128)(2,1)S(1)}, u32[]{:S(2)}, u32[]{:S(2)}) collective-permute-start(bf16[256,256]{1,0:T(8,128)(2,1)S(1)} %get-tuple-element.115), channel_id=1, source_target_pairs={{0,3},{1,2},{2,1},{3,0},{4,7},{5,6},{6,5},{7,4},{8,11},{9,10},{10,... | collective-permute-start | bytes 393224 | tf_op jit(solution)/shard_map/ppermute | solution.py:52
  170.2 3.1 %collective-permute-start.32 = (bf16[4,144,1024]{2,1,0:T(8,128)(2,1)}, bf16[4,144,1024]{2,1,0:T(8,128)(2,1)S(1)}, u32[]{:S(2)}, u32[]{:S(2)}) collective-permute-start(bf16[4,144,1024]{2,1,0:T(8,128)(2,1)} %get-tuple-element.135), channel_id=1, source_target_pairs={{0,4},{4,0},{8,12},{12,8},{16,20},{20,16},{24,28},{28,24},{1,5},{5... | collective-permute-start | bytes 3538952 | tf_op jit(solution)/shard_map/ppermute | solution.py:52
  174.7 13.5 %collective-permute-start.33 = (bf16[144,1024]{1,0:T(8,128)(2,1)S(1)}, bf16[144,1024]{1,0:T(8,128)(2,1)S(1)}, u32[]{:S(2)}, u32[]{:S(2)}) collective-permute-start(bf16[144,1024]{1,0:T(8,128)(2,1)S(1)} %get-tuple-element.156), channel_id=1, source_target_pairs={{0,8},{4,12},{8,0},{12,4},{16,24},{20,28},{24,16},{28,20},{1,9},{5... | collective-permute-start | bytes 884744 | tf_op jit(solution)/shard_map/ppermute | solution.py:52
  174.8 23.9 %collective-permute-start.34 = (bf16[144,1024]{1,0:T(8,128)(2,1)S(1)}, bf16[144,1024]{1,0:T(8,128)(2,1)S(1)}, u32[]{:S(2)}, u32[]{:S(2)}) collective-permute-start(bf16[144,1024]{1,0:T(8,128)(2,1)S(1)} %get-tuple-element.158), channel_id=1, source_target_pairs={{0,16},{4,20},{8,24},{12,28},{16,0},{20,4},{24,8},{28,12},{1,17},{... | collective-permute-start | bytes 884744 | tf_op jit(solution)/shard_map/ppermute | solution.py:52
  178.6 26.5 %collective-permute-start.35 = (bf16[144,1024]{1,0:T(8,128)(2,1)S(1)}, bf16[144,1024]{1,0:T(8,128)(2,1)S(1)}, u32[]{:S(2)}, u32[]{:S(2)}) collective-permute-start(bf16[144,1024]{1,0:T(8,128)(2,1)S(1)} %get-tuple-element.157), channel_id=1, source_target_pairs={{0,24},{4,28},{8,16},{12,20},{16,8},{20,12},{24,0},{28,4},{1,25},{... | collective-permute-start | bytes 884744 | tf_op jit(solution)/shard_map/ppermute | solution.py:52
  180.6 30.5 %collective-permute-start.40 = (bf16[256,1024]{1,0:T(8,128)(2,1)S(1)}, bf16[256,1024]{1,0:T(8,128)(2,1)S(1)}, u32[]{:S(2)}, u32[]{:S(2)}) collective-permute-start(bf16[256,1024]{1,0:T(8,128)(2,1)S(1)} %get-tuple-element.153), channel_id=1, source_target_pairs={{0,8},{4,12},{8,0},{12,4},{16,24},{20,28},{24,16},{28,20},{1,9},{5... | collective-permute-start | bytes 1572872 | tf_op jit(solution)/shard_map/ppermute | solution.py:52
  182.1 56.6 %collective-permute-start.41 = (bf16[256,1024]{1,0:T(8,128)(2,1)S(1)}, bf16[256,1024]{1,0:T(8,128)(2,1)S(1)}, u32[]{:S(2)}, u32[]{:S(2)}) collective-permute-start(bf16[256,1024]{1,0:T(8,128)(2,1)S(1)} %get-tuple-element.155), channel_id=1, source_target_pairs={{0,16},{4,20},{8,24},{12,28},{16,0},{20,4},{24,8},{28,12},{1,17},{... | collective-permute-start | bytes 1572872 | tf_op jit(solution)/shard_map/ppermute | solution.py:52
  188.2 60.8 %collective-permute-start.42 = (bf16[256,1024]{1,0:T(8,128)(2,1)S(1)}, bf16[256,1024]{1,0:T(8,128)(2,1)S(1)}, u32[]{:S(2)}, u32[]{:S(2)}) collective-permute-start(bf16[256,1024]{1,0:T(8,128)(2,1)S(1)} %get-tuple-element.154), channel_id=1, source_target_pairs={{0,24},{4,28},{8,16},{12,20},{16,8},{20,12},{24,0},{28,4},{1,25},{... | collective-permute-start | bytes 1572872 | tf_op jit(solution)/shard_map/ppermute | solution.py:52
  198.7 53.4 %collective-permute-start.29 = (bf16[256,1024]{1,0:T(8,128)(2,1)S(1)}, bf16[256,1024]{1,0:T(8,128)(2,1)S(1)}, u32[]{:S(2)}, u32[]{:S(2)}) collective-permute-start(bf16[256,1024]{1,0:T(8,128)(2,1)S(1)} %get-tuple-element.120), channel_id=1, source_target_pairs={{0,1},{1,0},{2,3},{3,2},{4,5},{5,4},{6,7},{7,6},{8,9},{9,8},{10,11... | collective-permute-start | bytes 1572872 | tf_op jit(solution)/shard_map/ppermute | solution.py:52
  205.1 47.6 %collective-permute-start.30 = (bf16[256,1024]{1,0:T(8,128)(2,1)S(1)}, bf16[256,1024]{1,0:T(8,128)(2,1)S(1)}, u32[]{:S(2)}, u32[]{:S(2)}) collective-permute-start(bf16[256,1024]{1,0:T(8,128)(2,1)S(1)} %get-tuple-element.121), channel_id=1, source_target_pairs={{0,2},{1,3},{2,0},{3,1},{4,6},{5,7},{6,4},{7,5},{8,10},{9,11},{10,... | collective-permute-start | bytes 1572872 | tf_op jit(solution)/shard_map/ppermute | solution.py:52
  211.1 43.0 %collective-permute-start.31 = (bf16[256,1024]{1,0:T(8,128)(2,1)S(1)}, bf16[256,1024]{1,0:T(8,128)(2,1)S(1)}, u32[]{:S(2)}, u32[]{:S(2)}) collective-permute-start(bf16[256,1024]{1,0:T(8,128)(2,1)S(1)} %get-tuple-element.122), channel_id=1, source_target_pairs={{0,3},{1,2},{2,1},{3,0},{4,7},{5,6},{6,5},{7,4},{8,11},{9,10},{10,... | collective-permute-start | bytes 1572872 | tf_op jit(solution)/shard_map/ppermute | solution.py:52
  238.7 17.1 %collective-permute-start.36 = (bf16[144,1024]{1,0:T(8,128)(2,1)S(1)}, bf16[144,1024]{1,0:T(8,128)(2,1)S(1)}, u32[]{:S(2)}, u32[]{:S(2)}) collective-permute-start(bf16[144,1024]{1,0:T(8,128)(2,1)S(1)} %fusion.5.s0), channel_id=1, source_target_pairs={{0,1},{1,0},{2,3},{3,2},{4,5},{5,4},{6,7},{7,6},{8,9},{9,8},{10,11... | collective-permute-start | bytes 884744 | tf_op jit(solution)/shard_map/ppermute | solution.py:52
  250.6 39.9 %collective-permute-start.43 = (bf16[256,1024]{1,0:T(8,128)(2,1)S(1)}, bf16[256,1024]{1,0:T(8,128)(2,1)S(1)}, u32[]{:S(2)}, u32[]{:S(2)}) collective-permute-start(bf16[256,1024]{1,0:T(8,128)(2,1)S(1)} %fusion.2.s0), channel_id=1, source_target_pairs={{0,1},{1,0},{2,3},{3,2},{4,5},{5,4},{6,7},{7,6},{8,9},{9,8},{10,11... | collective-permute-start | bytes 1572872 | tf_op jit(solution)/shard_map/ppermute | solution.py:52
  252.1 38.4 %collective-permute-start.44 = (bf16[256,1024]{1,0:T(8,128)(2,1)S(1)}, bf16[256,1024]{1,0:T(8,128)(2,1)S(1)}, u32[]{:S(2)}, u32[]{:S(2)}) collective-permute-start(bf16[256,1024]{1,0:T(8,128)(2,1)S(1)} %fusion.2.s0), channel_id=1, source_target_pairs={{0,2},{1,3},{2,0},{3,1},{4,6},{5,7},{6,4},{7,5},{8,10},{9,11},{10,... | collective-permute-start | bytes 1572872 | tf_op jit(solution)/shard_map/ppermute | solution.py:52
  252.7 37.8 %collective-permute-start.45 = (bf16[256,1024]{1,0:T(8,128)(2,1)S(1)}, bf16[256,1024]{1,0:T(8,128)(2,1)S(1)}, u32[]{:S(2)}, u32[]{:S(2)}) collective-permute-start(bf16[256,1024]{1,0:T(8,128)(2,1)S(1)} %fusion.2.s0), channel_id=1, source_target_pairs={{0,3},{1,2},{2,1},{3,0},{4,7},{5,6},{6,5},{7,4},{8,11},{9,10},{10,... | collective-permute-start | bytes 1572872 | tf_op jit(solution)/shard_map/ppermute | solution.py:52
  254.1 34.4 %collective-permute-start.37 = (bf16[144,1024]{1,0:T(8,128)(2,1)S(1)}, bf16[144,1024]{1,0:T(8,128)(2,1)S(1)}, u32[]{:S(2)}, u32[]{:S(2)}) collective-permute-start(bf16[144,1024]{1,0:T(8,128)(2,1)S(1)} %fusion.5.s0), channel_id=1, source_target_pairs={{0,2},{1,3},{2,0},{3,1},{4,6},{5,7},{6,4},{7,5},{8,10},{9,11},{10,... | collective-permute-start | bytes 884744 | tf_op jit(solution)/shard_map/ppermute | solution.py:52
  255.9 32.7 %collective-permute-start.38 = (bf16[144,1024]{1,0:T(8,128)(2,1)S(1)}, bf16[144,1024]{1,0:T(8,128)(2,1)S(1)}, u32[]{:S(2)}, u32[]{:S(2)}) collective-permute-start(bf16[144,1024]{1,0:T(8,128)(2,1)S(1)} %fusion.5.s0), channel_id=1, source_target_pairs={{0,3},{1,2},{2,1},{3,0},{4,7},{5,6},{6,5},{7,4},{8,11},{9,10},{10,... | collective-permute-start | bytes 884744 | tf_op jit(solution)/shard_map/ppermute | solution.py:52
  (31 other events, 403.4 us)

commit v3 on v2

--- a/solution.py
+++ b/solution.py
@@ -396,19 +396,16 @@
     return jax.ShapeDtypeStruct(dims, kind)
 
 
-def call(kernel, where, ins, outs, flops=0, name=None, scratch=(), in_hbm=(), out_hbm=False):
-    moved = sum(x.size * x.dtype.itemsize for x in ins) + sum(
-        math.prod(o.shape) * o.dtype.itemsize for o in outs
-    )
-    in_specs = [spec(pl.ANY) if i in in_hbm else spec() for i in range(len(ins))]
+def call(kernel, where, ins, outs, flops=0, name=None, scratch=(), in_hbm=False, limit=50):
+    in_specs = [spec(pltpu.HBM) if in_hbm else spec() for _ in ins]
     return pl.pallas_call(
         kernel,
         out_shape=outs,
         in_specs=[spec(pltpu.SMEM)] + in_specs,
-        out_specs=[spec(pl.ANY) if out_hbm else spec() for _ in outs],
+        out_specs=[spec() for _ in outs],
         scratch_shapes=list(scratch),
-        compiler_params=pltpu.CompilerParams(vmem_limit_bytes=50 * 1024 * 1024),
-        cost_estimate=pl.CostEstimate(flops=flops, bytes_accessed=moved, transcendentals=0),
+        compiler_params=pltpu.CompilerParams(vmem_limit_bytes=limit * 1024 * 1024),
+        cost_estimate=pl.CostEstimate(flops=0, bytes_accessed=0, transcendentals=0),
         name=name,
     )(where, *ins)
 
@@ -417,36 +414,63 @@
     return pl.ds(pl.multiple_of(index * size, size), size)
 
 
-def prepare(where, w_in, w_out, w_up, w_down, tokens, grad, vec, first, second, rows, sems):
-    s = where[1]
-    shard, parts = w_in.shape[0], first.shape[1]
-    cols, out_cols = w_in.shape[1] // 4, w_out.shape[1] // 4
-    lane, wide = 128, w_up.shape[1] // 8
-    pairs = [
-        (w_in.at[:, at(s, cols)], first.at[0:shard, 0:cols]),
-        (w_out.at[:, at(s, out_cols)], first.at[0:shard, cols:parts]),
-        (vec, first.at[shard : shard + 16]),
-        (tokens, rows.at[0:shard]),
-        (grad, rows.at[shard : 2 * shard]),
-        (w_down.at[at(s, lane)], second.at[shard : 2 * shard]),
-    ]
-    for i in range(8):
-        lanes = pl.ds(pl.multiple_of(i * wide + s * lane, lane), lane)
-        pairs.append((w_up.at[:, lanes], second.at[0:shard, i * lane : (i + 1) * lane]))
+def run_copies(pairs, sems):
     copies = [pltpu.make_async_copy(a, b, sems.at[i]) for i, (a, b) in enumerate(pairs)]
     for copy in copies:
         copy.start()
-    for copy in copies:
+    return copies
+
+
+def prepare_first(where, *refs):
+    w_in, w_out, tokens, grad, vectors = refs[0], refs[1], refs[2], refs[3], refs[4:15]
+    first, rows, held, (pack, sems) = refs[15], refs[16], refs[17:28], refs[28:]
+    s = where[1]
+    pairs = list(zip(vectors, held)) + [
+        (pair[0], pair[1])
+        for m in range(4)
+        for pair in (
+            (w_in.at[:, at(s, 768)], first.at[m, 0:128, 0:768]),
+            (w_out.at[:, at(s, 256)], first.at[m, 0:128, 768:1024]),
+        )
+    ]
+    pairs += [(tokens, rows.at[0:128]), (grad, rows.at[128:256])]
+    copies = run_copies(pairs, sems)
+    for copy in copies[:11]:
         copy.wait()
-
-
-def place_first(where, *refs):
-    blocks, (w_in, w_out, vecs) = refs[:8], refs[8:]
-    for j in range(8):
-        n = where[0] ^ j
-        w_in[at(n, 128)] = blocks[j][0:128, 0:768]
-        w_out[at(n, 128)] = blocks[j][0:128, 768:1024]
-        vecs[:, at(n, 128)] = blocks[j][128:144, 0:128].astype(f32)
+    pack[...] = jnp.zeros(pack.shape, f32)
+    for i in range(10):
+        pack[i : i + 1, 0:128] = held[i][...].astype(f32).reshape(1, 128)
+    for i in range(4):
+        pack[10 + i : 11 + i, 0:128] = (
+            held[10][i * 128 : (i + 1) * 128].astype(f32).reshape(1, 128)
+        )
+    for m in range(4):
+        first[m, 128:144] = pack[...].astype(bf16)
+    for copy in copies[11:]:
+        copy.wait()
+
+
+def prepare_second(where, w_up, w_down, second, sems):
+    s = where[1]
+    pairs = [(w_down.at[at(s, 128)], second.at[128:256])]
+    for i in range(8):
+        lanes = pl.ds(pl.multiple_of(i * 512 + s * 128, 128), 128)
+        pairs.append((w_up.at[:, lanes], second.at[0:128, i * 128 : (i + 1) * 128]))
+    for copy in run_copies(pairs, sems):
+        copy.wait()
+
+
+def owner(where, t, b):
+    return 2 * where[2 + t] + ((where[0] % 2) ^ b)
+
+
+def place_first(where, own, other, w_in, w_out, vecs):
+    for b, blocks in enumerate((own, other)):
+        for z in range(4):
+            n = 2 * z + ((where[0] % 2) ^ b)
+            w_in[at(n, 128)] = blocks[z, 0:128, 0:768]
+            w_out[at(n, 128)] = blocks[z, 0:128, 768:1024]
+            vecs[:, at(n, 128)] = blocks[z, 128:144, 0:128].astype(f32)
 
 
 def column_segments(where, seg):
@@ -480,16 +504,18 @@
         probs = (powers * (1.0 / totals)).astype(bf16)
         outs.append(product(probs, v).astype(bf16))
         logsum[:, h : h + 1] = highest + jnp.log(totals)
-    attended[...] = jnp.concatenate(outs, axis=1)
+    whole = jnp.concatenate(outs, axis=1)
+    for m in range(4):
+        attended[m] = whole
 
 
 def project(
-    where, a0, a1, a2, a3, w0, w1, w2, w3, t0, t1, t2, t3, vecs, full, hidden, own_middle, own_branch, branch
+    where, sent, w0, w1, w2, w3, t0, t1, t2, t3, vecs, full, hidden, own_middle, own_branch, branch
 ):
-    for k, ref in enumerate((a0, a1, a2, a3)):
-        cols = at(where[1] ^ k, 256)
+    for m in range(4):
         for j in range(4):
-            full[j * 128 : (j + 1) * 128, cols] = ref[(j ^ k) * 128 : ((j ^ k) + 1) * 128]
+            rows = at(where[1] ^ (j ^ m), 128)
+            full[j * 128 : (j + 1) * 128, m * 256 : (m + 1) * 256] = sent[m, rows]
     for k, ref in enumerate((w0, w1, w2, w3)):
         branch[:, at(where[1] ^ k, 256)] = product(full[...], ref[...])
     for r, ref in enumerate((t0, t1, t2, t3)):
@@ -507,7 +533,7 @@
     hidden, blocks, tokens, (vecs, seg_col) = refs[0], refs[1:9], refs[9:13], refs[13:15]
     w_down, act, grad_two, grad_before, sums, p0, p1, p2, p3, w_up = refs[15:]
     for j in range(8):
-        rows = at(where[0] ^ j, 128)
+        rows = at(owner(where, j // 2, j % 2), 128)
         w_up[rows] = blocks[j][0:128]
         w_down[rows] = blocks[j][128:256]
     valid = (column_segments(where, seg_col) >= 0).astype(f32)
@@ -529,36 +555,31 @@
         ref[...] = product_right(grad_before[k * 128 : (k + 1) * 128], w_up[...]).astype(bf16)
 
 
-def halves(where, mine, theirs, k, first_row, result):
-    rows = pl.ds(first_row, 128)
-
-    @pl.when(where[0] % 2 == 0)
-    def _():
-        mine[k, rows] = result[0:128]
-        theirs[k, rows] = result[128:256]
-
-    @pl.when(where[0] % 2 == 1)
-    def _():
-        mine[k, rows] = result[128:256]
-        theirs[k, rows] = result[0:128]
+def core_rows(where, z, own):
+    return at(2 * z + ((where[0] % 2) if own else 1 - (where[0] % 2)), 128)
+
+
+def feed_weights_sent(where, hidden, grad_before, act, grad_two, theirs):
+    for k in range(4):
+        cols = core_rows(where, k, False)
+        theirs[k, 0:128] = product_left(hidden[:, cols], grad_before[...]).astype(bf16)
+        theirs[k, 128:256] = product_left(act[:, cols], grad_two[...]).astype(bf16)
 
 
 def feed_weights(where, *refs):
-    hidden, grad_before, act, grad_two, w_down, t0, t1, t2, t3, vecs, seg_col = refs[:11]
-    mine, theirs, sums, o0, o1, o2, o3 = refs[11:]
+    hidden, grad_before, act, grad_two, w_down = refs[:5]
+    tokens, (vecs, seg_col, mine, sums, *two) = refs[5:9], refs[9:]
     for k in range(4):
-        cols = at((where[0] // 2) ^ k, 256)
-        up = product_left(hidden[:, cols], grad_before[...]).astype(bf16)
-        halves(where, mine, theirs, k, 0, up)
-        down = product_left(act[:, cols], grad_two[...]).astype(bf16)
-        halves(where, mine, theirs, k, 128, down)
+        cols = core_rows(where, k, True)
+        mine[k, 0:128] = product_left(hidden[:, cols], grad_before[...]).astype(bf16)
+        mine[k, 128:256] = product_left(act[:, cols], grad_two[...]).astype(bf16)
     valid = (column_segments(where, seg_col) >= 0).astype(f32)
     scale = jnp.zeros((1, 1024), f32)
-    for k, (ref, out) in enumerate(((t0, o0), (t1, o1), (t2, o2), (t3, o3))):
+    for k in range(4):
         rows = slice(k * 128, (k + 1) * 128)
         part = product(act[rows], w_down[...])
-        grad = ref[128:256].astype(f32) * valid[rows]
-        out[...] = part.astype(out.dtype)
+        grad = tokens[k][128:256].astype(f32) * valid[rows]
+        two[k][...] = part.astype(bf16)
         if k == 0:
             part = part + vecs[8:9]
         scale = scale + jnp.sum(grad * part, axis=0, keepdims=True)
@@ -567,13 +588,13 @@
 
 
 def middle_back(
-    where, p0, p1, p2, p3, own_middle, own_branch, t0, seg_col, vecs, w0, w1, w2, w3,
+    where, p0, p1, p2, p3, own_middle, own_branch, tokens, seg_col, vecs, w0, w1, w2, w3,
     grad_middle, sums, m0, m1, m2, m3, attended, one,
 ):
     total = p0[...] + p1[...].astype(f32) + p2[...].astype(f32) + p3[...].astype(f32)
     normed, spread = normalize(own_middle[...])
     valid = (seg_col[at(where[1], 128)] >= 0).astype(f32)
-    back = t0[128:256].astype(f32) * valid + normalize_back(total * vecs[6:7], normed, spread)
+    back = tokens[128:256].astype(f32) * valid + normalize_back(total * vecs[6:7], normed, spread)
     grad_middle[...] = back
     grad_one = (back * vecs[5:6]).astype(bf16)
     one[...] = grad_one
@@ -592,8 +613,8 @@
 
 
 def attention_back(
-    where, triple, logsum, m0, m1, m2, m3, seg_col, seg_row, w_in, t0, t1, t2, t3, o1, o2, o3,
-    grad_triple, sums, own, n1, n2, n3,
+    where, triple, logsum, m0, m1, m2, m3, seg_col, seg_row, w_in, t0, t1, t2, t3,
+    grad_triple, sums, *last,
 ):
     same = column_segments(where, seg_col) == row_segments(where, seg_row)
     grads = jnp.concatenate([m[0:128] for m in (m0, m1, m2, m3)], axis=0)
@@ -621,17 +642,12 @@
         )
     gain = jnp.zeros((1, 1024), f32)
     offset = jnp.zeros((1, 1024), f32)
-    sent = ((t0, own, None), (t1, n1, o1), (t2, n2, o2), (t3, n3, o3))
-    for k, (ref, out, other) in enumerate(sent):
+    for k, ref in enumerate((t0, t1, t2, t3)):
         part = product_right(grad_triple[k * 128 : (k + 1) * 128], w_in[...])
         normed, _ = normalize(ref[0:128].astype(f32))
         gain = gain + jnp.sum(part * normed, axis=0, keepdims=True)
         offset = offset + jnp.sum(part, axis=0, keepdims=True)
-        if k == 0:
-            out[...] = part
-        else:
-            out[0:128] = part.astype(bf16)
-            out[128:256] = other[...]
+        last[k][...] = part.astype(bf16)
     sums[0:1] = gain
     sums[1:2] = offset
 
@@ -649,33 +665,29 @@
     vecs[8:10] = two_sums[0:2]
     vecs[pl.ds(10 + where[1], 1)] = up_sums[...]
     blank = jnp.zeros((16, 896), bf16)
-    core = where[0] % 2
     for k in range(4):
-        pair = (where[0] // 2) ^ k
-        cols = at(pair, 256)
-        left = product_left(hidden[:, cols], grad_triple[...]).astype(bf16)
-        right = product_left(attended[:, cols], ones).astype(bf16)
-        halves(where, mine, theirs, k, 0, jnp.concatenate([left, right], axis=1))
-        for ref, half in ((mine, core), (theirs, 1 - core)):
-            block = vecs[:, at(2 * pair + half, 128)].astype(bf16)
-            ref[k, 128:144] = jnp.concatenate([block, blank], axis=1)
-
-
-def finish_rows(where, own, n1, n2, n3, own_two, own_middle, grad_middle, t0, vecs, out, grad):
-    total = own[...] + sum(n[0:128].astype(f32) for n in (n1, n2, n3))
-    two = own_two[...] + sum(n[128:256].astype(f32) for n in (n1, n2, n3)) + vecs[8:9]
+        for ref, own in ((mine, True), (theirs, False)):
+            cols = core_rows(where, where[2 + k], own)
+            ref[k, 0:128, 0:768] = product_left(hidden[:, cols], grad_triple[...]).astype(bf16)
+            ref[k, 0:128, 768:1024] = product_left(attended[:, cols], ones).astype(bf16)
+            ref[k, 128:144] = jnp.concatenate([vecs[:, cols].astype(bf16), blank], axis=1)
+
+
+def finish_rows(where, *refs):
+    ones, twos, (own_middle, grad_middle, tokens, vecs, out, grad) = refs[:4], refs[4:8], refs[8:]
+    total = sum(ref[...].astype(f32) for ref in ones)
+    two = sum(ref[...].astype(f32) for ref in twos) + vecs[8:9]
     out[...] = (own_middle[...] + vecs[9:10] * two).astype(bf16)
-    normed, spread = normalize(t0[0:128].astype(f32))
+    normed, spread = normalize(tokens[0:128].astype(f32))
     grad[...] = (grad_middle[...] + normalize_back(total * vecs[0:1], normed, spread)).astype(bf16)
 
 
-def finish_feed(where, s0, s1, s2, s3, up, down):
-    for k, ref in enumerate((s0, s1, s2, s3)):
-        m = where[1] ^ k
-        down[at(m, 128)] = ref[128:256].astype(f32)
+def finish_feed(where, got, up, down):
+    for m in range(4):
+        down[m * 128 : (m + 1) * 128] = got[m, 128:256].astype(f32)
         for n in range(8):
-            lanes = pl.ds(pl.multiple_of(n * 512 + m * 128, 128), 128)
-            up[:, lanes] = ref[0:128, n * 128 : (n + 1) * 128].astype(f32)
+            lanes = slice(n * 512 + m * 128, n * 512 + (m + 1) * 128)
+            up[:, lanes] = got[m, 0:128, n * 128 : (n + 1) * 128].astype(f32)
 
 
 def finish_attention(where, s0, s1, s2, s3, w_in, w_out, *refs):
@@ -691,21 +703,54 @@
     outs[10][...] = jnp.concatenate([total[i : i + 1] for i in range(10, 14)], axis=1)
 
 
-def gather_blocks(x):
-    out = []
-    for k in range(4):
-        block = swap(x, "fsdp", 2 * k) if k else x
-        out += [block, swap(block, "fsdp", 1)]
-    return out
-
-
-def scatter_blocks(mine, theirs):
-    other = swap(theirs, "fsdp", 1)
-    sums = [(mine[k].astype(f32) + other[k].astype(f32)).astype(bf16) for k in range(4)]
-    total = sums[0].astype(f32)
-    for k in range(1, 4):
-        total = total + swap(sums[k], "fsdp", 2 * k).astype(f32)
-    return total.astype(bf16)
+def ring(count):
+    return list(range(0, count, 2)) + list(range(count - 1, 0, -2))
+
+
+def step(x, hops=1):
+    order = ring(lax.axis_size("fsdp") // 2)
+    count = len(order)
+    pairs = [(order[i], order[(i + hops) % count]) for i in range(count)]
+    return lax.ppermute(x, "fsdp", [(2 * a + c, 2 * b + c) for a, b in pairs for c in (0, 1)])
+
+
+def along(x):
+    count = lax.axis_size("fsdp") // 2
+    groups = [[2 * z + c for z in range(count)] for c in (0, 1)]
+    return lax.all_to_all(
+        x, "fsdp", split_axis=0, concat_axis=0, axis_index_groups=groups, tiled=True
+    )
+
+
+def after(x, *earlier):
+    return lax.optimization_barrier((x,) + earlier)[0]
+
+
+def both_cores(blocks):
+    return [b for block in blocks for b in (block, swap(block, "fsdp", 1))]
+
+
+def pair_sums(mine, theirs):
+    return [add(mine[t], theirs[t]) for t in range(4)]
+
+
+def deal(x):
+    return lax.all_to_all(x, "seq", split_axis=0, concat_axis=0, tiled=True)
+
+
+def share_total(where, parts, out):
+    total = sum(parts[z].astype(f32) for z in range(4)).astype(bf16)
+    for m in range(4):
+        out[m] = total
+
+
+def deal_total(where, x, name):
+    (copies,) = call(share_total, where, [x], [shape(x.shape, bf16)], name=name)
+    return deal(copies)
+
+
+def add(x, y):
+    return (x.astype(f32) + y.astype(f32)).astype(bf16)
 
 
 def body(*args):
@@ -740,124 +785,147 @@
     scale_two,
     out_grad,
 ):
-    where = jnp.stack([lax.axis_index("fsdp"), lax.axis_index("seq")]).astype(jnp.int32)
-    vectors = (
+    f, s = lax.axis_index("fsdp"), lax.axis_index("seq")
+    z = f // 2
+    odd = (z ^ (z // 2)) % 2
+    where = jnp.stack([f, s, z, z ^ (1 + odd), z ^ 3, z ^ (2 - odd)]).astype(jnp.int32)
+    vectors = [
         first_gain, first_bias, query_bias, value_bias, output_bias,
-        scale_one, second_gain, second_bias, down_bias, scale_two,
-    )
-    packed = jnp.pad(up_bias.reshape(4, 128), ((10, 2), (0, 896)))
-    for i, v in enumerate(vectors):
-        packed = packed + jnp.pad(v.reshape(1, 128), ((i, 15 - i), (0, 896)))
+        scale_one, second_gain, second_bias, down_bias, scale_two, up_bias,
+    ]
     seg_col, seg_row = segment_ids.reshape(512, 1), segment_ids.reshape(1, 512)
     mat = shape((512, 1024), bf16)
     rows_f, rows_b = shape((128, 1024), f32), shape((128, 1024), bf16)
 
-    first, second, rows = call(
-        prepare,
-        where,
-        [input_weight, output_weight, up_weight, down_weight, tokens, out_grad, packed],
-        [shape((144, 1024), bf16), shape((256, 1024), bf16), shape((256, 1024), bf16)],
-        name="prepare",
-        scratch=[pltpu.SemaphoreType.DMA((14,))],
-        in_hbm=range(7),
-        out_hbm=True,
+    first, rows = call(
+        prepare_first,
+        where,
+        [input_weight, output_weight, tokens, out_grad] + vectors,
+        [shape((4, 144, 1024), bf16), shape((256, 1024), bf16)],
+        name="prepare_first",
+        scratch=[pltpu.VMEM(v.shape, bf16) for v in vectors] + [pltpu.VMEM((16, 1024), f32), pltpu.SemaphoreType.DMA((32,))],
+        in_hbm=True,
+        limit=63,
     )
     shared = from_others(rows)
-    first_blocks = gather_blocks(first)
+    first_own = along(first)
+    (second,) = call(
+        prepare_second,
+        where,
+        [up_weight, down_weight],
+        [shape((256, 1024), bf16)],
+        name="prepare_second",
+        scratch=[pltpu.SemaphoreType.DMA((36,))],
+        in_hbm=True,
+        limit=63,
+    )
+    second_1 = step(after(second, first_own, *shared[1:]))
     w_in, w_out_own, vecs = call(
         place_first,
         where,
-        first_blocks,
+        [first_own, swap(after(first_own, second, *shared[1:]), "fsdp", 1)],
         [shape((1024, 768), bf16), shape((1024, 256), bf16), shape((16, 1024), f32)],
         name="place_first",
-    )
-    second, _ = lax.optimization_barrier((second, vecs))
-    second_blocks = gather_blocks(second)
+        limit=63,
+    )
     w_out = from_others(w_out_own)
     triple, attended_own, logsum, hidden_one = call(
         attention,
         where,
         shared + [w_in, vecs, seg_col, seg_row],
-        [shape((512, 768), bf16), shape((512, 256), bf16), shape((512, 128), f32), mat],
-        flops=2 * 512 * (1024 * 768 + 4 * 512 * 128),
+        [shape((512, 768), bf16), shape((4, 512, 256), bf16), shape((512, 128), f32), mat],
         name="attention",
     )
+    second_2 = step(after(second_1, attended_own))
+    second_3 = step(after(second_2, *w_out[1:]))
+    shares = deal(attended_own)
     attended, hidden_two, own_middle, own_branch = call(
         project,
         where,
-        from_others(attended_own) + w_out + shared + [vecs],
+        [shares] + w_out + shared + [vecs],
         [mat, mat, rows_f, rows_f],
-        flops=2 * 512 * 1024 * 1024,
         name="project",
         scratch=[pltpu.VMEM((512, 1024), f32)],
     )
     w_down, act, grad_two, grad_before, up_sums, *partial = call(
         feed,
         where,
-        [hidden_two] + second_blocks + shared + [vecs, seg_col],
+        [hidden_two]
+        + both_cores([after(x, shares) for x in (second, second_1, second_2)] + [after(second_3, hidden_two)])
+        + shared + [vecs, seg_col],
         [shape((1024, 1024), bf16), mat, mat, mat, shape((1, 1024), f32), rows_f, rows_b, rows_b, rows_b],
-        flops=3 * 2 * 512 * 1024 * 1024,
         name="feed",
         scratch=[pltpu.VMEM((1024, 1024), bf16)],
     )
-    second_mine, second_theirs, two_sums, *two = call(
+    partial = exchange(partial)
+    (second_theirs,) = call(
+        feed_weights_sent,
+        where,
+        [hidden_two, grad_before, act, grad_two],
+        [shape((4, 256, 1024), bf16)],
+        name="feed_weights_sent",
+    )
+    second_mine, two_sums, *two = call(
         feed_weights,
         where,
         [hidden_two, grad_before, act, grad_two, w_down] + shared + [vecs, seg_col],
-        [shape((4, 256, 1024), bf16)] * 2 + [shape((2, 1024), f32), rows_f, rows_b, rows_b, rows_b],
-        flops=3 * 2 * 512 * 1024 * 1024,
+        [shape((4, 256, 1024), bf16), shape((2, 1024), f32)] + [rows_b] * 4,
         name="feed_weights",
     )
+    second_theirs = swap(after(second_theirs, two[0], *partial[1:]), "fsdp", 1)
     grad_middle, mid_sums, *messages = call(
         middle_back,
         where,
-        exchange(partial) + [own_middle, own_branch, shared[0], seg_col, vecs] + w_out,
+        partial + [own_middle, own_branch, rows, seg_col, vecs] + w_out,
         [rows_f, shape((4, 1024), f32)] + [shape((256, 256), bf16)] * 4,
-        flops=2 * 128 * 1024 * 1024,
         name="middle_back",
         scratch=[pltpu.VMEM((128, 1024), bf16), pltpu.VMEM((128, 1024), bf16)],
     )
-    second_mine, second_theirs, messages = lax.optimization_barrier(
-        (second_mine, second_theirs, messages)
-    )
     got = exchange(messages)
-    grad_triple, one_sums, own_one, *last = call(
+    second_sums = along(add(after(second_mine, messages[1]), second_theirs))
+    twos = exchange([two[0]] + [after(x, *got[1:]) for x in two[1:]])
+    grad_triple, one_sums, *last = call(
         attention_back,
         where,
-        [triple, logsum] + got + [seg_col, seg_row, w_in] + shared + two[1:],
-        [shape((512, 768), bf16), shape((4, 1024), f32), rows_f] + [shape((256, 1024), bf16)] * 3,
-        flops=2 * 512 * (1024 * 768 + 4 * 512 * 64 * 5),
+        [triple, logsum] + got + [seg_col, seg_row, w_in] + shared,
+        [shape((512, 768), bf16), shape((4, 1024), f32)] + [rows_b] * 4,
+        flops=20 * 512 * 1024 * 1024,
         name="attention_back",
     )
+    grad_triple = after(grad_triple, *twos[1:])
     first_mine, first_theirs = call(
         attention_weights,
         where,
         [hidden_one, grad_triple, attended] + got + [up_sums, two_sums, mid_sums, one_sums],
         [shape((4, 144, 1024), bf16)] * 2,
-        flops=2 * 512 * 1024 * 1024,
+        flops=20 * 512 * 1024 * 1024,
         name="attention_weights",
         scratch=[pltpu.VMEM((16, 1024), f32)],
     )
+    ones = exchange([last[0]] + [after(x, *twos[1:]) for x in last[1:]])
+    first_sums = pair_sums(first_mine, swap(first_theirs, "fsdp", 1))
+    first_total = step(after(first_sums[1], *ones[1:]))
     layer_out, tokens_grad = call(
         finish_rows,
         where,
-        exchange([own_one] + last) + [two[0], own_middle, grad_middle, shared[0], vecs],
+        ones + twos + [own_middle, grad_middle, rows, vecs],
         [rows_b, rows_b],
         name="finish_rows",
     )
-    second_share = scatter_blocks(second_mine, second_theirs)
     grad_up, grad_down = call(
         finish_feed,
         where,
-        from_others(second_share),
+        [deal_total(where, after(second_sums, first_total), "share_feed")],
         [shape((128, 4096), f32), shape((512, 1024), f32)],
         name="finish_feed",
     )
-    first_share = scatter_blocks(first_mine, first_theirs)
+    first_total = step(add(first_total, first_sums[2]))
+    first_total = step(after(add(first_total, first_sums[3]), layer_out))
+    first_share = from_others(add(first_total, first_sums[0]))
     grad_in, grad_out, *small = call(
         finish_attention,
         where,
-        from_others(first_share),
+        [after(first_share[0], grad_up)] + first_share[1:],
         [shape((128, 3072), f32), rows_f] + [shape((1, 128), f32)] * 10 + [shape((1, 512), f32)],
         name="finish_attention",
         scratch=[pltpu.VMEM((4, 16, 128), f32)],

time: 294 us -> 235 us (0.80)
  the two profiles are of different devices: /device:TPU:8 before, /device:TPU:0 now
where the time goes in v3:
time: 235 us; the launch traced here: 234 us
  waiting for transfers between devices  92.7 us (39%)
  Pallas kernels  65 us (28%)
  starting transfers between devices  50.1 us (21%)
  local copies, waits for them, and re-layouts  19.4 us (8%)
  other arithmetic  5.18 us (2%)
    pallas_call x15, Pallas kernels, call(): pl.pallas_call(kernel, out_shape=outs, in_specs=[spec(pltpu.SMEM)] + in_s...  65 us
    ppermute x28, waiting for transfers between devices, swap(): return lax.ppermute(x, axis, [(i, i ^ k) for i in range(count)])  61.1 us
    ppermute x28, starting transfers between devices, swap(): return lax.ppermute(x, axis, [(i, i ^ k) for i in range(count)])  25.8 us
    unnamed x96, local copies, waits for them, and re-layouts  18.7 us
    ppermute x6, waiting for transfers between devices, step(): lax.ppermute(x, 'fsdp', [(2 * a + c, 2 * b + c) for a, b in pairs for c i...  13.8 us
    all_to_all x2, waiting for transfers between devices, deal(): return lax.all_to_all(x, 'seq', split_axis=0, concat_axis=0, tiled=True)  13.8 us
    all_to_all x2, starting transfers between devices, along(): lax.all_to_all(x, 'fsdp', split_axis=0, concat_axis=0, axis_index_groups=...  11 us
    all_to_all x2, starting transfers between devices, deal(): return lax.all_to_all(x, 'seq', split_axis=0, concat_axis=0, tiled=True)  8.16 us
  transfers between devices with their start and end apart: 38, of which 20 were waited for; matrix products, arithmetic and copies ran while one was open for 1% of the time, Pallas kernels for 21%

profile of v3, /device:TPU:0, one launch (start us, length us, event | category | flops | bytes accessed | tf_op | source)
XLA Modules:
  0.0 233.6 jit_solution(6184378282092882616)
XLA Ops:
  1.3 3.7 %prepare_first.1 = (bf16[4,144,1024]{2,1,0:T(8,128)(2,1)}, bf16[256,1024]{1,0:T(8,128)(2,1)}) custom-call(s32[6]{0:T(128)} %stack.27.where, bf16[128,3072]{1,0:T(8,128)(2,1)} %refs_0_.1, bf16[128,1024]{1,0:T(8,128)(2,1)} %refs_1_.1, bf16[128,1024]{1,0:T(8,128)(2,1)} %refs_2_.1, bf16[128,1024]{1,0:T(8,128)(2,1)} %refs_3_.1, bf16[128]{0:T(256)(128)(2,1)} %refs_4_.1, ...), custom_call_target="tpu_custom_call" | custom-call | tf_op jit(solution)/shard_map/prepare_first/pallas_call | solution.py:401
  5.0 6.5 %all-to-all-start = ((bf16[4,144,1024]{2,1,0:T(8,128)(2,1)}), bf16[4,144,1024]{2,1,0:T(8,128)(2,1)}, u32[]{:S(2)}, u32[]{:S(2)}) async-start(bf16[4,144,1024]{2,1,0:T(8,128)(2,1)} %get-tuple-element.98), calls=%async_computation | async-start | bytes 2359296 | tf_op jit(solution)/shard_map/all_to_all | solution.py:720
  11.5 2.6 %collective-permute-start.2 = (bf16[256,1024]{1,0:T(8,128)(2,1)S(1)}, bf16[256,1024]{1,0:T(8,128)(2,1)}, u32[]{:S(2)}, u32[]{:S(2)}) collective-permute-start(bf16[256,1024]{1,0:T(8,128)(2,1)S(1)} %copy-done), channel_id=1, source_target_pairs={{0,3},{1,2},{2,1},{3,0},{4,7},{5,6},{6,5},{7,4},{8,11},{9,10},{10,... | collective-permute-start | bytes 1572872 | tf_op jit(solution)/shard_map/ppermute | solution.py:52
  15.0 2.7 %prepare_second.1.refs_1_ = bf16[256,1024]{1,0:T(8,128)(2,1)} custom-call(s32[6]{0:T(128)} %stack.27.where, bf16[128,4096]{1,0:T(8,128)(2,1)} %w_up.1, bf16[512,1024]{1,0:T(8,128)(2,1)} %w_down.1), custom_call_target="tpu_custom_call" | custom-call | tf_op jit(solution)/shard_map/prepare_second/pallas_call | solution.py:401
  17.8 9.7 %collective-permute-done.2.t3.refs_12_.refs_8_ = bf16[256,1024]{1,0:T(8,128)(2,1)} collective-permute-done((bf16[256,1024]{1,0:T(8,128)(2,1)S(1)}, bf16[256,1024]{1,0:T(8,128)(2,1)}, u32[]{:S(2)}, u32[]{:S(2)}) %collective-permute-start.2) | collective-permute-done | bytes 524320 | tf_op jit(solution)/shard_map/ppermute | solution.py:52
  27.4 9.7 %collective-permute-done.1.t2.refs_11_.refs_7_ = bf16[256,1024]{1,0:T(8,128)(2,1)} collective-permute-done((bf16[256,1024]{1,0:T(8,128)(2,1)S(1)}, bf16[256,1024]{1,0:T(8,128)(2,1)}, u32[]{:S(2)}, u32[]{:S(2)}) %collective-permute-start.1) | collective-permute-done | bytes 524320 | tf_op jit(solution)/shard_map/ppermute | solution.py:52
  37.2 2.9 %all-to-all-done.own = bf16[4,144,1024]{2,1,0:T(8,128)(2,1)} async-done(((bf16[4,144,1024]{2,1,0:T(8,128)(2,1)}), bf16[4,144,1024]{2,1,0:T(8,128)(2,1)}, u32[]{:S(2)}, u32[]{:S(2)}) %all-to-all-start) | async-done | bytes 1179680 | tf_op jit(solution)/shard_map/all_to_all | solution.py:720
  40.3 3.0 %collective-permute-done.3.other = bf16[4,144,1024]{2,1,0:T(8,128)(2,1)} collective-permute-done((bf16[4,144,1024]{2,1,0:T(8,128)(2,1)}, bf16[4,144,1024]{2,1,0:T(8,128)(2,1)}, u32[]{:S(2)}, u32[]{:S(2)}) %collective-permute-start.3) | collective-permute-done | bytes 1179680 | tf_op jit(solution)/shard_map/ppermute | solution.py:52
  43.3 3.1 %place_first.1 = (bf16[1024,768]{1,0:T(8,128)(2,1)}, bf16[1024,256]{1,0:T(8,128)(2,1)}, f32[16,1024]{1,0:T(8,128)}) custom-call(s32[6]{0:T(128)} %stack.27.where, bf16[4,144,1024]{2,1,0:T(8,128)(2,1)} %all-to-all-done.own, bf16[4,144,1024]{2,1,0:T(8,128)(2,1)} %collective-permute-done.3.other), custom_call_target="tpu_custom_call" | custom-call | tf_op jit(solution)/shard_map/place_first/pallas_call | solution.py:401
  46.4 2.6 %collective-permute-start.6 = (bf16[1024,256]{1,0:T(8,128)(2,1)}, bf16[1024,256]{1,0:T(8,128)(2,1)S(1)}, u32[]{:S(2)}, u32[]{:S(2)}) collective-permute-start(bf16[1024,256]{1,0:T(8,128)(2,1)} %get-tuple-element.105.w0), channel_id=1, source_target_pairs={{0,3},{1,2},{2,1},{3,0},{4,7},{5,6},{6,5},{7,4},{8,11},{9,10},{10,... | collective-permute-start | bytes 1572872 | tf_op jit(solution)/shard_map/ppermute | solution.py:52
  50.8 6.9 %attention.1 = (bf16[512,768]{1,0:T(8,128)(2,1)S(1)}, bf16[4,512,256]{2,1,0:T(8,128)(2,1)}, f32[512,128]{1,0:T(8,128)S(1)}, bf16[512,1024]{1,0:T(8,128)(2,1)}) custom-call(s32[6]{0:T(128)S(1)} %copy-done.38, bf16[256,1024]{1,0:T(8,128)(2,1)S(1)} %copy-done, bf16[256,1024]{1,0:T(8,128)(2,1)} %collective-permute-done.t1.refs_10_.refs_6_, ...), custom_call_target="tpu_custom_call" | custom-call | tf_op jit(solution)/shard_map/attention/pallas_call | solution.py:401
  58.6 4.3 %all-to-all-start.1 = ((bf16[4,512,256]{2,1,0:T(8,128)(2,1)}), bf16[4,512,256]{2,1,0:T(8,128)(2,1)}, u32[]{:S(2)}, u32[]{:S(2)}) async-start(bf16[4,512,256]{2,1,0:T(8,128)(2,1)} %get-tuple-element.104), calls=%async_computation.1 | async-start | bytes 2097152 | tf_op jit(solution)/shard_map/all_to_all | solution.py:738
  62.8 10.8 %collective-permute-done.5.w2 = bf16[1024,256]{1,0:T(8,128)(2,1)S(1)} collective-permute-done((bf16[1024,256]{1,0:T(8,128)(2,1)}, bf16[1024,256]{1,0:T(8,128)(2,1)S(1)}, u32[]{:S(2)}, u32[]{:S(2)}) %collective-permute-start.5) | collective-permute-done | bytes 524320 | tf_op jit(solution)/shard_map/ppermute | solution.py:52
  73.9 10.3 %all-to-all-done.1.sent = bf16[4,512,256]{2,1,0:T(8,128)(2,1)} async-done(((bf16[4,512,256]{2,1,0:T(8,128)(2,1)}), bf16[4,512,256]{2,1,0:T(8,128)(2,1)}, u32[]{:S(2)}, u32[]{:S(2)}) %all-to-all-start.1) | async-done | bytes 1048608 | tf_op jit(solution)/shard_map/all_to_all | solution.py:738
  84.8 5.2 %project.1 = (bf16[512,1024]{1,0:T(8,128)(2,1)}, bf16[512,1024]{1,0:T(8,128)(2,1)}, f32[128,1024]{1,0:T(8,128)S(1)}, f32[128,1024]{1,0:T(8,128)S(1)}) custom-call(s32[6]{0:T(128)S(1)} %copy-done.38, bf16[4,512,256]{2,1,0:T(8,128)(2,1)} %all-to-all-done.1.sent, bf16[1024,256]{1,0:T(8,128)(2,1)S(1)} %copy-done.11, ...), custom_call_target="tpu_custom_call" | custom-call | tf_op jit(solution)/shard_map/project/pallas_call | solution.py:401
  90.6 1.7 collective-permute-done.13.refs_8_
  94.2 8.5 %feed.1 = (bf16[1024,1024]{1,0:T(8,128)(2,1)}, bf16[512,1024]{1,0:T(8,128)(2,1)}, bf16[512,1024]{1,0:T(8,128)(2,1)}, bf16[512,1024]{1,0:T(8,128)(2,1)}, f32[1,10...) custom-call(s32[6]{0:T(128)S(1)} %copy-done.38, ...), custom_call_target="tpu_custom_call" | custom-call | tf_op jit(solution)/shard_map/feed/pallas_call | solution.py:401
  102.7 1.5 collective-permute-start.14
  104.1 1.6 collective-permute-start.15
  108.6 4.0 %feed_weights_sent.1 = bf16[4,256,1024]{2,1,0:T(8,128)(2,1)} custom-call(s32[6]{0:T(128)S(1)} %copy-done.38, bf16[512,1024]{1,0:T(8,128)(2,1)S(1)} %copy-done.3, bf16[512,1024]{1,0:T(8,128)(2,1)S(1)} %copy-done.6, bf16[512,1024]{1,0:T(8,128)(2,1)S(1)} %copy-done.5, bf16[512,1024]{1,0:T(8,128)(2,1)} %get-tuple-element.128.refs_3_.grad_two), custom_call_target="tpu_custom_call" | custom-call | tf_op jit(solution)/shard_map/feed_weights_sent/pallas_call | solution.py:401
  112.6 6.6 %feed_weights.1 = (bf16[4,256,1024]{2,1,0:T(8,128)(2,1)}, f32[2,1024]{1,0:T(2,128)S(1)}, bf16[128,1024]{1,0:T(8,128)(2,1)S(1)}, bf16[128,1024]{1,0:T(8,128)(2,1)...) custom-call(s32[6]{0:T(128)S(1)} %copy-done.38, bf16[512,1024]{1,0:T(8,128)(2,1)} %get-tuple-element.106.refs_0_.hidden, ...), custom_call_target="tpu_custom_call" | custom-call | tf_op jit(solution)/shard_map/feed_weights/pallas_call | solution.py:401
  119.4 3.6 %middle_back.1 = (f32[128,1024]{1,0:T(8,128)S(1)}, f32[4,1024]{1,0:T(4,128)S(1)}, bf16[256,256]{1,0:T(8,128)(2,1)S(1)}, bf16[256,256]{1,0:T(8,128)(2,1)S(1)}, bf...) custom-call(s32[6]{0:T(128)S(1)} %copy-done.38, f32[128,1024]{1,0:T(8,128)S(1)} %get-tuple-element.114.p0, ...), custom_call_target="tpu_custom_call" | custom-call | tf_op jit(solution)/shard_map/middle_back/pallas_call | solution.py:401
  123.7 2.3 add_convert_fusion
  126.0 4.6 %all-to-all-start.2 = ((bf16[4,256,1024]{2,1,0:T(8,128)(2,1)}), bf16[4,256,1024]{2,1,0:T(8,128)(2,1)}, u32[]{:S(2)}, u32[]{:S(2)}) async-start(bf16[4,256,1024]{2,1,0:T(8,128)(2,1)} %add_convert_fusion), calls=%async_computation.2 | async-start | bytes 4194304 | tf_op jit(solution)/shard_map/all_to_all | solution.py:720
  130.6 1.4 collective-permute-start.18
  132.1 1.6 collective-permute-start.19
  134.2 5.2 %collective-permute-done.18.m2 = bf16[256,256]{1,0:T(8,128)(2,1)S(1)} collective-permute-done((bf16[256,256]{1,0:T(8,128)(2,1)S(1)}, bf16[256,256]{1,0:T(8,128)(2,1)S(1)}, u32[]{:S(2)}, u32[]{:S(2)}) %collective-permute-start.18) | collective-permute-done | bytes 131104 | tf_op jit(solution)/shard_map/ppermute | solution.py:52
  140.6 2.5 %collective-permute-start.22 = (bf16[128,1024]{1,0:T(8,128)(2,1)}, bf16[128,1024]{1,0:T(8,128)(2,1)S(1)}, u32[]{:S(2)}, u32[]{:S(2)}) collective-permute-start(bf16[128,1024]{1,0:T(8,128)(2,1)} %get-tuple-element.135), channel_id=1, source_target_pairs={{0,3},{1,2},{2,1},{3,0},{4,7},{5,6},{6,5},{7,4},{8,11},{9,10},{10,... | collective-permute-start | bytes 786440 | tf_op jit(solution)/shard_map/ppermute | solution.py:52
  144.1 8.2 %attention_back.1 = (bf16[512,768]{1,0:T(8,128)(2,1)}, f32[4,1024]{1,0:T(4,128)S(1)}, bf16[128,1024]{1,0:T(8,128)(2,1)S(1)}, bf16[128,1024]{1,0:T(8,128)(2,1)S(1...) custom-call(s32[6]{0:T(128)S(1)} %copy-done.38, bf16[512,768]{1,0:T(8,128)(2,1)} %copy-done.19, ...), custom_call_target="tpu_custom_call" | custom-call | tf_op jit(solution)/shard_map/attention_back/pallas_call | solution.py:401
  156.4 3.3 %attention_weights.1 = (bf16[4,144,1024]{2,1,0:T(8,128)(2,1)}, bf16[4,144,1024]{2,1,0:T(8,128)(2,1)}) custom-call(s32[6]{0:T(128)S(1)} %copy-done.38, bf16[512,1024]{1,0:T(8,128)(2,1)S(1)} %copy-done.16, bf16[512,768]{1,0:T(8,128)(2,1)S(1)} %copy-done.18, bf16[512,1024]{1,0:T(8,128)(2,1)S(1)} %copy-done.17, bf16[256,256]{1,0:T(8,128)(2,1)S(1)} %get-tuple-element.120.m0, ...), custom_call_target="tpu_custom_call" | custom-call | tf_op jit(solution)/shard_map/attention_weights/pallas_call | solution.py:401
  159.7 1.5 collective-permute-start.23
  164.5 4.4 %collective-permute-done.23.refs_1_ = bf16[128,1024]{1,0:T(8,128)(2,1)S(1)} collective-permute-done((bf16[128,1024]{1,0:T(8,128)(2,1)S(1)}, bf16[128,1024]{1,0:T(8,128)(2,1)S(1)}, u32[]{:S(2)}, u32[]{:S(2)}) %collective-permute-start.23) | collective-permute-done | bytes 262176 | tf_op jit(solution)/shard_map/ppermute | solution.py:52
  168.8 6.4 %collective-permute-done.24.refs_2_ = bf16[128,1024]{1,0:T(8,128)(2,1)S(1)} collective-permute-done((bf16[128,1024]{1,0:T(8,128)(2,1)S(1)}, bf16[128,1024]{1,0:T(8,128)(2,1)S(1)}, u32[]{:S(2)}, u32[]{:S(2)}) %collective-permute-start.24) | collective-permute-done | bytes 262176 | tf_op jit(solution)/shard_map/ppermute | solution.py:52
  175.2 2.3 collective-permute-start.27
  177.5 7.6 %collective-permute-done.27 = bf16[144,1024]{1,0:T(8,128)(2,1)S(1)} collective-permute-done((bf16[144,1024]{1,0:T(8,128)(2,1)S(1)}, bf16[144,1024]{1,0:T(8,128)(2,1)S(1)}, u32[]{:S(2)}, u32[]{:S(2)}) %collective-permute-start.27) | collective-permute-done | bytes 294944 | tf_op jit(solution)/shard_map/ppermute | solution.py:714
  186.1 1.9 share_feed.1
  188.0 1.3 copy-done.4
  189.4 3.9 %all-to-all-start.3 = ((bf16[4,256,1024]{2,1,0:T(8,128)(2,1)}), bf16[4,256,1024]{2,1,0:T(8,128)(2,1)S(1)}, u32[]{:S(2)}, u32[]{:S(2)}) async-start(bf16[4,256,1024]{2,1,0:T(8,128)(2,1)} %copy-done.4), calls=%async_computation.3 | async-start | bytes 4194304 | tf_op jit(solution)/shard_map/all_to_all | solution.py:738
  193.3 1.4 fusion.2
  203.4 2.0 finish_rows.1
  205.6 1.5 collective-permute-start.29
  207.1 6.2 %collective-permute-done.29 = bf16[144,1024]{1,0:T(8,128)(2,1)S(1)} collective-permute-done((bf16[144,1024]{1,0:T(8,128)(2,1)S(1)}, bf16[144,1024]{1,0:T(8,128)(2,1)S(1)}, u32[]{:S(2)}, u32[]{:S(2)}) %collective-permute-start.29) | collective-permute-done | bytes 294944 | tf_op jit(solution)/shard_map/ppermute | solution.py:714
  213.5 2.7 %collective-permute-start.33 = (bf16[144,1024]{1,0:T(8,128)(2,1)S(1)}, bf16[144,1024]{1,0:T(8,128)(2,1)S(1)}, u32[]{:S(2)}, u32[]{:S(2)}) collective-permute-start(bf16[144,1024]{1,0:T(8,128)(2,1)S(1)} %fusion.s0), channel_id=1, source_target_pairs={{0,3},{1,2},{2,1},{3,0},{4,7},{5,6},{6,5},{7,4},{8,11},{9,10},{10,... | collective-permute-start | bytes 884744 | tf_op jit(solution)/shard_map/ppermute | solution.py:52
  217.0 3.5 %all-to-all-done.3.got = bf16[4,256,1024]{2,1,0:T(8,128)(2,1)S(1)} async-done(((bf16[4,256,1024]{2,1,0:T(8,128)(2,1)}), bf16[4,256,1024]{2,1,0:T(8,128)(2,1)S(1)}, u32[]{:S(2)}, u32[]{:S(2)}) %all-to-all-start.3) | async-done | bytes 2097184 | tf_op jit(solution)/shard_map/all_to_all | solution.py:738
  220.5 2.9 %finish_feed.1 = (f32[128,4096]{1,0:T(8,128)}, f32[512,1024]{1,0:T(8,128)}) custom-call(s32[6]{0:T(128)S(1)} %copy-done.38, bf16[4,256,1024]{2,1,0:T(8,128)(2,1)S(1)} %all-to-all-done.3.got), custom_call_target="tpu_custom_call" | custom-call | tf_op jit(solution)/shard_map/finish_feed/pallas_call | solution.py:401
  223.4 3.4 %collective-permute-done.33.s3 = bf16[144,1024]{1,0:T(8,128)(2,1)S(1)} collective-permute-done((bf16[144,1024]{1,0:T(8,128)(2,1)S(1)}, bf16[144,1024]{1,0:T(8,128)(2,1)S(1)}, u32[]{:S(2)}, u32[]{:S(2)}) %collective-permute-start.33) | collective-permute-done | bytes 294944 | tf_op jit(solution)/shard_map/ppermute | solution.py:52
  226.8 4.1 %collective-permute-done.32.s2 = bf16[144,1024]{1,0:T(8,128)(2,1)S(1)} collective-permute-done((bf16[144,1024]{1,0:T(8,128)(2,1)S(1)}, bf16[144,1024]{1,0:T(8,128)(2,1)S(1)}, u32[]{:S(2)}, u32[]{:S(2)}) %collective-permute-start.32) | collective-permute-done | bytes 294944 | tf_op jit(solution)/shard_map/ppermute | solution.py:52
  231.1 2.4 %finish_attention.1 = (f32[128,3072]{1,0:T(8,128)}, f32[128,1024]{1,0:T(8,128)}, f32[1,128]{1,0:T(1,128)}, f32[1,128]{1,0:T(1,128)}, f32[1,128]{1,0:T(1,128)}, /...) custom-call(s32[6]{0:T(128)S(1)} %copy-done.38, ...), custom_call_target="tpu_custom_call" | custom-call | tf_op jit(solution)/shard_map/finish_attention/pallas_call | solution.py:401
  (146 shorter events, 32.6 us)
Async XLA Ops:
  5.0 35.1 %copy-start.39 = (s32[512]{0:T(512)S(1)}, s32[512]{0:T(512)}, u32[]{:S(2)}) copy-start(s32[512]{0:T(512)} %param.19) | copy-start | bytes 6148
  5.0 35.1 %all-to-all-start = ((bf16[4,144,1024]{2,1,0:T(8,128)(2,1)}), bf16[4,144,1024]{2,1,0:T(8,128)(2,1)}, u32[]{:S(2)}, u32[]{:S(2)}) async-start(bf16[4,144,1024]{2,1,0:T(8,128)(2,1)} %get-tuple-element.98), calls=%async_computation | async-start | bytes 2359296 | tf_op jit(solution)/shard_map/all_to_all | solution.py:720
  11.5 38.4 %copy-start.38 = (s32[6]{0:T(128)S(1)}, s32[6]{0:T(128)}, u32[]{:S(2)}) copy-start(s32[6]{0:T(128)} %stack.27.where) | copy-start | bytes 76
  11.5 15.9 %collective-permute-start.2 = (bf16[256,1024]{1,0:T(8,128)(2,1)S(1)}, bf16[256,1024]{1,0:T(8,128)(2,1)}, u32[]{:S(2)}, u32[]{:S(2)}) collective-permute-start(bf16[256,1024]{1,0:T(8,128)(2,1)S(1)} %copy-done), channel_id=1, source_target_pairs={{0,3},{1,2},{2,1},{3,0},{4,7},{5,6},{6,5},{7,4},{8,11},{9,10},{10,... | collective-permute-start | bytes 1572872 | tf_op jit(solution)/shard_map/ppermute | solution.py:52
  14.1 23.0 %collective-permute-start.1 = (bf16[256,1024]{1,0:T(8,128)(2,1)S(1)}, bf16[256,1024]{1,0:T(8,128)(2,1)}, u32[]{:S(2)}, u32[]{:S(2)}) collective-permute-start(bf16[256,1024]{1,0:T(8,128)(2,1)S(1)} %copy-done), channel_id=1, source_target_pairs={{0,2},{1,3},{2,0},{3,1},{4,6},{5,7},{6,4},{7,5},{8,10},{9,11},{10,... | collective-permute-start | bytes 1572872 | tf_op jit(solution)/shard_map/ppermute | solution.py:52
  14.5 22.7 %collective-permute-start = (bf16[256,1024]{1,0:T(8,128)(2,1)S(1)}, bf16[256,1024]{1,0:T(8,128)(2,1)}, u32[]{:S(2)}, u32[]{:S(2)}) collective-permute-start(bf16[256,1024]{1,0:T(8,128)(2,1)S(1)} %copy-done), channel_id=1, source_target_pairs={{0,1},{1,0},{2,3},{3,2},{4,5},{5,4},{6,7},{7,6},{8,9},{9,8},{10,11... | collective-permute-start | bytes 1572872 | tf_op jit(solution)/shard_map/ppermute | solution.py:52
  40.2 3.2 %collective-permute-start.3 = (bf16[4,144,1024]{2,1,0:T(8,128)(2,1)}, bf16[4,144,1024]{2,1,0:T(8,128)(2,1)}, u32[]{:S(2)}, u32[]{:S(2)}) collective-permute-start(bf16[4,144,1024]{2,1,0:T(8,128)(2,1)} %all-to-all-done.own), channel_id=1, source_target_pairs={{0,4},{4,0},{8,12},{12,8},{16,20},{20,16},{24,28},{28,24},{1,5},{5... | collective-permute-start | bytes 3538952 | tf_op jit(solution)/shard_map/ppermute | solution.py:52
  40.2 18.4 %collective-permute-start.8 = (bf16[256,1024]{1,0:T(8,128)(2,1)}, bf16[256,1024]{1,0:T(8,128)(2,1)}, u32[]{:S(2)}, u32[]{:S(2)}) collective-permute-start(bf16[256,1024]{1,0:T(8,128)(2,1)} %prepare_second.1.refs_1_), channel_id=1, source_target_pairs={{0,16},{4,20},{16,24},{20,28},{24,8},{28,12},{8,0},{12,4},{1,17},{... | collective-permute-start | bytes 1572872 | tf_op jit(solution)/shard_map/ppermute | solution.py:714
  46.4 16.4 %collective-permute-start.6 = (bf16[1024,256]{1,0:T(8,128)(2,1)}, bf16[1024,256]{1,0:T(8,128)(2,1)S(1)}, u32[]{:S(2)}, u32[]{:S(2)}) collective-permute-start(bf16[1024,256]{1,0:T(8,128)(2,1)} %get-tuple-element.105.w0), channel_id=1, source_target_pairs={{0,3},{1,2},{2,1},{3,0},{4,7},{5,6},{6,5},{7,4},{8,11},{9,10},{10,... | collective-permute-start | bytes 1572872 | tf_op jit(solution)/shard_map/ppermute | solution.py:52
  49.0 24.6 %collective-permute-start.5 = (bf16[1024,256]{1,0:T(8,128)(2,1)}, bf16[1024,256]{1,0:T(8,128)(2,1)S(1)}, u32[]{:S(2)}, u32[]{:S(2)}) collective-permute-start(bf16[1024,256]{1,0:T(8,128)(2,1)} %get-tuple-element.105.w0), channel_id=1, source_target_pairs={{0,2},{1,3},{2,0},{3,1},{4,6},{5,7},{6,4},{7,5},{8,10},{9,11},{10,... | collective-permute-start | bytes 1572872 | tf_op jit(solution)/shard_map/ppermute | solution.py:52
  49.4 24.2 %collective-permute-start.4 = (bf16[1024,256]{1,0:T(8,128)(2,1)}, bf16[1024,256]{1,0:T(8,128)(2,1)S(1)}, u32[]{:S(2)}, u32[]{:S(2)}) collective-permute-start(bf16[1024,256]{1,0:T(8,128)(2,1)} %get-tuple-element.105.w0), channel_id=1, source_target_pairs={{0,1},{1,0},{2,3},{3,2},{4,5},{5,4},{6,7},{7,6},{8,9},{9,8},{10,11... | collective-permute-start | bytes 1572872 | tf_op jit(solution)/shard_map/ppermute | solution.py:52
  50.8 34.0 %copy-start.8 = (f32[16,1024]{1,0:T(8,128)S(1)}, f32[16,1024]{1,0:T(8,128)}, u32[]{:S(2)}) copy-start(f32[16,1024]{1,0:T(8,128)} %get-tuple-element.101.vecs.refs_13_.refs_9_.refs_11_) | copy-start | bytes 196612
  50.8 34.0 %copy-start.11 = (bf16[1024,256]{1,0:T(8,128)(2,1)S(1)}, bf16[1024,256]{1,0:T(8,128)(2,1)}, u32[]{:S(2)}) copy-start(bf16[1024,256]{1,0:T(8,128)(2,1)} %get-tuple-element.105.w0) | copy-start | bytes 1572868
  58.6 26.2 %copy-start.36 = (f32[512,128]{1,0:T(8,128)}, f32[512,128]{1,0:T(8,128)S(1)}, u32[]{:S(2)}) copy-start(f32[512,128]{1,0:T(8,128)S(1)} %get-tuple-element.103.logsum) | copy-start | bytes 786436
  58.6 15.1 %collective-permute-start.10 = (bf16[256,1024]{1,0:T(8,128)(2,1)}, bf16[256,1024]{1,0:T(8,128)(2,1)}, u32[]{:S(2)}, u32[]{:S(2)}) collective-permute-start(bf16[256,1024]{1,0:T(8,128)(2,1)} %collective-permute-done.8.refs_3_), channel_id=1, source_target_pairs={{0,16},{4,20},{16,24},{20,28},{24,8},{28,12},{8,0},{12,4},{1,17},{... | collective-permute-start | bytes 1572872 | tf_op jit(solution)/shard_map/ppermute | solution.py:714
  58.6 25.7 %all-to-all-start.1 = ((bf16[4,512,256]{2,1,0:T(8,128)(2,1)}), bf16[4,512,256]{2,1,0:T(8,128)(2,1)}, u32[]{:S(2)}, u32[]{:S(2)}) async-start(bf16[4,512,256]{2,1,0:T(8,128)(2,1)} %get-tuple-element.104), calls=%async_computation.1 | async-start | bytes 2097152 | tf_op jit(solution)/shard_map/all_to_all | solution.py:738
  62.8 27.1 %copy-start.12 = (bf16[1024,256]{1,0:T(8,128)(2,1)}, bf16[1024,256]{1,0:T(8,128)(2,1)S(1)}, u32[]{:S(2)}) copy-start(bf16[1024,256]{1,0:T(8,128)(2,1)S(1)} %collective-permute-done.6.w3) | copy-start | bytes 1572868
  73.7 16.3 %collective-permute-start.12 = (bf16[256,1024]{1,0:T(8,128)(2,1)}, bf16[256,1024]{1,0:T(8,128)(2,1)}, u32[]{:S(2)}, u32[]{:S(2)}) collective-permute-start(bf16[256,1024]{1,0:T(8,128)(2,1)} %collective-permute-done.10.refs_5_), channel_id=1, source_target_pairs={{0,16},{4,20},{16,24},{20,28},{24,8},{28,12},{8,0},{12,4},{1,17},{... | collective-permute-start | bytes 1572872 | tf_op jit(solution)/shard_map/ppermute | solution.py:714
  84.2 6.3 %collective-permute-start.7 = (bf16[256,1024]{1,0:T(8,128)(2,1)}, bf16[256,1024]{1,0:T(8,128)(2,1)S(1)}, u32[]{:S(2)}, u32[]{:S(2)}) collective-permute-start(bf16[256,1024]{1,0:T(8,128)(2,1)} %prepare_second.1.refs_1_), channel_id=1, source_target_pairs={{0,4},{4,0},{8,12},{12,8},{16,20},{20,16},{24,28},{28,24},{1,5},{5... | collective-permute-start | bytes 1572872 | tf_op jit(solution)/shard_map/ppermute | solution.py:52
  84.2 6.3 %collective-permute-start.9 = (bf16[256,1024]{1,0:T(8,128)(2,1)}, bf16[256,1024]{1,0:T(8,128)(2,1)S(1)}, u32[]{:S(2)}, u32[]{:S(2)}) collective-permute-start(bf16[256,1024]{1,0:T(8,128)(2,1)} %collective-permute-done.8.refs_3_), channel_id=1, source_target_pairs={{0,4},{4,0},{8,12},{12,8},{16,20},{20,16},{24,28},{28,24},{1,5},{5... | collective-permute-start | bytes 1572872 | tf_op jit(solution)/shard_map/ppermute | solution.py:52
  84.7 5.8 %collective-permute-start.11 = (bf16[256,1024]{1,0:T(8,128)(2,1)}, bf16[256,1024]{1,0:T(8,128)(2,1)S(1)}, u32[]{:S(2)}, u32[]{:S(2)}) collective-permute-start(bf16[256,1024]{1,0:T(8,128)(2,1)} %collective-permute-done.10.refs_5_), channel_id=1, source_target_pairs={{0,4},{4,0},{8,12},{12,8},{16,20},{20,16},{24,28},{28,24},{1,5},{5... | collective-permute-start | bytes 1572872 | tf_op jit(solution)/shard_map/ppermute | solution.py:52
  90.0 29.4 %copy-start.9 = (f32[128,1024]{1,0:T(8,128)}, f32[128,1024]{1,0:T(8,128)S(1)}, u32[]{:S(2)}) copy-start(f32[128,1024]{1,0:T(8,128)S(1)} %get-tuple-element.118.own_middle.refs_8_) | copy-start | bytes 1572868
  90.0 2.3 collective-permute-start.13
  102.7 16.6 %collective-permute-start.14 = (bf16[128,1024]{1,0:T(8,128)(2,1)S(1)}, bf16[128,1024]{1,0:T(8,128)(2,1)S(1)}, u32[]{:S(2)}, u32[]{:S(2)}) collective-permute-start(bf16[128,1024]{1,0:T(8,128)(2,1)S(1)} %get-tuple-element.115), channel_id=1, source_target_pairs={{0,1},{1,0},{2,3},{3,2},{4,5},{5,4},{6,7},{7,6},{8,9},{9,8},{10,11... | collective-permute-start | bytes 786440 | tf_op jit(solution)/shard_map/ppermute | solution.py:52
  104.1 15.1 %collective-permute-start.15 = (bf16[128,1024]{1,0:T(8,128)(2,1)S(1)}, bf16[128,1024]{1,0:T(8,128)(2,1)S(1)}, u32[]{:S(2)}, u32[]{:S(2)}) collective-permute-start(bf16[128,1024]{1,0:T(8,128)(2,1)S(1)} %get-tuple-element.116), channel_id=1, source_target_pairs={{0,2},{1,3},{2,0},{3,1},{4,6},{5,7},{6,4},{7,5},{8,10},{9,11},{10,... | collective-permute-start | bytes 786440 | tf_op jit(solution)/shard_map/ppermute | solution.py:52
  105.8 13.5 %collective-permute-start.16 = (bf16[128,1024]{1,0:T(8,128)(2,1)S(1)}, bf16[128,1024]{1,0:T(8,128)(2,1)S(1)}, u32[]{:S(2)}, u32[]{:S(2)}) collective-permute-start(bf16[128,1024]{1,0:T(8,128)(2,1)S(1)} %get-tuple-element.117), channel_id=1, source_target_pairs={{0,3},{1,2},{2,1},{3,0},{4,7},{5,6},{6,5},{7,4},{8,11},{9,10},{10,... | collective-permute-start | bytes 786440 | tf_op jit(solution)/shard_map/ppermute | solution.py:52
  119.3 4.5 %collective-permute-start.30 = (bf16[4,256,1024]{2,1,0:T(8,128)(2,1)S(1)}, bf16[4,256,1024]{2,1,0:T(8,128)(2,1)S(1)}, u32[]{:S(2)}, u32[]{:S(2)}) collective-permute-start(bf16[4,256,1024]{2,1,0:T(8,128)(2,1)S(1)} %copy-done.41), channel_id=1, source_target_pairs={{0,4},{4,0},{8,12},{12,8},{16,20},{20,16},{24,28},{28,24},{1,5},{5... | collective-permute-start | bytes 6291464 | tf_op jit(solution)/shard_map/ppermute | solution.py:52
  126.0 18.1 %copy-start.37 = (f32[512,128]{1,0:T(8,128)S(1)}, f32[512,128]{1,0:T(8,128)}, u32[]{:S(2)}) copy-start(f32[512,128]{1,0:T(8,128)} %copy-done.36) | copy-start | bytes 786436
  126.0 60.1 %all-to-all-start.2 = ((bf16[4,256,1024]{2,1,0:T(8,128)(2,1)}), bf16[4,256,1024]{2,1,0:T(8,128)(2,1)}, u32[]{:S(2)}, u32[]{:S(2)}) async-start(bf16[4,256,1024]{2,1,0:T(8,128)(2,1)} %add_convert_fusion), calls=%async_computation.2 | async-start | bytes 4194304 | tf_op jit(solution)/shard_map/all_to_all | solution.py:720
  130.6 8.8 %collective-permute-start.18 = (bf16[256,256]{1,0:T(8,128)(2,1)S(1)}, bf16[256,256]{1,0:T(8,128)(2,1)S(1)}, u32[]{:S(2)}, u32[]{:S(2)}) collective-permute-start(bf16[256,256]{1,0:T(8,128)(2,1)S(1)} %get-tuple-element.122), channel_id=1, source_target_pairs={{0,2},{1,3},{2,0},{3,1},{4,6},{5,7},{6,4},{7,5},{8,10},{9,11},{10,... | collective-permute-start | bytes 393224 | tf_op jit(solution)/shard_map/ppermute | solution.py:52
  132.1 7.3 %collective-permute-start.19 = (bf16[256,256]{1,0:T(8,128)(2,1)S(1)}, bf16[256,256]{1,0:T(8,128)(2,1)S(1)}, u32[]{:S(2)}, u32[]{:S(2)}) collective-permute-start(bf16[256,256]{1,0:T(8,128)(2,1)S(1)} %get-tuple-element.123), channel_id=1, source_target_pairs={{0,3},{1,2},{2,1},{3,0},{4,7},{5,6},{6,5},{7,4},{8,11},{9,10},{10,... | collective-permute-start | bytes 393224 | tf_op jit(solution)/shard_map/ppermute | solution.py:52
  133.6 7.0 %collective-permute-start.17 = (bf16[256,256]{1,0:T(8,128)(2,1)S(1)}, bf16[256,256]{1,0:T(8,128)(2,1)S(1)}, u32[]{:S(2)}, u32[]{:S(2)}) collective-permute-start(bf16[256,256]{1,0:T(8,128)(2,1)S(1)} %get-tuple-element.121), channel_id=1, source_target_pairs={{0,1},{1,0},{2,3},{3,2},{4,5},{5,4},{6,7},{7,6},{8,9},{9,8},{10,11... | collective-permute-start | bytes 393224 | tf_op jit(solution)/shard_map/ppermute | solution.py:52
  140.6 12.4 %collective-permute-start.22 = (bf16[128,1024]{1,0:T(8,128)(2,1)}, bf16[128,1024]{1,0:T(8,128)(2,1)S(1)}, u32[]{:S(2)}, u32[]{:S(2)}) collective-permute-start(bf16[128,1024]{1,0:T(8,128)(2,1)} %get-tuple-element.135), channel_id=1, source_target_pairs={{0,3},{1,2},{2,1},{3,0},{4,7},{5,6},{6,5},{7,4},{8,11},{9,10},{10,... | collective-permute-start | bytes 786440 | tf_op jit(solution)/shard_map/ppermute | solution.py:52
  143.1 11.9 %collective-permute-start.21 = (bf16[128,1024]{1,0:T(8,128)(2,1)}, bf16[128,1024]{1,0:T(8,128)(2,1)S(1)}, u32[]{:S(2)}, u32[]{:S(2)}) collective-permute-start(bf16[128,1024]{1,0:T(8,128)(2,1)} %get-tuple-element.133), channel_id=1, source_target_pairs={{0,2},{1,3},{2,0},{3,1},{4,6},{5,7},{6,4},{7,5},{8,10},{9,11},{10,... | collective-permute-start | bytes 786440 | tf_op jit(solution)/shard_map/ppermute | solution.py:52
  143.5 11.5 %collective-permute-start.20 = (bf16[128,1024]{1,0:T(8,128)(2,1)}, bf16[128,1024]{1,0:T(8,128)(2,1)S(1)}, u32[]{:S(2)}, u32[]{:S(2)}) collective-permute-start(bf16[128,1024]{1,0:T(8,128)(2,1)} %get-tuple-element.131), channel_id=1, source_target_pairs={{0,1},{1,0},{2,3},{3,2},{4,5},{5,4},{6,7},{7,6},{8,9},{9,8},{10,11... | collective-permute-start | bytes 786440 | tf_op jit(solution)/shard_map/ppermute | solution.py:52
  159.6 3.6 %collective-permute-start.26 = (bf16[4,144,1024]{2,1,0:T(8,128)(2,1)}, bf16[4,144,1024]{2,1,0:T(8,128)(2,1)S(1)}, u32[]{:S(2)}, u32[]{:S(2)}) collective-permute-start(bf16[4,144,1024]{2,1,0:T(8,128)(2,1)} %get-tuple-element.154), channel_id=1, source_target_pairs={{0,4},{4,0},{8,12},{12,8},{16,20},{20,16},{24,28},{28,24},{1,5},{5... | collective-permute-start | bytes 3538952 | tf_op jit(solution)/shard_map/ppermute | solution.py:52
  159.7 9.1 %collective-permute-start.23 = (bf16[128,1024]{1,0:T(8,128)(2,1)S(1)}, bf16[128,1024]{1,0:T(8,128)(2,1)S(1)}, u32[]{:S(2)}, u32[]{:S(2)}) collective-permute-start(bf16[128,1024]{1,0:T(8,128)(2,1)S(1)} %get-tuple-element.136), channel_id=1, source_target_pairs={{0,1},{1,0},{2,3},{3,2},{4,5},{5,4},{6,7},{7,6},{8,9},{9,8},{10,11... | collective-permute-start | bytes 786440 | tf_op jit(solution)/shard_map/ppermute | solution.py:52
  161.2 14.0 %collective-permute-start.24 = (bf16[128,1024]{1,0:T(8,128)(2,1)S(1)}, bf16[128,1024]{1,0:T(8,128)(2,1)S(1)}, u32[]{:S(2)}, u32[]{:S(2)}) collective-permute-start(bf16[128,1024]{1,0:T(8,128)(2,1)S(1)} %get-tuple-element.138), channel_id=1, source_target_pairs={{0,2},{1,3},{2,0},{3,1},{4,6},{5,7},{6,4},{7,5},{8,10},{9,11},{10,... | collective-permute-start | bytes 786440 | tf_op jit(solution)/shard_map/ppermute | solution.py:52
  161.9 13.3 %collective-permute-start.25 = (bf16[128,1024]{1,0:T(8,128)(2,1)S(1)}, bf16[128,1024]{1,0:T(8,128)(2,1)S(1)}, u32[]{:S(2)}, u32[]{:S(2)}) collective-permute-start(bf16[128,1024]{1,0:T(8,128)(2,1)S(1)} %get-tuple-element.140), channel_id=1, source_target_pairs={{0,3},{1,2},{2,1},{3,0},{4,7},{5,6},{6,5},{7,4},{8,11},{9,10},{10,... | collective-permute-start | bytes 786440 | tf_op jit(solution)/shard_map/ppermute | solution.py:52
  163.2 24.8 %copy-start.43 = (bf16[4,144,1024]{2,1,0:T(8,128)(2,1)}, bf16[4,144,1024]{2,1,0:T(8,128)(2,1)S(1)}, u32[]{:S(2)}) copy-start(bf16[4,144,1024]{2,1,0:T(8,128)(2,1)S(1)} %collective-permute-done.26) | copy-start | bytes 3538948
  168.8 19.2 %copy-start.30 = (bf16[128,1024]{1,0:T(8,128)(2,1)}, bf16[128,1024]{1,0:T(8,128)(2,1)S(1)}, u32[]{:S(2)}) copy-start(bf16[128,1024]{1,0:T(8,128)(2,1)S(1)} %collective-permute-done.23.refs_1_) | copy-start | bytes 786436
  175.2 9.9 %collective-permute-start.27 = (bf16[144,1024]{1,0:T(8,128)(2,1)S(1)}, bf16[144,1024]{1,0:T(8,128)(2,1)S(1)}, u32[]{:S(2)}, u32[]{:S(2)}) collective-permute-start(bf16[144,1024]{1,0:T(8,128)(2,1)S(1)} %fusion.3), channel_id=1, source_target_pairs={{0,16},{4,20},{16,24},{20,28},{24,8},{28,12},{8,0},{12,4},{1,17},{... | collective-permute-start | bytes 884744 | tf_op jit(solution)/shard_map/ppermute | solution.py:714
  189.4 31.2 %all-to-all-start.3 = ((bf16[4,256,1024]{2,1,0:T(8,128)(2,1)}), bf16[4,256,1024]{2,1,0:T(8,128)(2,1)S(1)}, u32[]{:S(2)}, u32[]{:S(2)}) async-start(bf16[4,256,1024]{2,1,0:T(8,128)(2,1)} %copy-done.4), calls=%async_computation.3 | async-start | bytes 4194304 | tf_op jit(solution)/shard_map/all_to_all | solution.py:738
  194.6 10.8 %collective-permute-start.28 = (bf16[144,1024]{1,0:T(8,128)(2,1)S(1)}, bf16[144,1024]{1,0:T(8,128)(2,1)S(1)}, u32[]{:S(2)}, u32[]{:S(2)}) collective-permute-start(bf16[144,1024]{1,0:T(8,128)(2,1)S(1)} %fusion.2), channel_id=1, source_target_pairs={{0,16},{4,20},{16,24},{20,28},{24,8},{28,12},{8,0},{12,4},{1,17},{... | collective-permute-start | bytes 884744 | tf_op jit(solution)/shard_map/ppermute | solution.py:714
  205.6 7.7 %collective-permute-start.29 = (bf16[144,1024]{1,0:T(8,128)(2,1)S(1)}, bf16[144,1024]{1,0:T(8,128)(2,1)S(1)}, u32[]{:S(2)}, u32[]{:S(2)}) collective-permute-start(bf16[144,1024]{1,0:T(8,128)(2,1)S(1)} %fusion.1), channel_id=1, source_target_pairs={{0,16},{4,20},{16,24},{20,28},{24,8},{28,12},{8,0},{12,4},{1,17},{... | collective-permute-start | bytes 884744 | tf_op jit(solution)/shard_map/ppermute | solution.py:714
  213.5 13.3 %collective-permute-start.33 = (bf16[144,1024]{1,0:T(8,128)(2,1)S(1)}, bf16[144,1024]{1,0:T(8,128)(2,1)S(1)}, u32[]{:S(2)}, u32[]{:S(2)}) collective-permute-start(bf16[144,1024]{1,0:T(8,128)(2,1)S(1)} %fusion.s0), channel_id=1, source_target_pairs={{0,3},{1,2},{2,1},{3,0},{4,7},{5,6},{6,5},{7,4},{8,11},{9,10},{10,... | collective-permute-start | bytes 884744 | tf_op jit(solution)/shard_map/ppermute | solution.py:52
  216.1 14.7 %collective-permute-start.32 = (bf16[144,1024]{1,0:T(8,128)(2,1)S(1)}, bf16[144,1024]{1,0:T(8,128)(2,1)S(1)}, u32[]{:S(2)}, u32[]{:S(2)}) collective-permute-start(bf16[144,1024]{1,0:T(8,128)(2,1)S(1)} %fusion.s0), channel_id=1, source_target_pairs={{0,2},{1,3},{2,0},{3,1},{4,6},{5,7},{6,4},{7,5},{8,10},{9,11},{10,... | collective-permute-start | bytes 884744 | tf_op jit(solution)/shard_map/ppermute | solution.py:52
  216.7 14.4 %collective-permute-start.31 = (bf16[144,1024]{1,0:T(8,128)(2,1)S(1)}, bf16[144,1024]{1,0:T(8,128)(2,1)}, u32[]{:S(2)}, u32[]{:S(2)}) collective-permute-start(bf16[144,1024]{1,0:T(8,128)(2,1)S(1)} %fusion.s0), channel_id=1, source_target_pairs={{0,1},{1,0},{2,3},{3,2},{4,5},{5,4},{6,7},{7,6},{8,9},{9,8},{10,11... | collective-permute-start | bytes 884744 | tf_op jit(solution)/shard_map/ppermute | solution.py:52
  (38 other events, 196.6 us)

commit v4 on v3

--- a/solution.py
+++ b/solution.py
@@ -559,20 +559,14 @@
     return at(2 * z + ((where[0] % 2) if own else 1 - (where[0] % 2)), 128)
 
 
-def feed_weights_sent(where, hidden, grad_before, act, grad_two, theirs):
-    for k in range(4):
-        cols = core_rows(where, k, False)
-        theirs[k, 0:128] = product_left(hidden[:, cols], grad_before[...]).astype(bf16)
-        theirs[k, 128:256] = product_left(act[:, cols], grad_two[...]).astype(bf16)
-
-
 def feed_weights(where, *refs):
     hidden, grad_before, act, grad_two, w_down = refs[:5]
-    tokens, (vecs, seg_col, mine, sums, *two) = refs[5:9], refs[9:]
+    tokens, (vecs, seg_col, mine, theirs, sums, *two) = refs[5:9], refs[9:]
     for k in range(4):
-        cols = core_rows(where, k, True)
-        mine[k, 0:128] = product_left(hidden[:, cols], grad_before[...]).astype(bf16)
-        mine[k, 128:256] = product_left(act[:, cols], grad_two[...]).astype(bf16)
+        for ref, own in ((mine, True), (theirs, False)):
+            cols = core_rows(where, where[2 + k], own)
+            ref[k, 0:128] = product_left(hidden[:, cols], grad_before[...]).astype(bf16)
+            ref[k, 128:256] = product_left(act[:, cols], grad_two[...]).astype(bf16)
     valid = (column_segments(where, seg_col) >= 0).astype(f32)
     scale = jnp.zeros((1, 1024), f32)
     for k in range(4):
@@ -738,14 +732,14 @@
     return lax.all_to_all(x, "seq", split_axis=0, concat_axis=0, tiled=True)
 
 
-def share_total(where, parts, out):
-    total = sum(parts[z].astype(f32) for z in range(4)).astype(bf16)
+def share(where, received, own, out):
+    total = (received[...].astype(f32) + own[...].astype(f32)).astype(bf16)
     for m in range(4):
         out[m] = total
 
 
-def deal_total(where, x, name):
-    (copies,) = call(share_total, where, [x], [shape(x.shape, bf16)], name=name)
+def deal_sum(where, x, y, name):
+    (copies,) = call(share, where, [x, y], [shape((4,) + x.shape, bf16)], name=name)
     return deal(copies)
 
 
@@ -858,18 +852,11 @@
         scratch=[pltpu.VMEM((1024, 1024), bf16)],
     )
     partial = exchange(partial)
-    (second_theirs,) = call(
-        feed_weights_sent,
-        where,
-        [hidden_two, grad_before, act, grad_two],
-        [shape((4, 256, 1024), bf16)],
-        name="feed_weights_sent",
-    )
-    second_mine, two_sums, *two = call(
+    second_mine, second_theirs, two_sums, *two = call(
         feed_weights,
         where,
         [hidden_two, grad_before, act, grad_two, w_down] + shared + [vecs, seg_col],
-        [shape((4, 256, 1024), bf16), shape((2, 1024), f32)] + [rows_b] * 4,
+        [shape((4, 256, 1024), bf16)] * 2 + [shape((2, 1024), f32)] + [rows_b] * 4,
         name="feed_weights",
     )
     second_theirs = swap(after(second_theirs, two[0], *partial[1:]), "fsdp", 1)
@@ -882,7 +869,10 @@
         scratch=[pltpu.VMEM((128, 1024), bf16), pltpu.VMEM((128, 1024), bf16)],
     )
     got = exchange(messages)
-    second_sums = along(add(after(second_mine, messages[1]), second_theirs))
+    second_sums = pair_sums(after(second_mine, messages[1]), second_theirs)
+    second_added = add(step(second_sums[1]), after(second_sums[2], *got[1:]))
+    got = [after(got[0], second_added)] + got[1:]
+    second_total = step(second_added)
     twos = exchange([two[0]] + [after(x, *got[1:]) for x in two[1:]])
     grad_triple, one_sums, *last = call(
         attention_back,
@@ -892,7 +882,6 @@
         flops=20 * 512 * 1024 * 1024,
         name="attention_back",
     )
-    grad_triple = after(grad_triple, *twos[1:])
     first_mine, first_theirs = call(
         attention_weights,
         where,
@@ -903,23 +892,25 @@
         scratch=[pltpu.VMEM((16, 1024), f32)],
     )
     ones = exchange([last[0]] + [after(x, *twos[1:]) for x in last[1:]])
-    first_sums = pair_sums(first_mine, swap(first_theirs, "fsdp", 1))
-    first_total = step(after(first_sums[1], *ones[1:]))
+    first_sums = pair_sums(first_mine, swap(after(first_theirs, second_total, *twos[1:]), "fsdp", 1))
+    second_total = step(add(second_total, second_sums[3]))
+    first_added = after(add(step(first_sums[1]), first_sums[2]), second_total, *ones[1:])
     layer_out, tokens_grad = call(
         finish_rows,
         where,
         ones + twos + [own_middle, grad_middle, rows, vecs],
         [rows_b, rows_b],
         name="finish_rows",
+        limit=63,
     )
     grad_up, grad_down = call(
         finish_feed,
         where,
-        [deal_total(where, after(second_sums, first_total), "share_feed")],
+        [deal_sum(where, second_total, second_sums[0], "share_feed")],
         [shape((128, 4096), f32), shape((512, 1024), f32)],
         name="finish_feed",
     )
-    first_total = step(add(first_total, first_sums[2]))
+    first_total = step(first_added)
     first_total = step(after(add(first_total, first_sums[3]), layer_out))
     first_share = from_others(add(first_total, first_sums[0]))
     grad_in, grad_out, *small = call(

time: 235 us -> 221 us (0.940)
  waiting for transfers between devices: 92.7 us -> 84.6 us
  local copies, waits for them, and re-layouts: 19.4 us -> 14 us
    ppermute x28, waiting for transfers between devices: 61.1 us -> 52.2 us  [swap(): return lax.ppermute(x, axis, [(i, i ^ k) for i in range(count)])]
    ppermute x6 -> x9, waiting for transfers between devices: 13.8 us -> 19.6 us  [step(): lax.ppermute(x, 'fsdp', [(2 * a + c, 2 * b + c) for a, b in pairs for c i...]
    unnamed x96 -> x74, local copies, waits for them, and re-layouts: 18.7 us -> 13.2 us
    all_to_all x2 -> x1, starting transfers between devices: 11 us -> 6.46 us  [along(): lax.all_to_all(x, 'fsdp', split_axis=0, concat_axis=0, axis_index_groups=...]
    all_to_all x2, waiting for transfers between devices: 13.8 us -> 9.97 us  [deal(): return lax.all_to_all(x, 'seq', split_axis=0, concat_axis=0, tiled=True)]
    ppermute x6 -> x9, starting transfers between devices: 5.12 us -> 7.52 us  [step(): lax.ppermute(x, 'fsdp', [(2 * a + c, 2 * b + c) for a, b in pairs for c i...]
    convert_element_type x5 -> x7, other arithmetic: 5.18 us -> 6.63 us  [add(): return (x.astype(f32) + y.astype(f32)).astype(bf16)]
    pallas_call x15 -> x14, Pallas kernels: 65 us -> 64.9 us  [call(): pl.pallas_call(kernel, out_shape=outs, in_specs=[spec(pltpu.SMEM)] + in_s...]
  transfers between devices with their start and end apart: 38 -> 40, of which waited for: 20 -> 22; matrix products, arithmetic and copies ran while one was open for 1% -> 3% of each run, Pallas kernels for 21% -> 23%
where the time goes in v4:
time: 221 us; the launch traced here: 220 us
  waiting for transfers between devices  84.6 us (38%)
  Pallas kernels  64.9 us (29%)
  starting transfers between devices  48.5 us (22%)
  local copies, waits for them, and re-layouts  14 us (6%)
  other arithmetic  6.63 us (3%)
    pallas_call x14, Pallas kernels, call(): pl.pallas_call(kernel, out_shape=outs, in_specs=[spec(pltpu.SMEM)] + in_s...  64.9 us
    ppermute x28, waiting for transfers between devices, swap(): return lax.ppermute(x, axis, [(i, i ^ k) for i in range(count)])  52.2 us
    ppermute x28, starting transfers between devices, swap(): return lax.ppermute(x, axis, [(i, i ^ k) for i in range(count)])  25.7 us
    ppermute x9, waiting for transfers between devices, step(): lax.ppermute(x, 'fsdp', [(2 * a + c, 2 * b + c) for a, b in pairs for c i...  19.6 us
    unnamed x74, local copies, waits for them, and re-layouts  13.2 us
    all_to_all x2, waiting for transfers between devices, deal(): return lax.all_to_all(x, 'seq', split_axis=0, concat_axis=0, tiled=True)  9.97 us
    all_to_all x2, starting transfers between devices, deal(): return lax.all_to_all(x, 'seq', split_axis=0, concat_axis=0, tiled=True)  8.84 us
    ppermute x9, starting transfers between devices, step(): lax.ppermute(x, 'fsdp', [(2 * a + c, 2 * b + c) for a, b in pairs for c i...  7.52 us
  transfers between devices with their start and end apart: 40, of which 22 were waited for; matrix products, arithmetic and copies ran while one was open for 3% of the time, Pallas kernels for 23%

profile of v4, /device:TPU:0, one launch (start us, length us, event | category | flops | bytes accessed | tf_op | source)
XLA Modules:
  0.0 219.9 jit_solution(16957470731390133104)
XLA Ops:
  1.3 3.7 %prepare_first.1 = (bf16[4,144,1024]{2,1,0:T(8,128)(2,1)}, bf16[256,1024]{1,0:T(8,128)(2,1)}) custom-call(s32[6]{0:T(128)} %stack.27.where, bf16[128,3072]{1,0:T(8,128)(2,1)} %refs_0_.1, bf16[128,1024]{1,0:T(8,128)(2,1)} %refs_1_.1, bf16[128,1024]{1,0:T(8,128)(2,1)} %refs_2_.1, bf16[128,1024]{1,0:T(8,128)(2,1)} %refs_3_.1, bf16[128]{0:T(256)(128)(2,1)} %refs_4_.1, ...), custom_call_target="tpu_custom_call" | custom-call | tf_op jit(solution)/shard_map/prepare_first/pallas_call | solution.py:401
  5.0 6.5 %all-to-all-start = ((bf16[4,144,1024]{2,1,0:T(8,128)(2,1)}), bf16[4,144,1024]{2,1,0:T(8,128)(2,1)}, u32[]{:S(2)}, u32[]{:S(2)}) async-start(bf16[4,144,1024]{2,1,0:T(8,128)(2,1)} %get-tuple-element.100), calls=%async_computation | async-start | bytes 2359296 | tf_op jit(solution)/shard_map/all_to_all | solution.py:714
  11.5 2.6 %collective-permute-start.2 = (bf16[256,1024]{1,0:T(8,128)(2,1)S(1)}, bf16[256,1024]{1,0:T(8,128)(2,1)}, u32[]{:S(2)}, u32[]{:S(2)}) collective-permute-start(bf16[256,1024]{1,0:T(8,128)(2,1)S(1)} %copy-done), channel_id=1, source_target_pairs={{0,3},{1,2},{2,1},{3,0},{4,7},{5,6},{6,5},{7,4},{8,11},{9,10},{10,... | collective-permute-start | bytes 1572872 | tf_op jit(solution)/shard_map/ppermute | solution.py:52
  15.0 2.7 %prepare_second.1.refs_1_ = bf16[256,1024]{1,0:T(8,128)(2,1)} custom-call(s32[6]{0:T(128)} %stack.27.where, bf16[128,4096]{1,0:T(8,128)(2,1)} %w_up.1, bf16[512,1024]{1,0:T(8,128)(2,1)} %w_down.1), custom_call_target="tpu_custom_call" | custom-call | tf_op jit(solution)/shard_map/prepare_second/pallas_call | solution.py:401
  17.8 9.6 %collective-permute-done.2.t3.refs_12_.refs_8_ = bf16[256,1024]{1,0:T(8,128)(2,1)} collective-permute-done((bf16[256,1024]{1,0:T(8,128)(2,1)S(1)}, bf16[256,1024]{1,0:T(8,128)(2,1)}, u32[]{:S(2)}, u32[]{:S(2)}) %collective-permute-start.2) | collective-permute-done | bytes 524320 | tf_op jit(solution)/shard_map/ppermute | solution.py:52
  27.4 9.7 %collective-permute-done.1.t2.refs_11_.refs_7_ = bf16[256,1024]{1,0:T(8,128)(2,1)} collective-permute-done((bf16[256,1024]{1,0:T(8,128)(2,1)S(1)}, bf16[256,1024]{1,0:T(8,128)(2,1)}, u32[]{:S(2)}, u32[]{:S(2)}) %collective-permute-start.1) | collective-permute-done | bytes 524320 | tf_op jit(solution)/shard_map/ppermute | solution.py:52
  37.2 2.9 %all-to-all-done.own = bf16[4,144,1024]{2,1,0:T(8,128)(2,1)} async-done(((bf16[4,144,1024]{2,1,0:T(8,128)(2,1)}), bf16[4,144,1024]{2,1,0:T(8,128)(2,1)}, u32[]{:S(2)}, u32[]{:S(2)}) %all-to-all-start) | async-done | bytes 1179680 | tf_op jit(solution)/shard_map/all_to_all | solution.py:714
  40.3 3.0 %collective-permute-done.3.other = bf16[4,144,1024]{2,1,0:T(8,128)(2,1)} collective-permute-done((bf16[4,144,1024]{2,1,0:T(8,128)(2,1)}, bf16[4,144,1024]{2,1,0:T(8,128)(2,1)}, u32[]{:S(2)}, u32[]{:S(2)}) %collective-permute-start.3) | collective-permute-done | bytes 1179680 | tf_op jit(solution)/shard_map/ppermute | solution.py:52
  43.3 3.1 %place_first.1 = (bf16[1024,768]{1,0:T(8,128)(2,1)}, bf16[1024,256]{1,0:T(8,128)(2,1)}, f32[16,1024]{1,0:T(8,128)}) custom-call(s32[6]{0:T(128)} %stack.27.where, bf16[4,144,1024]{2,1,0:T(8,128)(2,1)} %all-to-all-done.own, bf16[4,144,1024]{2,1,0:T(8,128)(2,1)} %collective-permute-done.3.other), custom_call_target="tpu_custom_call" | custom-call | tf_op jit(solution)/shard_map/place_first/pallas_call | solution.py:401
  46.4 2.6 %collective-permute-start.6 = (bf16[1024,256]{1,0:T(8,128)(2,1)}, bf16[1024,256]{1,0:T(8,128)(2,1)S(1)}, u32[]{:S(2)}, u32[]{:S(2)}) collective-permute-start(bf16[1024,256]{1,0:T(8,128)(2,1)} %get-tuple-element.107.w0), channel_id=1, source_target_pairs={{0,3},{1,2},{2,1},{3,0},{4,7},{5,6},{6,5},{7,4},{8,11},{9,10},{10,... | collective-permute-start | bytes 1572872 | tf_op jit(solution)/shard_map/ppermute | solution.py:52
  50.8 6.9 %attention.1 = (bf16[512,768]{1,0:T(8,128)(2,1)S(1)}, bf16[4,512,256]{2,1,0:T(8,128)(2,1)}, f32[512,128]{1,0:T(8,128)S(1)}, bf16[512,1024]{1,0:T(8,128)(2,1)}) custom-call(s32[6]{0:T(128)S(1)} %copy-done.22, bf16[256,1024]{1,0:T(8,128)(2,1)S(1)} %copy-done, bf16[256,1024]{1,0:T(8,128)(2,1)} %collective-permute-done.t1.refs_10_.refs_6_, ...), custom_call_target="tpu_custom_call" | custom-call | tf_op jit(solution)/shard_map/attention/pallas_call | solution.py:401
  59.2 4.4 %all-to-all-start.1 = ((bf16[4,512,256]{2,1,0:T(8,128)(2,1)}), bf16[4,512,256]{2,1,0:T(8,128)(2,1)}, u32[]{:S(2)}, u32[]{:S(2)}) async-start(bf16[4,512,256]{2,1,0:T(8,128)(2,1)} %get-tuple-element.106), calls=%async_computation.1 | async-start | bytes 2097152 | tf_op jit(solution)/shard_map/all_to_all | solution.py:732
  64.4 9.2 %collective-permute-done.5.w2 = bf16[1024,256]{1,0:T(8,128)(2,1)S(1)} collective-permute-done((bf16[1024,256]{1,0:T(8,128)(2,1)}, bf16[1024,256]{1,0:T(8,128)(2,1)S(1)}, u32[]{:S(2)}, u32[]{:S(2)}) %collective-permute-start.5) | collective-permute-done | bytes 524320 | tf_op jit(solution)/shard_map/ppermute | solution.py:52
  75.3 8.9 %all-to-all-done.1.sent = bf16[4,512,256]{2,1,0:T(8,128)(2,1)} async-done(((bf16[4,512,256]{2,1,0:T(8,128)(2,1)}), bf16[4,512,256]{2,1,0:T(8,128)(2,1)}, u32[]{:S(2)}, u32[]{:S(2)}) %all-to-all-start.1) | async-done | bytes 1048608 | tf_op jit(solution)/shard_map/all_to_all | solution.py:732
  88.9 5.2 %project.1 = (bf16[512,1024]{1,0:T(8,128)(2,1)}, bf16[512,1024]{1,0:T(8,128)(2,1)}, f32[128,1024]{1,0:T(8,128)S(1)}, f32[128,1024]{1,0:T(8,128)S(1)}) custom-call(s32[6]{0:T(128)S(1)} %copy-done.22, bf16[4,512,256]{2,1,0:T(8,128)(2,1)} %all-to-all-done.1.sent, bf16[1024,256]{1,0:T(8,128)(2,1)S(1)} %copy-done.6, bf16[1024,256]{1,0:T(8,128)(2,1)S(1)} %copy-done.12, ...), custom_call_target="tpu_custom_call" | custom-call | tf_op jit(solution)/shard_map/project/pallas_call | solution.py:401
  94.7 1.5 collective-permute-done.13.refs_8_
  97.0 9.0 %feed.1 = (bf16[1024,1024]{1,0:T(8,128)(2,1)}, bf16[512,1024]{1,0:T(8,128)(2,1)}, bf16[512,1024]{1,0:T(8,128)(2,1)}, bf16[512,1024]{1,0:T(8,128)(2,1)}, f32[1,10...) custom-call(s32[6]{0:T(128)S(1)} %copy-done.22, ...), custom_call_target="tpu_custom_call" | custom-call | tf_op jit(solution)/shard_map/feed/pallas_call | solution.py:401
  106.0 1.5 collective-permute-start.14
  107.5 1.6 collective-permute-start.15
  109.5 7.9 %feed_weights.1 = (bf16[4,256,1024]{2,1,0:T(8,128)(2,1)}, bf16[4,256,1024]{2,1,0:T(8,128)(2,1)}, f32[2,1024]{1,0:T(2,128)S(1)}, bf16[128,1024]{1,0:T(8,128)(2,1)...) custom-call(s32[6]{0:T(128)S(1)} %copy-done.22, ...), custom_call_target="tpu_custom_call" | custom-call | tf_op jit(solution)/shard_map/feed_weights/pallas_call | solution.py:401
  118.1 3.3 %collective-permute-done.15.p2 = bf16[128,1024]{1,0:T(8,128)(2,1)S(1)} collective-permute-done((bf16[128,1024]{1,0:T(8,128)(2,1)S(1)}, bf16[128,1024]{1,0:T(8,128)(2,1)S(1)}, u32[]{:S(2)}, u32[]{:S(2)}) %collective-permute-start.15) | collective-permute-done | bytes 262176 | tf_op jit(solution)/shard_map/ppermute | solution.py:52
  121.4 3.6 %middle_back.1 = (f32[128,1024]{1,0:T(8,128)S(1)}, f32[4,1024]{1,0:T(4,128)S(1)}, bf16[256,256]{1,0:T(8,128)(2,1)S(1)}, bf16[256,256]{1,0:T(8,128)(2,1)S(1)}, bf...) custom-call(s32[6]{0:T(128)S(1)} %copy-done.22, f32[128,1024]{1,0:T(8,128)S(1)} %get-tuple-element.116.p0, ...), custom_call_target="tpu_custom_call" | custom-call | tf_op jit(solution)/shard_map/middle_back/pallas_call | solution.py:401
  126.5 1.7 collective-permute-start.20
  130.1 4.3 %collective-permute-done.20.m2 = bf16[256,256]{1,0:T(8,128)(2,1)S(1)} collective-permute-done((bf16[256,256]{1,0:T(8,128)(2,1)S(1)}, bf16[256,256]{1,0:T(8,128)(2,1)S(1)}, u32[]{:S(2)}, u32[]{:S(2)}) %collective-permute-start.20) | collective-permute-done | bytes 131104 | tf_op jit(solution)/shard_map/ppermute | solution.py:52
  136.2 4.3 %collective-permute-done.18 = bf16[256,1024]{1,0:T(8,128)(2,1)S(1)} collective-permute-done((bf16[256,1024]{1,0:T(8,128)(2,1)S(1)}, bf16[256,1024]{1,0:T(8,128)(2,1)S(1)}, u32[]{:S(2)}, u32[]{:S(2)}) %collective-permute-start.18) | collective-permute-done | bytes 524320 | tf_op jit(solution)/shard_map/ppermute | solution.py:708
  140.7 1.2 collective-permute-start.28
  141.9 1.3 collective-permute-start.22
  143.9 1.5 collective-permute-start.24
  145.4 8.2 %attention_back.1 = (bf16[512,768]{1,0:T(8,128)(2,1)}, f32[4,1024]{1,0:T(4,128)S(1)}, bf16[128,1024]{1,0:T(8,128)(2,1)S(1)}, bf16[128,1024]{1,0:T(8,128)(2,1)S(1...) custom-call(s32[6]{0:T(128)S(1)} %copy-done.22, bf16[512,768]{1,0:T(8,128)(2,1)} %copy-done.16, ...), custom_call_target="tpu_custom_call" | custom-call | tf_op jit(solution)/shard_map/attention_back/pallas_call | solution.py:401
  154.9 3.3 %attention_weights.1 = (bf16[4,144,1024]{2,1,0:T(8,128)(2,1)}, bf16[4,144,1024]{2,1,0:T(8,128)(2,1)}) custom-call(s32[6]{0:T(128)S(1)} %copy-done.22, bf16[512,1024]{1,0:T(8,128)(2,1)S(1)} %copy-done.13, bf16[512,768]{1,0:T(8,128)(2,1)S(1)} %copy-done.15, bf16[512,1024]{1,0:T(8,128)(2,1)S(1)} %copy-done.14, bf16[256,256]{1,0:T(8,128)(2,1)S(1)} %get-tuple-element.136.m0, ...), custom_call_target="tpu_custom_call" | custom-call | tf_op jit(solution)/shard_map/attention_weights/pallas_call | solution.py:401
  160.1 1.9 collective-permute-done.29
  162.0 1.2 fusion.8
  164.1 1.4 collective-permute-start.27
  165.5 1.4 collective-permute-start.26
  167.6 6.4 %collective-permute-done.31.received = bf16[256,1024]{1,0:T(8,128)(2,1)S(1)} collective-permute-done((bf16[256,1024]{1,0:T(8,128)(2,1)S(1)}, bf16[256,1024]{1,0:T(8,128)(2,1)S(1)}, u32[]{:S(2)}, u32[]{:S(2)}) %collective-permute-start.31) | collective-permute-done | bytes 524320 | tf_op jit(solution)/shard_map/ppermute | solution.py:708
  174.0 2.0 share_feed.1
  176.0 4.4 %all-to-all-start.2 = ((bf16[4,256,1024]{2,1,0:T(8,128)(2,1)}), bf16[4,256,1024]{2,1,0:T(8,128)(2,1)}, u32[]{:S(2)}, u32[]{:S(2)}) async-start(bf16[4,256,1024]{2,1,0:T(8,128)(2,1)} %share_feed.1), calls=%async_computation.2 | async-start | bytes 4194304 | tf_op jit(solution)/shard_map/all_to_all | solution.py:732
  180.5 1.9 fusion.3
  183.1 1.7 collective-permute-start.32
  184.8 3.5 %finish_rows.1 = (bf16[128,1024]{1,0:T(8,128)(2,1)}, bf16[128,1024]{1,0:T(8,128)(2,1)}) custom-call(s32[6]{0:T(128)} %stack.27.where, bf16[128,1024]{1,0:T(8,128)(2,1)} %copy-done.19, bf16[128,1024]{1,0:T(8,128)(2,1)} %copy-done.36, bf16[128,1024]{1,0:T(8,128)(2,1)} %copy-done.35, bf16[128,1024]{1,0:T(8,128)(2,1)} %copy-done.34, ...), custom_call_target="tpu_custom_call" | custom-call | tf_op jit(solution)/shard_map/finish_rows/pallas_call | solution.py:401
  188.4 3.2 %collective-permute-done.32 = bf16[144,1024]{1,0:T(8,128)(2,1)S(1)} collective-permute-done((bf16[144,1024]{1,0:T(8,128)(2,1)}, bf16[144,1024]{1,0:T(8,128)(2,1)S(1)}, u32[]{:S(2)}, u32[]{:S(2)}) %collective-permute-start.32) | collective-permute-done | bytes 294944 | tf_op jit(solution)/shard_map/ppermute | solution.py:708
  192.8 2.7 %collective-permute-start.33 = (bf16[144,1024]{1,0:T(8,128)(2,1)S(1)}, bf16[144,1024]{1,0:T(8,128)(2,1)S(1)}, u32[]{:S(2)}, u32[]{:S(2)}) collective-permute-start(bf16[144,1024]{1,0:T(8,128)(2,1)S(1)} %fusion.2), channel_id=1, source_target_pairs={{0,16},{4,20},{16,24},{20,28},{24,8},{28,12},{8,0},{12,4},{1,17},{... | collective-permute-start | bytes 884744 | tf_op jit(solution)/shard_map/ppermute | solution.py:708
  195.5 5.7 %collective-permute-done.33 = bf16[144,1024]{1,0:T(8,128)(2,1)S(1)} collective-permute-done((bf16[144,1024]{1,0:T(8,128)(2,1)S(1)}, bf16[144,1024]{1,0:T(8,128)(2,1)S(1)}, u32[]{:S(2)}, u32[]{:S(2)}) %collective-permute-start.33) | collective-permute-done | bytes 294944 | tf_op jit(solution)/shard_map/ppermute | solution.py:708
  202.3 2.3 %collective-permute-start.36 = (bf16[144,1024]{1,0:T(8,128)(2,1)S(1)}, bf16[144,1024]{1,0:T(8,128)(2,1)S(1)}, u32[]{:S(2)}, u32[]{:S(2)}) collective-permute-start(bf16[144,1024]{1,0:T(8,128)(2,1)S(1)} %fusion.1.s0), channel_id=1, source_target_pairs={{0,3},{1,2},{2,1},{3,0},{4,7},{5,6},{6,5},{7,4},{8,11},{9,10},{10,... | collective-permute-start | bytes 884744 | tf_op jit(solution)/shard_map/ppermute | solution.py:52
  206.9 3.9 %finish_feed.1 = (f32[128,4096]{1,0:T(8,128)}, f32[512,1024]{1,0:T(8,128)}) custom-call(s32[6]{0:T(128)S(1)} %copy-done.23, bf16[4,256,1024]{2,1,0:T(8,128)(2,1)} %all-to-all-done.2.got), custom_call_target="tpu_custom_call" | custom-call | tf_op jit(solution)/shard_map/finish_feed/pallas_call | solution.py:401
  210.9 3.1 %collective-permute-done.36.s3 = bf16[144,1024]{1,0:T(8,128)(2,1)S(1)} collective-permute-done((bf16[144,1024]{1,0:T(8,128)(2,1)S(1)}, bf16[144,1024]{1,0:T(8,128)(2,1)S(1)}, u32[]{:S(2)}, u32[]{:S(2)}) %collective-permute-start.36) | collective-permute-done | bytes 294944 | tf_op jit(solution)/shard_map/ppermute | solution.py:52
  214.0 3.7 %collective-permute-done.35.s2 = bf16[144,1024]{1,0:T(8,128)(2,1)S(1)} collective-permute-done((bf16[144,1024]{1,0:T(8,128)(2,1)S(1)}, bf16[144,1024]{1,0:T(8,128)(2,1)S(1)}, u32[]{:S(2)}, u32[]{:S(2)}) %collective-permute-start.35) | collective-permute-done | bytes 294944 | tf_op jit(solution)/shard_map/ppermute | solution.py:52
  217.7 1.9 finish_attention.1
  (129 shorter events, 30.9 us)
Async XLA Ops:
  5.0 35.1 %all-to-all-start = ((bf16[4,144,1024]{2,1,0:T(8,128)(2,1)}), bf16[4,144,1024]{2,1,0:T(8,128)(2,1)}, u32[]{:S(2)}, u32[]{:S(2)}) async-start(bf16[4,144,1024]{2,1,0:T(8,128)(2,1)} %get-tuple-element.100), calls=%async_computation | async-start | bytes 2359296 | tf_op jit(solution)/shard_map/all_to_all | solution.py:714
  11.5 28.6 %copy-start.24 = (s32[512]{0:T(512)S(1)}, s32[512]{0:T(512)}, u32[]{:S(2)}) copy-start(s32[512]{0:T(512)} %param.19) | copy-start | bytes 6148
  11.5 15.9 %collective-permute-start.2 = (bf16[256,1024]{1,0:T(8,128)(2,1)S(1)}, bf16[256,1024]{1,0:T(8,128)(2,1)}, u32[]{:S(2)}, u32[]{:S(2)}) collective-permute-start(bf16[256,1024]{1,0:T(8,128)(2,1)S(1)} %copy-done), channel_id=1, source_target_pairs={{0,3},{1,2},{2,1},{3,0},{4,7},{5,6},{6,5},{7,4},{8,11},{9,10},{10,... | collective-permute-start | bytes 1572872 | tf_op jit(solution)/shard_map/ppermute | solution.py:52
  14.1 23.0 %collective-permute-start.1 = (bf16[256,1024]{1,0:T(8,128)(2,1)S(1)}, bf16[256,1024]{1,0:T(8,128)(2,1)}, u32[]{:S(2)}, u32[]{:S(2)}) collective-permute-start(bf16[256,1024]{1,0:T(8,128)(2,1)S(1)} %copy-done), channel_id=1, source_target_pairs={{0,2},{1,3},{2,0},{3,1},{4,6},{5,7},{6,4},{7,5},{8,10},{9,11},{10,... | collective-permute-start | bytes 1572872 | tf_op jit(solution)/shard_map/ppermute | solution.py:52
  14.5 22.7 %collective-permute-start = (bf16[256,1024]{1,0:T(8,128)(2,1)S(1)}, bf16[256,1024]{1,0:T(8,128)(2,1)}, u32[]{:S(2)}, u32[]{:S(2)}) collective-permute-start(bf16[256,1024]{1,0:T(8,128)(2,1)S(1)} %copy-done), channel_id=1, source_target_pairs={{0,1},{1,0},{2,3},{3,2},{4,5},{5,4},{6,7},{7,6},{8,9},{9,8},{10,11... | collective-permute-start | bytes 1572872 | tf_op jit(solution)/shard_map/ppermute | solution.py:52
  17.7 32.2 %copy-start.22 = (s32[6]{0:T(128)S(1)}, s32[6]{0:T(128)}, u32[]{:S(2)}) copy-start(s32[6]{0:T(128)} %stack.27.where) | copy-start | bytes 76
  40.1 3.2 %collective-permute-start.3 = (bf16[4,144,1024]{2,1,0:T(8,128)(2,1)}, bf16[4,144,1024]{2,1,0:T(8,128)(2,1)}, u32[]{:S(2)}, u32[]{:S(2)}) collective-permute-start(bf16[4,144,1024]{2,1,0:T(8,128)(2,1)} %all-to-all-done.own), channel_id=1, source_target_pairs={{0,4},{4,0},{8,12},{12,8},{16,20},{20,16},{24,28},{28,24},{1,5},{5... | collective-permute-start | bytes 3538952 | tf_op jit(solution)/shard_map/ppermute | solution.py:52
  40.1 19.1 %collective-permute-start.8 = (bf16[256,1024]{1,0:T(8,128)(2,1)}, bf16[256,1024]{1,0:T(8,128)(2,1)}, u32[]{:S(2)}, u32[]{:S(2)}) collective-permute-start(bf16[256,1024]{1,0:T(8,128)(2,1)} %prepare_second.1.refs_1_), channel_id=1, source_target_pairs={{0,16},{4,20},{16,24},{20,28},{24,8},{28,12},{8,0},{12,4},{1,17},{... | collective-permute-start | bytes 1572872 | tf_op jit(solution)/shard_map/ppermute | solution.py:708
  46.4 17.2 %collective-permute-start.6 = (bf16[1024,256]{1,0:T(8,128)(2,1)}, bf16[1024,256]{1,0:T(8,128)(2,1)S(1)}, u32[]{:S(2)}, u32[]{:S(2)}) collective-permute-start(bf16[1024,256]{1,0:T(8,128)(2,1)} %get-tuple-element.107.w0), channel_id=1, source_target_pairs={{0,3},{1,2},{2,1},{3,0},{4,7},{5,6},{6,5},{7,4},{8,11},{9,10},{10,... | collective-permute-start | bytes 1572872 | tf_op jit(solution)/shard_map/ppermute | solution.py:52
  49.0 24.6 %collective-permute-start.5 = (bf16[1024,256]{1,0:T(8,128)(2,1)}, bf16[1024,256]{1,0:T(8,128)(2,1)S(1)}, u32[]{:S(2)}, u32[]{:S(2)}) collective-permute-start(bf16[1024,256]{1,0:T(8,128)(2,1)} %get-tuple-element.107.w0), channel_id=1, source_target_pairs={{0,2},{1,3},{2,0},{3,1},{4,6},{5,7},{6,4},{7,5},{8,10},{9,11},{10,... | collective-permute-start | bytes 1572872 | tf_op jit(solution)/shard_map/ppermute | solution.py:52
  49.4 25.0 %collective-permute-start.4 = (bf16[1024,256]{1,0:T(8,128)(2,1)}, bf16[1024,256]{1,0:T(8,128)(2,1)S(1)}, u32[]{:S(2)}, u32[]{:S(2)}) collective-permute-start(bf16[1024,256]{1,0:T(8,128)(2,1)} %get-tuple-element.107.w0), channel_id=1, source_target_pairs={{0,1},{1,0},{2,3},{3,2},{4,5},{5,4},{6,7},{7,6},{8,9},{9,8},{10,11... | collective-permute-start | bytes 1572872 | tf_op jit(solution)/shard_map/ppermute | solution.py:52
  59.2 25.5 %copy-start.4 = (f32[16,1024]{1,0:T(8,128)S(1)}, f32[16,1024]{1,0:T(8,128)}, u32[]{:S(2)}) copy-start(f32[16,1024]{1,0:T(8,128)} %get-tuple-element.103.vecs.refs_13_.refs_9_.refs_11_) | copy-start | bytes 196612
  59.2 16.1 %collective-permute-start.10 = (bf16[256,1024]{1,0:T(8,128)(2,1)}, bf16[256,1024]{1,0:T(8,128)(2,1)S(1)}, u32[]{:S(2)}, u32[]{:S(2)}) collective-permute-start(bf16[256,1024]{1,0:T(8,128)(2,1)} %collective-permute-done.8.refs_3_), channel_id=1, source_target_pairs={{0,16},{4,20},{16,24},{20,28},{24,8},{28,12},{8,0},{12,4},{1,17},{... | collective-permute-start | bytes 1572872 | tf_op jit(solution)/shard_map/ppermute | solution.py:708
  59.2 25.0 %all-to-all-start.1 = ((bf16[4,512,256]{2,1,0:T(8,128)(2,1)}), bf16[4,512,256]{2,1,0:T(8,128)(2,1)}, u32[]{:S(2)}, u32[]{:S(2)}) async-start(bf16[4,512,256]{2,1,0:T(8,128)(2,1)} %get-tuple-element.106), calls=%async_computation.1 | async-start | bytes 2097152 | tf_op jit(solution)/shard_map/all_to_all | solution.py:732
  75.3 18.8 %copy-start.27 = (bf16[256,1024]{1,0:T(8,128)(2,1)}, bf16[256,1024]{1,0:T(8,128)(2,1)S(1)}, u32[]{:S(2)}) copy-start(bf16[256,1024]{1,0:T(8,128)(2,1)S(1)} %collective-permute-done.10.refs_5_) | copy-start | bytes 1572868
  75.3 18.8 %collective-permute-start.12 = (bf16[256,1024]{1,0:T(8,128)(2,1)S(1)}, bf16[256,1024]{1,0:T(8,128)(2,1)S(1)}, u32[]{:S(2)}, u32[]{:S(2)}) collective-permute-start(bf16[256,1024]{1,0:T(8,128)(2,1)S(1)} %collective-permute-done.10.refs_5_), channel_id=1, source_target_pairs={{0,16},{4,20},{16,24},{20,28},{24,8},{28,12},{8,0},{12,4},{1,17},{... | collective-permute-start | bytes 1572872 | tf_op jit(solution)/shard_map/ppermute | solution.py:708
  84.2 10.5 %collective-permute-start.7 = (bf16[256,1024]{1,0:T(8,128)(2,1)}, bf16[256,1024]{1,0:T(8,128)(2,1)S(1)}, u32[]{:S(2)}, u32[]{:S(2)}) collective-permute-start(bf16[256,1024]{1,0:T(8,128)(2,1)} %prepare_second.1.refs_1_), channel_id=1, source_target_pairs={{0,4},{4,0},{8,12},{12,8},{16,20},{20,16},{24,28},{28,24},{1,5},{5... | collective-permute-start | bytes 1572872 | tf_op jit(solution)/shard_map/ppermute | solution.py:52
  84.2 10.5 %collective-permute-start.9 = (bf16[256,1024]{1,0:T(8,128)(2,1)}, bf16[256,1024]{1,0:T(8,128)(2,1)S(1)}, u32[]{:S(2)}, u32[]{:S(2)}) collective-permute-start(bf16[256,1024]{1,0:T(8,128)(2,1)} %collective-permute-done.8.refs_3_), channel_id=1, source_target_pairs={{0,4},{4,0},{8,12},{12,8},{16,20},{20,16},{24,28},{28,24},{1,5},{5... | collective-permute-start | bytes 1572872 | tf_op jit(solution)/shard_map/ppermute | solution.py:52
  84.7 10.0 %collective-permute-start.11 = (bf16[256,1024]{1,0:T(8,128)(2,1)S(1)}, bf16[256,1024]{1,0:T(8,128)(2,1)S(1)}, u32[]{:S(2)}, u32[]{:S(2)}) collective-permute-start(bf16[256,1024]{1,0:T(8,128)(2,1)S(1)} %collective-permute-done.10.refs_5_), channel_id=1, source_target_pairs={{0,4},{4,0},{8,12},{12,8},{16,20},{20,16},{24,28},{28,24},{1,5},{5... | collective-permute-start | bytes 1572872 | tf_op jit(solution)/shard_map/ppermute | solution.py:52
  94.1 27.3 %copy-start.5 = (f32[128,1024]{1,0:T(8,128)}, f32[128,1024]{1,0:T(8,128)S(1)}, u32[]{:S(2)}) copy-start(f32[128,1024]{1,0:T(8,128)S(1)} %get-tuple-element.120.own_middle.refs_8_) | copy-start | bytes 1572868
  94.1 2.1 collective-permute-start.13
  106.0 12.1 %collective-permute-start.14 = (bf16[128,1024]{1,0:T(8,128)(2,1)S(1)}, bf16[128,1024]{1,0:T(8,128)(2,1)S(1)}, u32[]{:S(2)}, u32[]{:S(2)}) collective-permute-start(bf16[128,1024]{1,0:T(8,128)(2,1)S(1)} %get-tuple-element.117), channel_id=1, source_target_pairs={{0,1},{1,0},{2,3},{3,2},{4,5},{5,4},{6,7},{7,6},{8,9},{9,8},{10,11... | collective-permute-start | bytes 786440 | tf_op jit(solution)/shard_map/ppermute | solution.py:52
  107.5 13.9 %collective-permute-start.15 = (bf16[128,1024]{1,0:T(8,128)(2,1)S(1)}, bf16[128,1024]{1,0:T(8,128)(2,1)S(1)}, u32[]{:S(2)}, u32[]{:S(2)}) collective-permute-start(bf16[128,1024]{1,0:T(8,128)(2,1)S(1)} %get-tuple-element.118), channel_id=1, source_target_pairs={{0,2},{1,3},{2,0},{3,1},{4,6},{5,7},{6,4},{7,5},{8,10},{9,11},{10,... | collective-permute-start | bytes 786440 | tf_op jit(solution)/shard_map/ppermute | solution.py:52
  109.1 12.3 %collective-permute-start.16 = (bf16[128,1024]{1,0:T(8,128)(2,1)S(1)}, bf16[128,1024]{1,0:T(8,128)(2,1)S(1)}, u32[]{:S(2)}, u32[]{:S(2)}) collective-permute-start(bf16[128,1024]{1,0:T(8,128)(2,1)S(1)} %get-tuple-element.119), channel_id=1, source_target_pairs={{0,3},{1,2},{2,1},{3,0},{4,7},{5,6},{6,5},{7,4},{8,11},{9,10},{10,... | collective-permute-start | bytes 786440 | tf_op jit(solution)/shard_map/ppermute | solution.py:52
  121.4 4.4 %collective-permute-start.17 = (bf16[4,256,1024]{2,1,0:T(8,128)(2,1)}, bf16[4,256,1024]{2,1,0:T(8,128)(2,1)S(1)}, u32[]{:S(2)}, u32[]{:S(2)}) collective-permute-start(bf16[4,256,1024]{2,1,0:T(8,128)(2,1)} %get-tuple-element.132), channel_id=1, source_target_pairs={{0,4},{4,0},{8,12},{12,8},{16,20},{20,16},{24,28},{28,24},{1,5},{5... | collective-permute-start | bytes 6291464 | tf_op jit(solution)/shard_map/ppermute | solution.py:52
  126.5 19.0 %copy-start.2 = (bf16[256,1024]{1,0:T(8,128)(2,1)S(1)}, bf16[256,1024]{1,0:T(8,128)(2,1)}, u32[]{:S(2)}) copy-start(bf16[256,1024]{1,0:T(8,128)(2,1)} %get-tuple-element.99.t0.refs_9_.tokens.refs_5_.refs_10_) | copy-start | bytes 1572868
  126.5 19.0 %copy-start.21 = (f32[512,128]{1,0:T(8,128)S(1)}, f32[512,128]{1,0:T(8,128)}, u32[]{:S(2)}) copy-start(f32[512,128]{1,0:T(8,128)} %copy-done.20) | copy-start | bytes 786436
  126.5 14.0 %collective-permute-start.18 = (bf16[256,1024]{1,0:T(8,128)(2,1)S(1)}, bf16[256,1024]{1,0:T(8,128)(2,1)S(1)}, u32[]{:S(2)}, u32[]{:S(2)}) collective-permute-start(bf16[256,1024]{1,0:T(8,128)(2,1)S(1)} %get-tuple-element.183), channel_id=1, source_target_pairs={{0,16},{4,20},{16,24},{20,28},{24,8},{28,12},{8,0},{12,4},{1,17},{... | collective-permute-start | bytes 1572872 | tf_op jit(solution)/shard_map/ppermute | solution.py:708
  126.5 7.9 %collective-permute-start.20 = (bf16[256,256]{1,0:T(8,128)(2,1)S(1)}, bf16[256,256]{1,0:T(8,128)(2,1)S(1)}, u32[]{:S(2)}, u32[]{:S(2)}) collective-permute-start(bf16[256,256]{1,0:T(8,128)(2,1)S(1)} %get-tuple-element.133), channel_id=1, source_target_pairs={{0,2},{1,3},{2,0},{3,1},{4,6},{5,7},{6,4},{7,5},{8,10},{9,11},{10,... | collective-permute-start | bytes 393224 | tf_op jit(solution)/shard_map/ppermute | solution.py:52
  128.2 7.3 %collective-permute-start.21 = (bf16[256,256]{1,0:T(8,128)(2,1)S(1)}, bf16[256,256]{1,0:T(8,128)(2,1)S(1)}, u32[]{:S(2)}, u32[]{:S(2)}) collective-permute-start(bf16[256,256]{1,0:T(8,128)(2,1)S(1)} %get-tuple-element.134), channel_id=1, source_target_pairs={{0,3},{1,2},{2,1},{3,0},{4,7},{5,6},{6,5},{7,4},{8,11},{9,10},{10,... | collective-permute-start | bytes 393224 | tf_op jit(solution)/shard_map/ppermute | solution.py:52
  129.4 6.8 %collective-permute-start.19 = (bf16[256,256]{1,0:T(8,128)(2,1)S(1)}, bf16[256,256]{1,0:T(8,128)(2,1)S(1)}, u32[]{:S(2)}, u32[]{:S(2)}) collective-permute-start(bf16[256,256]{1,0:T(8,128)(2,1)S(1)} %get-tuple-element.128), channel_id=1, source_target_pairs={{0,1},{1,0},{2,3},{3,2},{4,5},{5,4},{6,7},{7,6},{8,9},{9,8},{10,11... | collective-permute-start | bytes 393224 | tf_op jit(solution)/shard_map/ppermute | solution.py:52
  140.7 17.5 %collective-permute-start.28 = (bf16[256,1024]{1,0:T(8,128)(2,1)S(1)}, bf16[256,1024]{1,0:T(8,128)(2,1)S(1)}, u32[]{:S(2)}, u32[]{:S(2)}) collective-permute-start(bf16[256,1024]{1,0:T(8,128)(2,1)S(1)} %add_convert_fusion.2), channel_id=1, source_target_pairs={{0,16},{4,20},{16,24},{20,28},{24,8},{28,12},{8,0},{12,4},{1,17},{... | collective-permute-start | bytes 1572872 | tf_op jit(solution)/shard_map/ppermute | solution.py:708
  141.9 16.2 %collective-permute-start.22 = (bf16[128,1024]{1,0:T(8,128)(2,1)S(1)}, bf16[128,1024]{1,0:T(8,128)(2,1)S(1)}, u32[]{:S(2)}, u32[]{:S(2)}) collective-permute-start(bf16[128,1024]{1,0:T(8,128)(2,1)S(1)} %get-tuple-element.140), channel_id=1, source_target_pairs={{0,1},{1,0},{2,3},{3,2},{4,5},{5,4},{6,7},{7,6},{8,9},{9,8},{10,11... | collective-permute-start | bytes 786440 | tf_op jit(solution)/shard_map/ppermute | solution.py:52
  143.3 14.9 %collective-permute-start.23 = (bf16[128,1024]{1,0:T(8,128)(2,1)S(1)}, bf16[128,1024]{1,0:T(8,128)(2,1)S(1)}, u32[]{:S(2)}, u32[]{:S(2)}) collective-permute-start(bf16[128,1024]{1,0:T(8,128)(2,1)S(1)} %get-tuple-element.142), channel_id=1, source_target_pairs={{0,2},{1,3},{2,0},{3,1},{4,6},{5,7},{6,4},{7,5},{8,10},{9,11},{10,... | collective-permute-start | bytes 786440 | tf_op jit(solution)/shard_map/ppermute | solution.py:52
  143.9 14.3 %collective-permute-start.24 = (bf16[128,1024]{1,0:T(8,128)(2,1)S(1)}, bf16[128,1024]{1,0:T(8,128)(2,1)S(1)}, u32[]{:S(2)}, u32[]{:S(2)}) collective-permute-start(bf16[128,1024]{1,0:T(8,128)(2,1)S(1)} %get-tuple-element.144), channel_id=1, source_target_pairs={{0,3},{1,2},{2,1},{3,0},{4,7},{5,6},{6,5},{7,4},{8,11},{9,10},{10,... | collective-permute-start | bytes 786440 | tf_op jit(solution)/shard_map/ppermute | solution.py:52
  158.9 3.1 %collective-permute-start.29 = (bf16[4,144,1024]{2,1,0:T(8,128)(2,1)}, bf16[4,144,1024]{2,1,0:T(8,128)(2,1)S(1)}, u32[]{:S(2)}, u32[]{:S(2)}) collective-permute-start(bf16[4,144,1024]{2,1,0:T(8,128)(2,1)} %get-tuple-element.162), channel_id=1, source_target_pairs={{0,4},{4,0},{8,12},{12,8},{16,20},{20,16},{24,28},{28,24},{1,5},{5... | collective-permute-start | bytes 3538952 | tf_op jit(solution)/shard_map/ppermute | solution.py:52
  159.2 14.8 %collective-permute-start.31 = (bf16[256,1024]{1,0:T(8,128)(2,1)S(1)}, bf16[256,1024]{1,0:T(8,128)(2,1)S(1)}, u32[]{:S(2)}, u32[]{:S(2)}) collective-permute-start(bf16[256,1024]{1,0:T(8,128)(2,1)S(1)} %fusion), channel_id=1, source_target_pairs={{0,16},{4,20},{16,24},{20,28},{24,8},{28,12},{8,0},{12,4},{1,17},{... | collective-permute-start | bytes 1572872 | tf_op jit(solution)/shard_map/ppermute | solution.py:708
  163.2 17.2 %collective-permute-start.30 = (bf16[144,1024]{1,0:T(8,128)(2,1)S(1)}, bf16[144,1024]{1,0:T(8,128)(2,1)S(1)}, u32[]{:S(2)}, u32[]{:S(2)}) collective-permute-start(bf16[144,1024]{1,0:T(8,128)(2,1)S(1)} %fusion.8), channel_id=1, source_target_pairs={{0,16},{4,20},{16,24},{20,28},{24,8},{28,12},{8,0},{12,4},{1,17},{... | collective-permute-start | bytes 884744 | tf_op jit(solution)/shard_map/ppermute | solution.py:708
  164.1 18.2 %collective-permute-start.27 = (bf16[128,1024]{1,0:T(8,128)(2,1)S(1)}, bf16[128,1024]{1,0:T(8,128)(2,1)S(1)}, u32[]{:S(2)}, u32[]{:S(2)}) collective-permute-start(bf16[128,1024]{1,0:T(8,128)(2,1)S(1)} %get-tuple-element.149), channel_id=1, source_target_pairs={{0,3},{1,2},{2,1},{3,0},{4,7},{5,6},{6,5},{7,4},{8,11},{9,10},{10,... | collective-permute-start | bytes 786440 | tf_op jit(solution)/shard_map/ppermute | solution.py:52
  165.5 16.9 %collective-permute-start.26 = (bf16[128,1024]{1,0:T(8,128)(2,1)S(1)}, bf16[128,1024]{1,0:T(8,128)(2,1)S(1)}, u32[]{:S(2)}, u32[]{:S(2)}) collective-permute-start(bf16[128,1024]{1,0:T(8,128)(2,1)S(1)} %get-tuple-element.147), channel_id=1, source_target_pairs={{0,2},{1,3},{2,0},{3,1},{4,6},{5,7},{6,4},{7,5},{8,10},{9,11},{10,... | collective-permute-start | bytes 786440 | tf_op jit(solution)/shard_map/ppermute | solution.py:52
  166.9 15.5 %collective-permute-start.25 = (bf16[128,1024]{1,0:T(8,128)(2,1)S(1)}, bf16[128,1024]{1,0:T(8,128)(2,1)S(1)}, u32[]{:S(2)}, u32[]{:S(2)}) collective-permute-start(bf16[128,1024]{1,0:T(8,128)(2,1)S(1)} %get-tuple-element.145), channel_id=1, source_target_pairs={{0,1},{1,0},{2,3},{3,2},{4,5},{5,4},{6,7},{7,6},{8,9},{9,8},{10,11... | collective-permute-start | bytes 786440 | tf_op jit(solution)/shard_map/ppermute | solution.py:52
  176.0 30.9 %all-to-all-start.2 = ((bf16[4,256,1024]{2,1,0:T(8,128)(2,1)}), bf16[4,256,1024]{2,1,0:T(8,128)(2,1)}, u32[]{:S(2)}, u32[]{:S(2)}) async-start(bf16[4,256,1024]{2,1,0:T(8,128)(2,1)} %share_feed.1), calls=%async_computation.2 | async-start | bytes 4194304 | tf_op jit(solution)/shard_map/all_to_all | solution.py:732
  183.1 8.5 %collective-permute-start.32 = (bf16[144,1024]{1,0:T(8,128)(2,1)}, bf16[144,1024]{1,0:T(8,128)(2,1)S(1)}, u32[]{:S(2)}, u32[]{:S(2)}) collective-permute-start(bf16[144,1024]{1,0:T(8,128)(2,1)} %fusion.3), channel_id=1, source_target_pairs={{0,16},{4,20},{16,24},{20,28},{24,8},{28,12},{8,0},{12,4},{1,17},{... | collective-permute-start | bytes 884744 | tf_op jit(solution)/shard_map/ppermute | solution.py:708
  188.3 18.6 %copy-start.23 = (s32[6]{0:T(128)S(1)}, s32[6]{0:T(128)}, u32[]{:S(2)}) copy-start(s32[6]{0:T(128)} %stack.27.where) | copy-start | bytes 76
  192.8 8.4 %collective-permute-start.33 = (bf16[144,1024]{1,0:T(8,128)(2,1)S(1)}, bf16[144,1024]{1,0:T(8,128)(2,1)S(1)}, u32[]{:S(2)}, u32[]{:S(2)}) collective-permute-start(bf16[144,1024]{1,0:T(8,128)(2,1)S(1)} %fusion.2), channel_id=1, source_target_pairs={{0,16},{4,20},{16,24},{20,28},{24,8},{28,12},{8,0},{12,4},{1,17},{... | collective-permute-start | bytes 884744 | tf_op jit(solution)/shard_map/ppermute | solution.py:708
  202.3 11.7 %collective-permute-start.36 = (bf16[144,1024]{1,0:T(8,128)(2,1)S(1)}, bf16[144,1024]{1,0:T(8,128)(2,1)S(1)}, u32[]{:S(2)}, u32[]{:S(2)}) collective-permute-start(bf16[144,1024]{1,0:T(8,128)(2,1)S(1)} %fusion.1.s0), channel_id=1, source_target_pairs={{0,3},{1,2},{2,1},{3,0},{4,7},{5,6},{6,5},{7,4},{8,11},{9,10},{10,... | collective-permute-start | bytes 884744 | tf_op jit(solution)/shard_map/ppermute | solution.py:52
  204.6 13.1 %collective-permute-start.35 = (bf16[144,1024]{1,0:T(8,128)(2,1)S(1)}, bf16[144,1024]{1,0:T(8,128)(2,1)S(1)}, u32[]{:S(2)}, u32[]{:S(2)}) collective-permute-start(bf16[144,1024]{1,0:T(8,128)(2,1)S(1)} %fusion.1.s0), channel_id=1, source_target_pairs={{0,2},{1,3},{2,0},{3,1},{4,6},{5,7},{6,4},{7,5},{8,10},{9,11},{10,... | collective-permute-start | bytes 884744 | tf_op jit(solution)/shard_map/ppermute | solution.py:52
  205.1 12.6 %collective-permute-start.34 = (bf16[144,1024]{1,0:T(8,128)(2,1)S(1)}, bf16[144,1024]{1,0:T(8,128)(2,1)S(1)}, u32[]{:S(2)}, u32[]{:S(2)}) collective-permute-start(bf16[144,1024]{1,0:T(8,128)(2,1)S(1)} %fusion.1.s0), channel_id=1, source_target_pairs={{0,1},{1,0},{2,3},{3,2},{4,5},{5,4},{6,7},{7,6},{8,9},{9,8},{10,11... | collective-permute-start | bytes 884744 | tf_op jit(solution)/shard_map/ppermute | solution.py:52
  (29 other events, 98.3 us)

commit v5 on v4

--- a/solution.py
+++ b/solution.py
@@ -396,18 +396,28 @@
     return jax.ShapeDtypeStruct(dims, kind)
 
 
-def call(kernel, where, ins, outs, flops=0, name=None, scratch=(), in_hbm=False, limit=50):
+def place():
+    f, s = lax.axis_index("fsdp"), lax.axis_index("seq")
+    z = f // 2
+    odd = (z ^ (z // 2)) % 2
+    return (f, s, z, z ^ (1 + odd), z ^ 3, z ^ (2 - odd))
+
+
+def call(kernel, ins, outs, flops=0, name=None, scratch=(), in_hbm=False, limit=50):
+    def placed(*refs):
+        kernel(place(), *refs)
+
     in_specs = [spec(pltpu.HBM) if in_hbm else spec() for _ in ins]
     return pl.pallas_call(
-        kernel,
+        placed,
         out_shape=outs,
-        in_specs=[spec(pltpu.SMEM)] + in_specs,
+        in_specs=in_specs,
         out_specs=[spec() for _ in outs],
         scratch_shapes=list(scratch),
         compiler_params=pltpu.CompilerParams(vmem_limit_bytes=limit * 1024 * 1024),
         cost_estimate=pl.CostEstimate(flops=0, bytes_accessed=0, transcendentals=0),
         name=name,
-    )(where, *ins)
+    )(*ins)
 
 
 def at(index, size):
@@ -738,8 +748,8 @@
         out[m] = total
 
 
-def deal_sum(where, x, y, name):
-    (copies,) = call(share, where, [x, y], [shape((4,) + x.shape, bf16)], name=name)
+def deal_sum(x, y, name):
+    (copies,) = call(share, [x, y], [shape((4,) + x.shape, bf16)], name=name)
     return deal(copies)
 
 
@@ -779,10 +789,6 @@
     scale_two,
     out_grad,
 ):
-    f, s = lax.axis_index("fsdp"), lax.axis_index("seq")
-    z = f // 2
-    odd = (z ^ (z // 2)) % 2
-    where = jnp.stack([f, s, z, z ^ (1 + odd), z ^ 3, z ^ (2 - odd)]).astype(jnp.int32)
     vectors = [
         first_gain, first_bias, query_bias, value_bias, output_bias,
         scale_one, second_gain, second_bias, down_bias, scale_two, up_bias,
@@ -793,7 +799,6 @@
 
     first, rows = call(
         prepare_first,
-        where,
         [input_weight, output_weight, tokens, out_grad] + vectors,
         [shape((4, 144, 1024), bf16), shape((256, 1024), bf16)],
         name="prepare_first",
@@ -805,7 +810,6 @@
     first_own = along(first)
     (second,) = call(
         prepare_second,
-        where,
         [up_weight, down_weight],
         [shape((256, 1024), bf16)],
         name="prepare_second",
@@ -816,7 +820,6 @@
     second_1 = step(after(second, first_own, *shared[1:]))
     w_in, w_out_own, vecs = call(
         place_first,
-        where,
         [first_own, swap(after(first_own, second, *shared[1:]), "fsdp", 1)],
         [shape((1024, 768), bf16), shape((1024, 256), bf16), shape((16, 1024), f32)],
         name="place_first",
@@ -825,7 +828,6 @@
     w_out = from_others(w_out_own)
     triple, attended_own, logsum, hidden_one = call(
         attention,
-        where,
         shared + [w_in, vecs, seg_col, seg_row],
         [shape((512, 768), bf16), shape((4, 512, 256), bf16), shape((512, 128), f32), mat],
         name="attention",
@@ -835,7 +837,6 @@
     shares = deal(attended_own)
     attended, hidden_two, own_middle, own_branch = call(
         project,
-        where,
         [shares] + w_out + shared + [vecs],
         [mat, mat, rows_f, rows_f],
         name="project",
@@ -843,7 +844,6 @@
     )
     w_down, act, grad_two, grad_before, up_sums, *partial = call(
         feed,
-        where,
         [hidden_two]
         + both_cores([after(x, shares) for x in (second, second_1, second_2)] + [after(second_3, hidden_two)])
         + shared + [vecs, seg_col],
@@ -854,7 +854,6 @@
     partial = exchange(partial)
     second_mine, second_theirs, two_sums, *two = call(
         feed_weights,
-        where,
         [hidden_two, grad_before, act, grad_two, w_down] + shared + [vecs, seg_col],
         [shape((4, 256, 1024), bf16)] * 2 + [shape((2, 1024), f32)] + [rows_b] * 4,
         name="feed_weights",
@@ -862,7 +861,6 @@
     second_theirs = swap(after(second_theirs, two[0], *partial[1:]), "fsdp", 1)
     grad_middle, mid_sums, *messages = call(
         middle_back,
-        where,
         partial + [own_middle, own_branch, rows, seg_col, vecs] + w_out,
         [rows_f, shape((4, 1024), f32)] + [shape((256, 256), bf16)] * 4,
         name="middle_back",
@@ -876,7 +874,6 @@
     twos = exchange([two[0]] + [after(x, *got[1:]) for x in two[1:]])
     grad_triple, one_sums, *last = call(
         attention_back,
-        where,
         [triple, logsum] + got + [seg_col, seg_row, w_in] + shared,
         [shape((512, 768), bf16), shape((4, 1024), f32)] + [rows_b] * 4,
         flops=20 * 512 * 1024 * 1024,
@@ -884,7 +881,6 @@
     )
     first_mine, first_theirs = call(
         attention_weights,
-        where,
         [hidden_one, grad_triple, attended] + got + [up_sums, two_sums, mid_sums, one_sums],
         [shape((4, 144, 1024), bf16)] * 2,
         flops=20 * 512 * 1024 * 1024,
@@ -897,7 +893,6 @@
     first_added = after(add(step(first_sums[1]), first_sums[2]), second_total, *ones[1:])
     layer_out, tokens_grad = call(
         finish_rows,
-        where,
         ones + twos + [own_middle, grad_middle, rows, vecs],
         [rows_b, rows_b],
         name="finish_rows",
@@ -905,8 +900,7 @@
     )
     grad_up, grad_down = call(
         finish_feed,
-        where,
-        [deal_sum(where, second_total, second_sums[0], "share_feed")],
+        [deal_sum(second_total, second_sums[0], "share_feed")],
         [shape((128, 4096), f32), shape((512, 1024), f32)],
         name="finish_feed",
     )
@@ -915,7 +909,6 @@
     first_share = from_others(add(first_total, first_sums[0]))
     grad_in, grad_out, *small = call(
         finish_attention,
-        where,
         [after(first_share[0], grad_up)] + first_share[1:],
         [shape((128, 3072), f32), rows_f] + [shape((1, 128), f32)] * 10 + [shape((1, 512), f32)],
         name="finish_attention",

time: 221 us -> 217 us (0.982)
  waiting for transfers between devices: 84.6 us -> 88.8 us
  Pallas kernels: 64.9 us -> 61.9 us
  local copies, waits for them, and re-layouts: 14 us -> 11.2 us
    all_to_all x2, waiting for transfers between devices: 9.97 us -> 14.8 us  [deal(): return lax.all_to_all(x, 'seq', split_axis=0, concat_axis=0, tiled=True)]
    pallas_call x14, Pallas kernels: 64.9 us -> 61.9 us  [call(): pl.pallas_call(placed, out_shape=outs, in_specs=in_specs, out_specs=[spec...]
    ppermute x28, waiting for transfers between devices: 52.2 us -> 49.8 us  [swap(): return lax.ppermute(x, axis, [(i, i ^ k) for i in range(count)])]
    unnamed x74 -> x62, local copies, waits for them, and re-layouts: 13.2 us -> 11.1 us
  transfers between devices with their start and end apart: 40 -> 40, of which waited for: 22 -> 21; matrix products, arithmetic and copies ran while one was open for 3% -> 2% of each run, Pallas kernels for 23% -> 22%
where the time goes in v5:
time: 217 us; the launch traced here: 216 us
  waiting for transfers between devices  88.8 us (41%)
  Pallas kernels  61.9 us (29%)
  starting transfers between devices  48.6 us (22%)
  local copies, waits for them, and re-layouts  11.2 us (5%)
  other arithmetic  4.68 us (2%)
    pallas_call x14, Pallas kernels, call(): pl.pallas_call(placed, out_shape=outs, in_specs=in_specs, out_specs=[spec...  61.9 us
    ppermute x28, waiting for transfers between devices, swap(): return lax.ppermute(x, axis, [(i, i ^ k) for i in range(count)])  49.8 us
    ppermute x28, starting transfers between devices, swap(): return lax.ppermute(x, axis, [(i, i ^ k) for i in range(count)])  25.7 us
    ppermute x9, waiting for transfers between devices, step(): lax.ppermute(x, 'fsdp', [(2 * a + c, 2 * b + c) for a, b in pairs for c i...  21.3 us
    all_to_all x2, waiting for transfers between devices, deal(): return lax.all_to_all(x, 'seq', split_axis=0, concat_axis=0, tiled=True)  14.8 us
    unnamed x62, local copies, waits for them, and re-layouts  11.1 us
    all_to_all x2, starting transfers between devices, deal(): return lax.all_to_all(x, 'seq', split_axis=0, concat_axis=0, tiled=True)  8.83 us
    ppermute x9, starting transfers between devices, step(): lax.ppermute(x, 'fsdp', [(2 * a + c, 2 * b + c) for a, b in pairs for c i...  7.63 us
  transfers between devices with their start and end apart: 40, of which 21 were waited for; matrix products, arithmetic and copies ran while one was open for 2% of the time, Pallas kernels for 22%

profile of v5, /device:TPU:0, one launch (start us, length us, event | category | flops | bytes accessed | tf_op | source)
XLA Modules:
  0.0 216.4 jit_solution(8409370533379311668)
XLA Ops:
  0.7 3.0 %prepare_first.1 = (bf16[4,144,1024]{2,1,0:T(8,128)(2,1)}, bf16[256,1024]{1,0:T(8,128)(2,1)}) custom-call(bf16[128,3072]{1,0:T(8,128)(2,1)} %refs_0_.2, bf16[128,1024]{1,0:T(8,128)(2,1)} %refs_1_.2, bf16[128,1024]{1,0:T(8,128)(2,1)} %refs_2_.1, bf16[128,1024]{1,0:T(8,128)(2,1)} %refs_3_.1, bf16[128]{0:T(256)(128)(2,1)} %refs_4_.1, bf16[128]{0:T(256)(128)(2,1)} %refs_5_.1, ...), custom_call_target="tpu_custom_call" | custom-call | tf_op jit(solution)/shard_map/prepare_first/pallas_call | solution.py:411
  3.7 6.5 %all-to-all-start = ((bf16[4,144,1024]{2,1,0:T(8,128)(2,1)}), bf16[4,144,1024]{2,1,0:T(8,128)(2,1)}, u32[]{:S(2)}, u32[]{:S(2)}) async-start(bf16[4,144,1024]{2,1,0:T(8,128)(2,1)} %get-tuple-element.100), calls=%async_computation | async-start | bytes 2359296 | tf_op jit(solution)/shard_map/all_to_all | solution.py:724
  10.2 2.6 %collective-permute-start.2 = (bf16[256,1024]{1,0:T(8,128)(2,1)S(1)}, bf16[256,1024]{1,0:T(8,128)(2,1)}, u32[]{:S(2)}, u32[]{:S(2)}) collective-permute-start(bf16[256,1024]{1,0:T(8,128)(2,1)S(1)} %copy-done), channel_id=1, source_target_pairs={{0,3},{1,2},{2,1},{3,0},{4,7},{5,6},{6,5},{7,4},{8,11},{9,10},{10,... | collective-permute-start | bytes 1572872 | tf_op jit(solution)/shard_map/ppermute | solution.py:52
  13.7 2.1 prepare_second.1.refs_1_
  15.8 10.3 %collective-permute-done.2.refs_3_.refs_8_.refs_12_ = bf16[256,1024]{1,0:T(8,128)(2,1)} collective-permute-done((bf16[256,1024]{1,0:T(8,128)(2,1)S(1)}, bf16[256,1024]{1,0:T(8,128)(2,1)}, u32[]{:S(2)}, u32[]{:S(2)}) %collective-permute-start.2) | collective-permute-done | bytes 524320 | tf_op jit(solution)/shard_map/ppermute | solution.py:52
  26.1 9.7 %collective-permute-done.1.refs_2_.refs_7_.refs_11_ = bf16[256,1024]{1,0:T(8,128)(2,1)} collective-permute-done((bf16[256,1024]{1,0:T(8,128)(2,1)S(1)}, bf16[256,1024]{1,0:T(8,128)(2,1)}, u32[]{:S(2)}, u32[]{:S(2)}) %collective-permute-start.1) | collective-permute-done | bytes 524320 | tf_op jit(solution)/shard_map/ppermute | solution.py:52
  35.9 2.9 %all-to-all-done.refs_0_ = bf16[4,144,1024]{2,1,0:T(8,128)(2,1)} async-done(((bf16[4,144,1024]{2,1,0:T(8,128)(2,1)}), bf16[4,144,1024]{2,1,0:T(8,128)(2,1)}, u32[]{:S(2)}, u32[]{:S(2)}) %all-to-all-start) | async-done | bytes 1179680 | tf_op jit(solution)/shard_map/all_to_all | solution.py:724
  39.0 3.0 %collective-permute-done.3.refs_1_ = bf16[4,144,1024]{2,1,0:T(8,128)(2,1)} collective-permute-done((bf16[4,144,1024]{2,1,0:T(8,128)(2,1)}, bf16[4,144,1024]{2,1,0:T(8,128)(2,1)}, u32[]{:S(2)}, u32[]{:S(2)}) %collective-permute-start.3) | collective-permute-done | bytes 1179680 | tf_op jit(solution)/shard_map/ppermute | solution.py:52
  42.0 3.1 %place_first.1 = (bf16[1024,768]{1,0:T(8,128)(2,1)}, bf16[1024,256]{1,0:T(8,128)(2,1)}, f32[16,1024]{1,0:T(8,128)}) custom-call(bf16[4,144,1024]{2,1,0:T(8,128)(2,1)} %all-to-all-done.refs_0_, bf16[4,144,1024]{2,1,0:T(8,128)(2,1)} %collective-permute-done.3.refs_1_), custom_call_target="tpu_custom_call" | custom-call | tf_op jit(solution)/shard_map/place_first/pallas_call | solution.py:411
  45.1 2.6 %collective-permute-start.6 = (bf16[1024,256]{1,0:T(8,128)(2,1)}, bf16[1024,256]{1,0:T(8,128)(2,1)S(1)}, u32[]{:S(2)}, u32[]{:S(2)}) collective-permute-start(bf16[1024,256]{1,0:T(8,128)(2,1)} %get-tuple-element.107.refs_1_.refs_9_), channel_id=1, source_target_pairs={{0,3},{1,2},{2,1},{3,0},{4,7},{5,6},{6,5},{7,4},{8,11},{9,10},{10,... | collective-permute-start | bytes 1572872 | tf_op jit(solution)/shard_map/ppermute | solution.py:52
  49.4 6.9 %attention.1 = (bf16[512,768]{1,0:T(8,128)(2,1)S(1)}, bf16[4,512,256]{2,1,0:T(8,128)(2,1)}, f32[512,128]{1,0:T(8,128)S(1)}, bf16[512,1024]{1,0:T(8,128)(2,1)}) custom-call(bf16[256,1024]{1,0:T(8,128)(2,1)S(1)} %copy-done, bf16[256,1024]{1,0:T(8,128)(2,1)} %collective-permute-done.refs_1_.refs_6_.refs_10_, ...), custom_call_target="tpu_custom_call" | custom-call | tf_op jit(solution)/shard_map/attention/pallas_call | solution.py:411
  57.2 4.4 %all-to-all-start.1 = ((bf16[4,512,256]{2,1,0:T(8,128)(2,1)}), bf16[4,512,256]{2,1,0:T(8,128)(2,1)}, u32[]{:S(2)}, u32[]{:S(2)}) async-start(bf16[4,512,256]{2,1,0:T(8,128)(2,1)} %get-tuple-element.106), calls=%async_computation.1 | async-start | bytes 2097152 | tf_op jit(solution)/shard_map/all_to_all | solution.py:742
  62.4 10.0 %collective-permute-done.5.refs_3_.refs_11_ = bf16[1024,256]{1,0:T(8,128)(2,1)S(1)} collective-permute-done((bf16[1024,256]{1,0:T(8,128)(2,1)}, bf16[1024,256]{1,0:T(8,128)(2,1)S(1)}, u32[]{:S(2)}, u32[]{:S(2)}) %collective-permute-start.5) | collective-permute-done | bytes 524320 | tf_op jit(solution)/shard_map/ppermute | solution.py:52
  73.9 9.0 %all-to-all-done.1.refs_0_ = bf16[4,512,256]{2,1,0:T(8,128)(2,1)} async-done(((bf16[4,512,256]{2,1,0:T(8,128)(2,1)}), bf16[4,512,256]{2,1,0:T(8,128)(2,1)}, u32[]{:S(2)}, u32[]{:S(2)}) %all-to-all-start.1) | async-done | bytes 1048608 | tf_op jit(solution)/shard_map/all_to_all | solution.py:742
  87.6 5.2 %project.1 = (bf16[512,1024]{1,0:T(8,128)(2,1)}, bf16[512,1024]{1,0:T(8,128)(2,1)}, f32[128,1024]{1,0:T(8,128)S(1)}, f32[128,1024]{1,0:T(8,128)S(1)}) custom-call(bf16[4,512,256]{2,1,0:T(8,128)(2,1)} %all-to-all-done.1.refs_0_, bf16[1024,256]{1,0:T(8,128)(2,1)S(1)} %copy-done.6, bf16[1024,256]{1,0:T(8,128)(2,1)S(1)} %copy-done.12, ...), custom_call_target="tpu_custom_call" | custom-call | tf_op jit(solution)/shard_map/project/pallas_call | solution.py:411
  93.4 1.7 collective-permute-done.13.refs_8_
  95.9 8.9 %feed.1 = (bf16[1024,1024]{1,0:T(8,128)(2,1)}, bf16[512,1024]{1,0:T(8,128)(2,1)}, bf16[512,1024]{1,0:T(8,128)(2,1)}, bf16[512,1024]{1,0:T(8,128)(2,1)}, f32[1,10...) custom-call(bf16[512,1024]{1,0:T(8,128)(2,1)} %get-tuple-element.108, ...), custom_call_target="tpu_custom_call" | custom-call | tf_op jit(solution)/shard_map/feed/pallas_call | solution.py:411
  104.8 1.5 collective-permute-start.14
  106.3 1.6 collective-permute-start.15
  108.4 7.9 %feed_weights.1 = (bf16[4,256,1024]{2,1,0:T(8,128)(2,1)}, bf16[4,256,1024]{2,1,0:T(8,128)(2,1)}, f32[2,1024]{1,0:T(2,128)S(1)}, bf16[128,1024]{1,0:T(8,128)(2,1)...) custom-call(bf16[512,1024]{1,0:T(8,128)(2,1)} %get-tuple-element.108.refs_0_, ...), custom_call_target="tpu_custom_call" | custom-call | tf_op jit(solution)/shard_map/feed_weights/pallas_call | solution.py:411
  117.0 3.3 %collective-permute-done.15.refs_2_ = bf16[128,1024]{1,0:T(8,128)(2,1)S(1)} collective-permute-done((bf16[128,1024]{1,0:T(8,128)(2,1)S(1)}, bf16[128,1024]{1,0:T(8,128)(2,1)S(1)}, u32[]{:S(2)}, u32[]{:S(2)}) %collective-permute-start.15) | collective-permute-done | bytes 262176 | tf_op jit(solution)/shard_map/ppermute | solution.py:52
  120.2 3.5 %middle_back.1 = (f32[128,1024]{1,0:T(8,128)S(1)}, f32[4,1024]{1,0:T(4,128)S(1)}, bf16[256,256]{1,0:T(8,128)(2,1)S(1)}, bf16[256,256]{1,0:T(8,128)(2,1)S(1)}, bf...) custom-call(f32[128,1024]{1,0:T(8,128)S(1)} %get-tuple-element.116.refs_0_, ...), custom_call_target="tpu_custom_call" | custom-call | tf_op jit(solution)/shard_map/middle_back/pallas_call | solution.py:411
  125.4 1.7 collective-permute-start.20
  128.9 4.3 %collective-permute-done.20.refs_4_.refs_5_ = bf16[256,256]{1,0:T(8,128)(2,1)S(1)} collective-permute-done((bf16[256,256]{1,0:T(8,128)(2,1)S(1)}, bf16[256,256]{1,0:T(8,128)(2,1)S(1)}, u32[]{:S(2)}, u32[]{:S(2)}) %collective-permute-start.20) | collective-permute-done | bytes 131104 | tf_op jit(solution)/shard_map/ppermute | solution.py:52
  135.0 4.3 %collective-permute-done.18 = bf16[256,1024]{1,0:T(8,128)(2,1)S(1)} collective-permute-done((bf16[256,1024]{1,0:T(8,128)(2,1)S(1)}, bf16[256,1024]{1,0:T(8,128)(2,1)S(1)}, u32[]{:S(2)}, u32[]{:S(2)}) %collective-permute-start.18) | collective-permute-done | bytes 524320 | tf_op jit(solution)/shard_map/ppermute | solution.py:718
  139.5 1.2 collective-permute-start.28
  140.7 1.3 collective-permute-start.22
  142.7 1.5 collective-permute-start.24
  144.2 8.2 %attention_back.1 = (bf16[512,768]{1,0:T(8,128)(2,1)}, f32[4,1024]{1,0:T(4,128)S(1)}, bf16[128,1024]{1,0:T(8,128)(2,1)S(1)}, bf16[128,1024]{1,0:T(8,128)(2,1)S(1...) custom-call(bf16[512,768]{1,0:T(8,128)(2,1)} %copy-done.15, f32[512,128]{1,0:T(8,128)S(1)} %get-tuple-element.105.refs_1_, ...), custom_call_target="tpu_custom_call" | custom-call | tf_op jit(solution)/shard_map/attention_back/pallas_call | solution.py:411
  152.5 1.2 copy-done.16
  153.7 2.7 %attention_weights.1 = (bf16[4,144,1024]{2,1,0:T(8,128)(2,1)}, bf16[4,144,1024]{2,1,0:T(8,128)(2,1)}) custom-call(bf16[512,1024]{1,0:T(8,128)(2,1)S(1)} %copy-done.13, bf16[512,768]{1,0:T(8,128)(2,1)S(1)} %copy-done.16, bf16[512,1024]{1,0:T(8,128)(2,1)S(1)} %copy-done.14, bf16[256,256]{1,0:T(8,128)(2,1)S(1)} %get-tuple-element.136.refs_2_.refs_3_, ...), custom_call_target="tpu_custom_call" | custom-call | tf_op jit(solution)/shard_map/attention_weights/pallas_call | solution.py:411
  157.7 1.9 collective-permute-done.29
  160.6 1.4 collective-permute-start.27
  162.0 1.4 collective-permute-start.26
  164.1 7.5 %collective-permute-done.31.refs_0_ = bf16[256,1024]{1,0:T(8,128)(2,1)S(1)} collective-permute-done((bf16[256,1024]{1,0:T(8,128)(2,1)S(1)}, bf16[256,1024]{1,0:T(8,128)(2,1)S(1)}, u32[]{:S(2)}, u32[]{:S(2)}) %collective-permute-start.31) | collective-permute-done | bytes 524320 | tf_op jit(solution)/shard_map/ppermute | solution.py:718
  171.6 1.5 share_feed.1
  173.1 4.4 %all-to-all-start.2 = ((bf16[4,256,1024]{2,1,0:T(8,128)(2,1)}), bf16[4,256,1024]{2,1,0:T(8,128)(2,1)}, u32[]{:S(2)}, u32[]{:S(2)}) async-start(bf16[4,256,1024]{2,1,0:T(8,128)(2,1)} %share_feed.1), calls=%async_computation.2 | async-start | bytes 4194304 | tf_op jit(solution)/shard_map/all_to_all | solution.py:742
  178.7 1.8 collective-permute-start.32
  180.5 3.5 %finish_rows.1 = (bf16[128,1024]{1,0:T(8,128)(2,1)}, bf16[128,1024]{1,0:T(8,128)(2,1)}) custom-call(bf16[128,1024]{1,0:T(8,128)(2,1)} %copy-done.19, bf16[128,1024]{1,0:T(8,128)(2,1)} %collective-permute-done.25.refs_1_, bf16[128,1024]{1,0:T(8,128)(2,1)} %copy-done.30, bf16[128,1024]{1,0:T(8,128)(2,1)} %copy-done.29, bf16[128,1024]{1,0:T(8,128)(2,1)} %copy-done.18, ...), custom_call_target="tpu_custom_call" | custom-call | tf_op jit(solution)/shard_map/finish_rows/pallas_call | solution.py:411
  184.0 3.4 %collective-permute-done.32 = bf16[144,1024]{1,0:T(8,128)(2,1)S(1)} collective-permute-done((bf16[144,1024]{1,0:T(8,128)(2,1)S(1)}, bf16[144,1024]{1,0:T(8,128)(2,1)S(1)}, u32[]{:S(2)}, u32[]{:S(2)}) %collective-permute-start.32) | collective-permute-done | bytes 294944 | tf_op jit(solution)/shard_map/ppermute | solution.py:718
  188.6 2.7 %collective-permute-start.33 = (bf16[144,1024]{1,0:T(8,128)(2,1)S(1)}, bf16[144,1024]{1,0:T(8,128)(2,1)S(1)}, u32[]{:S(2)}, u32[]{:S(2)}) collective-permute-start(bf16[144,1024]{1,0:T(8,128)(2,1)S(1)} %fusion.2), channel_id=1, source_target_pairs={{0,16},{4,20},{16,24},{20,28},{24,8},{28,12},{8,0},{12,4},{1,17},{... | collective-permute-start | bytes 884744 | tf_op jit(solution)/shard_map/ppermute | solution.py:718
  191.3 6.1 %collective-permute-done.33 = bf16[144,1024]{1,0:T(8,128)(2,1)S(1)} collective-permute-done((bf16[144,1024]{1,0:T(8,128)(2,1)S(1)}, bf16[144,1024]{1,0:T(8,128)(2,1)S(1)}, u32[]{:S(2)}, u32[]{:S(2)}) %collective-permute-start.33) | collective-permute-done | bytes 294944 | tf_op jit(solution)/shard_map/ppermute | solution.py:718
  198.5 1.5 collective-permute-start.36
  200.6 1.5 collective-permute-start.34
  202.1 5.9 %all-to-all-done.2.refs_0_ = bf16[4,256,1024]{2,1,0:T(8,128)(2,1)} async-done(((bf16[4,256,1024]{2,1,0:T(8,128)(2,1)}), bf16[4,256,1024]{2,1,0:T(8,128)(2,1)}, u32[]{:S(2)}, u32[]{:S(2)}) %all-to-all-start.2) | async-done | bytes 2097184 | tf_op jit(solution)/shard_map/all_to_all | solution.py:742
  208.0 3.9 %finish_feed.1 = (f32[128,4096]{1,0:T(8,128)}, f32[512,1024]{1,0:T(8,128)}) custom-call(bf16[4,256,1024]{2,1,0:T(8,128)(2,1)} %all-to-all-done.2.refs_0_), custom_call_target="tpu_custom_call" | custom-call | tf_op jit(solution)/shard_map/finish_feed/pallas_call | solution.py:411
  211.9 2.8 %collective-permute-done.35.refs_2_ = bf16[144,1024]{1,0:T(8,128)(2,1)S(1)} collective-permute-done((bf16[144,1024]{1,0:T(8,128)(2,1)S(1)}, bf16[144,1024]{1,0:T(8,128)(2,1)S(1)}, u32[]{:S(2)}, u32[]{:S(2)}) %collective-permute-start.35) | collective-permute-done | bytes 294944 | tf_op jit(solution)/shard_map/ppermute | solution.py:52
  214.8 1.4 finish_attention.1
  (116 shorter events, 26.6 us)
Async XLA Ops:
  3.7 35.1 %all-to-all-start = ((bf16[4,144,1024]{2,1,0:T(8,128)(2,1)}), bf16[4,144,1024]{2,1,0:T(8,128)(2,1)}, u32[]{:S(2)}, u32[]{:S(2)}) async-start(bf16[4,144,1024]{2,1,0:T(8,128)(2,1)} %get-tuple-element.100), calls=%async_computation | async-start | bytes 2359296 | tf_op jit(solution)/shard_map/all_to_all | solution.py:724
  10.2 28.6 %copy-start.20 = (s32[512]{0:T(512)S(1)}, s32[512]{0:T(512)}, u32[]{:S(2)}) copy-start(s32[512]{0:T(512)} %param.19) | copy-start | bytes 6148
  10.2 15.9 %collective-permute-start.2 = (bf16[256,1024]{1,0:T(8,128)(2,1)S(1)}, bf16[256,1024]{1,0:T(8,128)(2,1)}, u32[]{:S(2)}, u32[]{:S(2)}) collective-permute-start(bf16[256,1024]{1,0:T(8,128)(2,1)S(1)} %copy-done), channel_id=1, source_target_pairs={{0,3},{1,2},{2,1},{3,0},{4,7},{5,6},{6,5},{7,4},{8,11},{9,10},{10,... | collective-permute-start | bytes 1572872 | tf_op jit(solution)/shard_map/ppermute | solution.py:52
  12.8 23.0 %collective-permute-start.1 = (bf16[256,1024]{1,0:T(8,128)(2,1)S(1)}, bf16[256,1024]{1,0:T(8,128)(2,1)}, u32[]{:S(2)}, u32[]{:S(2)}) collective-permute-start(bf16[256,1024]{1,0:T(8,128)(2,1)S(1)} %copy-done), channel_id=1, source_target_pairs={{0,2},{1,3},{2,0},{3,1},{4,6},{5,7},{6,4},{7,5},{8,10},{9,11},{10,... | collective-permute-start | bytes 1572872 | tf_op jit(solution)/shard_map/ppermute | solution.py:52
  13.2 22.7 %collective-permute-start = (bf16[256,1024]{1,0:T(8,128)(2,1)S(1)}, bf16[256,1024]{1,0:T(8,128)(2,1)}, u32[]{:S(2)}, u32[]{:S(2)}) collective-permute-start(bf16[256,1024]{1,0:T(8,128)(2,1)S(1)} %copy-done), channel_id=1, source_target_pairs={{0,1},{1,0},{2,3},{3,2},{4,5},{5,4},{6,7},{7,6},{8,9},{9,8},{10,11... | collective-permute-start | bytes 1572872 | tf_op jit(solution)/shard_map/ppermute | solution.py:52
  38.8 3.2 %collective-permute-start.3 = (bf16[4,144,1024]{2,1,0:T(8,128)(2,1)}, bf16[4,144,1024]{2,1,0:T(8,128)(2,1)}, u32[]{:S(2)}, u32[]{:S(2)}) collective-permute-start(bf16[4,144,1024]{2,1,0:T(8,128)(2,1)} %all-to-all-done.refs_0_), channel_id=1, source_target_pairs={{0,4},{4,0},{8,12},{12,8},{16,20},{20,16},{24,28},{28,24},{1,5},{5... | collective-permute-start | bytes 3538952 | tf_op jit(solution)/shard_map/ppermute | solution.py:52
  38.8 18.3 %collective-permute-start.8 = (bf16[256,1024]{1,0:T(8,128)(2,1)}, bf16[256,1024]{1,0:T(8,128)(2,1)}, u32[]{:S(2)}, u32[]{:S(2)}) collective-permute-start(bf16[256,1024]{1,0:T(8,128)(2,1)} %prepare_second.1.refs_1_), channel_id=1, source_target_pairs={{0,16},{4,20},{16,24},{20,28},{24,8},{28,12},{8,0},{12,4},{1,17},{... | collective-permute-start | bytes 1572872 | tf_op jit(solution)/shard_map/ppermute | solution.py:718
  45.1 16.5 %collective-permute-start.6 = (bf16[1024,256]{1,0:T(8,128)(2,1)}, bf16[1024,256]{1,0:T(8,128)(2,1)S(1)}, u32[]{:S(2)}, u32[]{:S(2)}) collective-permute-start(bf16[1024,256]{1,0:T(8,128)(2,1)} %get-tuple-element.107.refs_1_.refs_9_), channel_id=1, source_target_pairs={{0,3},{1,2},{2,1},{3,0},{4,7},{5,6},{6,5},{7,4},{8,11},{9,10},{10,... | collective-permute-start | bytes 1572872 | tf_op jit(solution)/shard_map/ppermute | solution.py:52
  47.7 24.6 %collective-permute-start.5 = (bf16[1024,256]{1,0:T(8,128)(2,1)}, bf16[1024,256]{1,0:T(8,128)(2,1)S(1)}, u32[]{:S(2)}, u32[]{:S(2)}) collective-permute-start(bf16[1024,256]{1,0:T(8,128)(2,1)} %get-tuple-element.107.refs_1_.refs_9_), channel_id=1, source_target_pairs={{0,2},{1,3},{2,0},{3,1},{4,6},{5,7},{6,4},{7,5},{8,10},{9,11},{10,... | collective-permute-start | bytes 1572872 | tf_op jit(solution)/shard_map/ppermute | solution.py:52
  48.1 25.0 %collective-permute-start.4 = (bf16[1024,256]{1,0:T(8,128)(2,1)}, bf16[1024,256]{1,0:T(8,128)(2,1)S(1)}, u32[]{:S(2)}, u32[]{:S(2)}) collective-permute-start(bf16[1024,256]{1,0:T(8,128)(2,1)} %get-tuple-element.107.refs_1_.refs_9_), channel_id=1, source_target_pairs={{0,1},{1,0},{2,3},{3,2},{4,5},{5,4},{6,7},{7,6},{8,9},{9,8},{10,11... | collective-permute-start | bytes 1572872 | tf_op jit(solution)/shard_map/ppermute | solution.py:52
  57.2 26.2 %copy-start.4 = (f32[16,1024]{1,0:T(8,128)S(1)}, f32[16,1024]{1,0:T(8,128)}, u32[]{:S(2)}) copy-start(f32[16,1024]{1,0:T(8,128)} %get-tuple-element.103.refs_5_.refs_9_.refs_13_.refs_8_.refs_11_) | copy-start | bytes 196612
  57.2 16.8 %collective-permute-start.10 = (bf16[256,1024]{1,0:T(8,128)(2,1)}, bf16[256,1024]{1,0:T(8,128)(2,1)}, u32[]{:S(2)}, u32[]{:S(2)}) collective-permute-start(bf16[256,1024]{1,0:T(8,128)(2,1)} %collective-permute-done.8.refs_3_), channel_id=1, source_target_pairs={{0,16},{4,20},{16,24},{20,28},{24,8},{28,12},{8,0},{12,4},{1,17},{... | collective-permute-start | bytes 1572872 | tf_op jit(solution)/shard_map/ppermute | solution.py:718
  57.2 25.7 %all-to-all-start.1 = ((bf16[4,512,256]{2,1,0:T(8,128)(2,1)}), bf16[4,512,256]{2,1,0:T(8,128)(2,1)}, u32[]{:S(2)}, u32[]{:S(2)}) async-start(bf16[4,512,256]{2,1,0:T(8,128)(2,1)} %get-tuple-element.106), calls=%async_computation.1 | async-start | bytes 2097152 | tf_op jit(solution)/shard_map/all_to_all | solution.py:742
  73.9 18.8 %collective-permute-start.12 = (bf16[256,1024]{1,0:T(8,128)(2,1)}, bf16[256,1024]{1,0:T(8,128)(2,1)}, u32[]{:S(2)}, u32[]{:S(2)}) collective-permute-start(bf16[256,1024]{1,0:T(8,128)(2,1)} %collective-permute-done.10.refs_5_), channel_id=1, source_target_pairs={{0,16},{4,20},{16,24},{20,28},{24,8},{28,12},{8,0},{12,4},{1,17},{... | collective-permute-start | bytes 1572872 | tf_op jit(solution)/shard_map/ppermute | solution.py:718
  82.9 10.5 %collective-permute-start.7 = (bf16[256,1024]{1,0:T(8,128)(2,1)}, bf16[256,1024]{1,0:T(8,128)(2,1)S(1)}, u32[]{:S(2)}, u32[]{:S(2)}) collective-permute-start(bf16[256,1024]{1,0:T(8,128)(2,1)} %prepare_second.1.refs_1_), channel_id=1, source_target_pairs={{0,4},{4,0},{8,12},{12,8},{16,20},{20,16},{24,28},{28,24},{1,5},{5... | collective-permute-start | bytes 1572872 | tf_op jit(solution)/shard_map/ppermute | solution.py:52
  82.9 10.5 %collective-permute-start.9 = (bf16[256,1024]{1,0:T(8,128)(2,1)}, bf16[256,1024]{1,0:T(8,128)(2,1)S(1)}, u32[]{:S(2)}, u32[]{:S(2)}) collective-permute-start(bf16[256,1024]{1,0:T(8,128)(2,1)} %collective-permute-done.8.refs_3_), channel_id=1, source_target_pairs={{0,4},{4,0},{8,12},{12,8},{16,20},{20,16},{24,28},{28,24},{1,5},{5... | collective-permute-start | bytes 1572872 | tf_op jit(solution)/shard_map/ppermute | solution.py:52
  83.4 9.9 %collective-permute-start.11 = (bf16[256,1024]{1,0:T(8,128)(2,1)}, bf16[256,1024]{1,0:T(8,128)(2,1)S(1)}, u32[]{:S(2)}, u32[]{:S(2)}) collective-permute-start(bf16[256,1024]{1,0:T(8,128)(2,1)} %collective-permute-done.10.refs_5_), channel_id=1, source_target_pairs={{0,4},{4,0},{8,12},{12,8},{16,20},{20,16},{24,28},{28,24},{1,5},{5... | collective-permute-start | bytes 1572872 | tf_op jit(solution)/shard_map/ppermute | solution.py:52
  92.8 27.5 %copy-start.5 = (f32[128,1024]{1,0:T(8,128)}, f32[128,1024]{1,0:T(8,128)S(1)}, u32[]{:S(2)}) copy-start(f32[128,1024]{1,0:T(8,128)S(1)} %get-tuple-element.120.refs_4_.refs_8_) | copy-start | bytes 1572868
  92.8 15.6 %copy-start.1 = (bf16[256,1024]{1,0:T(8,128)(2,1)S(1)}, bf16[256,1024]{1,0:T(8,128)(2,1)}, u32[]{:S(2)}) copy-start(bf16[256,1024]{1,0:T(8,128)(2,1)} %get-tuple-element.99.refs_0_.refs_5_.refs_9_.refs_6_.refs_10_) | copy-start | bytes 1572868
  92.8 2.3 %collective-permute-start.13 = (bf16[256,1024]{1,0:T(8,128)(2,1)}, bf16[256,1024]{1,0:T(8,128)(2,1)S(1)}, u32[]{:S(2)}, u32[]{:S(2)}) collective-permute-start(bf16[256,1024]{1,0:T(8,128)(2,1)} %collective-permute-done.12.refs_7_), channel_id=1, source_target_pairs={{0,4},{4,0},{8,12},{12,8},{16,20},{20,16},{24,28},{28,24},{1,5},{5... | collective-permute-start | bytes 1572872 | tf_op jit(solution)/shard_map/ppermute | solution.py:52
  104.8 12.1 %collective-permute-start.14 = (bf16[128,1024]{1,0:T(8,128)(2,1)S(1)}, bf16[128,1024]{1,0:T(8,128)(2,1)S(1)}, u32[]{:S(2)}, u32[]{:S(2)}) collective-permute-start(bf16[128,1024]{1,0:T(8,128)(2,1)S(1)} %get-tuple-element.117), channel_id=1, source_target_pairs={{0,1},{1,0},{2,3},{3,2},{4,5},{5,4},{6,7},{7,6},{8,9},{9,8},{10,11... | collective-permute-start | bytes 786440 | tf_op jit(solution)/shard_map/ppermute | solution.py:52
  106.3 13.9 %collective-permute-start.15 = (bf16[128,1024]{1,0:T(8,128)(2,1)S(1)}, bf16[128,1024]{1,0:T(8,128)(2,1)S(1)}, u32[]{:S(2)}, u32[]{:S(2)}) collective-permute-start(bf16[128,1024]{1,0:T(8,128)(2,1)S(1)} %get-tuple-element.118), channel_id=1, source_target_pairs={{0,2},{1,3},{2,0},{3,1},{4,6},{5,7},{6,4},{7,5},{8,10},{9,11},{10,... | collective-permute-start | bytes 786440 | tf_op jit(solution)/shard_map/ppermute | solution.py:52
  107.9 12.3 %collective-permute-start.16 = (bf16[128,1024]{1,0:T(8,128)(2,1)S(1)}, bf16[128,1024]{1,0:T(8,128)(2,1)S(1)}, u32[]{:S(2)}, u32[]{:S(2)}) collective-permute-start(bf16[128,1024]{1,0:T(8,128)(2,1)S(1)} %get-tuple-element.119), channel_id=1, source_target_pairs={{0,3},{1,2},{2,1},{3,0},{4,7},{5,6},{6,5},{7,4},{8,11},{9,10},{10,... | collective-permute-start | bytes 786440 | tf_op jit(solution)/shard_map/ppermute | solution.py:52
  120.2 4.4 %collective-permute-start.17 = (bf16[4,256,1024]{2,1,0:T(8,128)(2,1)}, bf16[4,256,1024]{2,1,0:T(8,128)(2,1)S(1)}, u32[]{:S(2)}, u32[]{:S(2)}) collective-permute-start(bf16[4,256,1024]{2,1,0:T(8,128)(2,1)} %get-tuple-element.132), channel_id=1, source_target_pairs={{0,4},{4,0},{8,12},{12,8},{16,20},{20,16},{24,28},{28,24},{1,5},{5... | collective-permute-start | bytes 6291464 | tf_op jit(solution)/shard_map/ppermute | solution.py:52
  125.3 19.0 %copy-start.2 = (bf16[256,1024]{1,0:T(8,128)(2,1)S(1)}, bf16[256,1024]{1,0:T(8,128)(2,1)}, u32[]{:S(2)}) copy-start(bf16[256,1024]{1,0:T(8,128)(2,1)} %get-tuple-element.99.refs_0_.refs_5_.refs_9_.refs_6_.refs_10_) | copy-start | bytes 1572868
  125.3 14.0 %collective-permute-start.18 = (bf16[256,1024]{1,0:T(8,128)(2,1)S(1)}, bf16[256,1024]{1,0:T(8,128)(2,1)S(1)}, u32[]{:S(2)}, u32[]{:S(2)}) collective-permute-start(bf16[256,1024]{1,0:T(8,128)(2,1)S(1)} %get-tuple-element.183), channel_id=1, source_target_pairs={{0,16},{4,20},{16,24},{20,28},{24,8},{28,12},{8,0},{12,4},{1,17},{... | collective-permute-start | bytes 1572872 | tf_op jit(solution)/shard_map/ppermute | solution.py:718
  125.4 7.9 %collective-permute-start.20 = (bf16[256,256]{1,0:T(8,128)(2,1)S(1)}, bf16[256,256]{1,0:T(8,128)(2,1)S(1)}, u32[]{:S(2)}, u32[]{:S(2)}) collective-permute-start(bf16[256,256]{1,0:T(8,128)(2,1)S(1)} %get-tuple-element.133), channel_id=1, source_target_pairs={{0,2},{1,3},{2,0},{3,1},{4,6},{5,7},{6,4},{7,5},{8,10},{9,11},{10,... | collective-permute-start | bytes 393224 | tf_op jit(solution)/shard_map/ppermute | solution.py:52
  127.0 7.3 %collective-permute-start.21 = (bf16[256,256]{1,0:T(8,128)(2,1)S(1)}, bf16[256,256]{1,0:T(8,128)(2,1)S(1)}, u32[]{:S(2)}, u32[]{:S(2)}) collective-permute-start(bf16[256,256]{1,0:T(8,128)(2,1)S(1)} %get-tuple-element.134), channel_id=1, source_target_pairs={{0,3},{1,2},{2,1},{3,0},{4,7},{5,6},{6,5},{7,4},{8,11},{9,10},{10,... | collective-permute-start | bytes 393224 | tf_op jit(solution)/shard_map/ppermute | solution.py:52
  128.2 6.8 %collective-permute-start.19 = (bf16[256,256]{1,0:T(8,128)(2,1)S(1)}, bf16[256,256]{1,0:T(8,128)(2,1)S(1)}, u32[]{:S(2)}, u32[]{:S(2)}) collective-permute-start(bf16[256,256]{1,0:T(8,128)(2,1)S(1)} %get-tuple-element.128), channel_id=1, source_target_pairs={{0,1},{1,0},{2,3},{3,2},{4,5},{5,4},{6,7},{7,6},{8,9},{9,8},{10,11... | collective-permute-start | bytes 393224 | tf_op jit(solution)/shard_map/ppermute | solution.py:52
  139.5 17.0 %collective-permute-start.28 = (bf16[256,1024]{1,0:T(8,128)(2,1)S(1)}, bf16[256,1024]{1,0:T(8,128)(2,1)S(1)}, u32[]{:S(2)}, u32[]{:S(2)}) collective-permute-start(bf16[256,1024]{1,0:T(8,128)(2,1)S(1)} %add_convert_fusion.2), channel_id=1, source_target_pairs={{0,16},{4,20},{16,24},{20,28},{24,8},{28,12},{8,0},{12,4},{1,17},{... | collective-permute-start | bytes 1572872 | tf_op jit(solution)/shard_map/ppermute | solution.py:718
  140.7 15.7 %collective-permute-start.22 = (bf16[128,1024]{1,0:T(8,128)(2,1)S(1)}, bf16[128,1024]{1,0:T(8,128)(2,1)S(1)}, u32[]{:S(2)}, u32[]{:S(2)}) collective-permute-start(bf16[128,1024]{1,0:T(8,128)(2,1)S(1)} %get-tuple-element.140), channel_id=1, source_target_pairs={{0,1},{1,0},{2,3},{3,2},{4,5},{5,4},{6,7},{7,6},{8,9},{9,8},{10,11... | collective-permute-start | bytes 786440 | tf_op jit(solution)/shard_map/ppermute | solution.py:52
  142.1 14.4 %collective-permute-start.23 = (bf16[128,1024]{1,0:T(8,128)(2,1)S(1)}, bf16[128,1024]{1,0:T(8,128)(2,1)S(1)}, u32[]{:S(2)}, u32[]{:S(2)}) collective-permute-start(bf16[128,1024]{1,0:T(8,128)(2,1)S(1)} %get-tuple-element.142), channel_id=1, source_target_pairs={{0,2},{1,3},{2,0},{3,1},{4,6},{5,7},{6,4},{7,5},{8,10},{9,11},{10,... | collective-permute-start | bytes 786440 | tf_op jit(solution)/shard_map/ppermute | solution.py:52
  142.7 13.8 %collective-permute-start.24 = (bf16[128,1024]{1,0:T(8,128)(2,1)S(1)}, bf16[128,1024]{1,0:T(8,128)(2,1)S(1)}, u32[]{:S(2)}, u32[]{:S(2)}) collective-permute-start(bf16[128,1024]{1,0:T(8,128)(2,1)S(1)} %get-tuple-element.144), channel_id=1, source_target_pairs={{0,3},{1,2},{2,1},{3,0},{4,7},{5,6},{6,5},{7,4},{8,11},{9,10},{10,... | collective-permute-start | bytes 786440 | tf_op jit(solution)/shard_map/ppermute | solution.py:52
  144.2 8.2 %copy-start.13 = (bf16[512,1024]{1,0:T(8,128)(2,1)S(1)}, bf16[512,1024]{1,0:T(8,128)(2,1)}, u32[]{:S(2)}) copy-start(bf16[512,1024]{1,0:T(8,128)(2,1)} %get-tuple-element.153.refs_0_) | copy-start | bytes 3145732
  144.2 8.2 %copy-start.14 = (bf16[512,1024]{1,0:T(8,128)(2,1)S(1)}, bf16[512,1024]{1,0:T(8,128)(2,1)}, u32[]{:S(2)}) copy-start(bf16[512,1024]{1,0:T(8,128)(2,1)} %get-tuple-element.155.refs_2_) | copy-start | bytes 3145732
  156.5 3.1 %collective-permute-start.29 = (bf16[4,144,1024]{2,1,0:T(8,128)(2,1)}, bf16[4,144,1024]{2,1,0:T(8,128)(2,1)S(1)}, u32[]{:S(2)}, u32[]{:S(2)}) collective-permute-start(bf16[4,144,1024]{2,1,0:T(8,128)(2,1)} %get-tuple-element.162), channel_id=1, source_target_pairs={{0,4},{4,0},{8,12},{12,8},{16,20},{20,16},{24,28},{28,24},{1,5},{5... | collective-permute-start | bytes 3538952 | tf_op jit(solution)/shard_map/ppermute | solution.py:52
  156.8 14.8 %collective-permute-start.31 = (bf16[256,1024]{1,0:T(8,128)(2,1)S(1)}, bf16[256,1024]{1,0:T(8,128)(2,1)S(1)}, u32[]{:S(2)}, u32[]{:S(2)}) collective-permute-start(bf16[256,1024]{1,0:T(8,128)(2,1)S(1)} %fusion), channel_id=1, source_target_pairs={{0,16},{4,20},{16,24},{20,28},{24,8},{28,12},{8,0},{12,4},{1,17},{... | collective-permute-start | bytes 1572872 | tf_op jit(solution)/shard_map/ppermute | solution.py:718
  159.6 12.0 %copy-start.23 = (bf16[4,144,1024]{2,1,0:T(8,128)(2,1)}, bf16[4,144,1024]{2,1,0:T(8,128)(2,1)S(1)}, u32[]{:S(2)}) copy-start(bf16[4,144,1024]{2,1,0:T(8,128)(2,1)S(1)} %collective-permute-done.29) | copy-start | bytes 3538948
  159.7 17.8 %collective-permute-start.30 = (bf16[144,1024]{1,0:T(8,128)(2,1)S(1)}, bf16[144,1024]{1,0:T(8,128)(2,1)S(1)}, u32[]{:S(2)}, u32[]{:S(2)}) collective-permute-start(bf16[144,1024]{1,0:T(8,128)(2,1)S(1)} %fusion.8), channel_id=1, source_target_pairs={{0,16},{4,20},{16,24},{20,28},{24,8},{28,12},{8,0},{12,4},{1,17},{... | collective-permute-start | bytes 884744 | tf_op jit(solution)/shard_map/ppermute | solution.py:718
  160.6 18.0 %collective-permute-start.27 = (bf16[128,1024]{1,0:T(8,128)(2,1)S(1)}, bf16[128,1024]{1,0:T(8,128)(2,1)S(1)}, u32[]{:S(2)}, u32[]{:S(2)}) collective-permute-start(bf16[128,1024]{1,0:T(8,128)(2,1)S(1)} %get-tuple-element.149), channel_id=1, source_target_pairs={{0,3},{1,2},{2,1},{3,0},{4,7},{5,6},{6,5},{7,4},{8,11},{9,10},{10,... | collective-permute-start | bytes 786440 | tf_op jit(solution)/shard_map/ppermute | solution.py:52
  162.0 16.7 %collective-permute-start.26 = (bf16[128,1024]{1,0:T(8,128)(2,1)S(1)}, bf16[128,1024]{1,0:T(8,128)(2,1)S(1)}, u32[]{:S(2)}, u32[]{:S(2)}) collective-permute-start(bf16[128,1024]{1,0:T(8,128)(2,1)S(1)} %get-tuple-element.147), channel_id=1, source_target_pairs={{0,2},{1,3},{2,0},{3,1},{4,6},{5,7},{6,4},{7,5},{8,10},{9,11},{10,... | collective-permute-start | bytes 786440 | tf_op jit(solution)/shard_map/ppermute | solution.py:52
  163.4 15.3 %collective-permute-start.25 = (bf16[128,1024]{1,0:T(8,128)(2,1)S(1)}, bf16[128,1024]{1,0:T(8,128)(2,1)}, u32[]{:S(2)}, u32[]{:S(2)}) collective-permute-start(bf16[128,1024]{1,0:T(8,128)(2,1)S(1)} %get-tuple-element.145), channel_id=1, source_target_pairs={{0,1},{1,0},{2,3},{3,2},{4,5},{5,4},{6,7},{7,6},{8,9},{9,8},{10,11... | collective-permute-start | bytes 786440 | tf_op jit(solution)/shard_map/ppermute | solution.py:52
  173.1 34.9 %all-to-all-start.2 = ((bf16[4,256,1024]{2,1,0:T(8,128)(2,1)}), bf16[4,256,1024]{2,1,0:T(8,128)(2,1)}, u32[]{:S(2)}, u32[]{:S(2)}) async-start(bf16[4,256,1024]{2,1,0:T(8,128)(2,1)} %share_feed.1), calls=%async_computation.2 | async-start | bytes 4194304 | tf_op jit(solution)/shard_map/all_to_all | solution.py:742
  178.7 8.7 %collective-permute-start.32 = (bf16[144,1024]{1,0:T(8,128)(2,1)S(1)}, bf16[144,1024]{1,0:T(8,128)(2,1)S(1)}, u32[]{:S(2)}, u32[]{:S(2)}) collective-permute-start(bf16[144,1024]{1,0:T(8,128)(2,1)S(1)} %fusion.3), channel_id=1, source_target_pairs={{0,16},{4,20},{16,24},{20,28},{24,8},{28,12},{8,0},{12,4},{1,17},{... | collective-permute-start | bytes 884744 | tf_op jit(solution)/shard_map/ppermute | solution.py:718
  188.6 8.8 %collective-permute-start.33 = (bf16[144,1024]{1,0:T(8,128)(2,1)S(1)}, bf16[144,1024]{1,0:T(8,128)(2,1)S(1)}, u32[]{:S(2)}, u32[]{:S(2)}) collective-permute-start(bf16[144,1024]{1,0:T(8,128)(2,1)S(1)} %fusion.2), channel_id=1, source_target_pairs={{0,16},{4,20},{16,24},{20,28},{24,8},{28,12},{8,0},{12,4},{1,17},{... | collective-permute-start | bytes 884744 | tf_op jit(solution)/shard_map/ppermute | solution.py:718
  198.5 13.3 %collective-permute-start.36 = (bf16[144,1024]{1,0:T(8,128)(2,1)S(1)}, bf16[144,1024]{1,0:T(8,128)(2,1)S(1)}, u32[]{:S(2)}, u32[]{:S(2)}) collective-permute-start(bf16[144,1024]{1,0:T(8,128)(2,1)S(1)} %fusion.1.refs_0_), channel_id=1, source_target_pairs={{0,3},{1,2},{2,1},{3,0},{4,7},{5,6},{6,5},{7,4},{8,11},{9,10},{10,... | collective-permute-start | bytes 884744 | tf_op jit(solution)/shard_map/ppermute | solution.py:52
  200.0 14.7 %collective-permute-start.35 = (bf16[144,1024]{1,0:T(8,128)(2,1)S(1)}, bf16[144,1024]{1,0:T(8,128)(2,1)S(1)}, u32[]{:S(2)}, u32[]{:S(2)}) collective-permute-start(bf16[144,1024]{1,0:T(8,128)(2,1)S(1)} %fusion.1.refs_0_), channel_id=1, source_target_pairs={{0,2},{1,3},{2,0},{3,1},{4,6},{5,7},{6,4},{7,5},{8,10},{9,11},{10,... | collective-permute-start | bytes 884744 | tf_op jit(solution)/shard_map/ppermute | solution.py:52
  200.6 14.2 %collective-permute-start.34 = (bf16[144,1024]{1,0:T(8,128)(2,1)S(1)}, bf16[144,1024]{1,0:T(8,128)(2,1)S(1)}, u32[]{:S(2)}, u32[]{:S(2)}) collective-permute-start(bf16[144,1024]{1,0:T(8,128)(2,1)S(1)} %fusion.1.refs_0_), channel_id=1, source_target_pairs={{0,1},{1,0},{2,3},{3,2},{4,5},{5,4},{6,7},{7,6},{8,9},{9,8},{10,11... | collective-permute-start | bytes 884744 | tf_op jit(solution)/shard_map/ppermute | solution.py:52
  (23 other events, 45.4 us)

commit v6 on v5

--- a/solution.py
+++ b/solution.py
@@ -840,6 +840,7 @@
         [shares] + w_out + shared + [vecs],
         [mat, mat, rows_f, rows_f],
         name="project",
+        limit=63,
         scratch=[pltpu.VMEM((512, 1024), f32)],
     )
     w_down, act, grad_two, grad_before, up_sums, *partial = call(

time: 217 us -> 216 us (level)
  local copies, waits for them, and re-layouts: 11.2 us -> 7.43 us
    unnamed x62 -> x54, local copies, waits for them, and re-layouts: 11.1 us -> 7.29 us
  transfers between devices with their start and end apart: 40 -> 40, of which waited for: 21 -> 21; matrix products, arithmetic and copies ran while one was open for 2% -> 2% of each run, Pallas kernels for 22% -> 23%
where the time goes in v6:
time: 216 us
  waiting for transfers between devices  90.4 us (42%)
  Pallas kernels  62.4 us (29%)
  starting transfers between devices  48.7 us (23%)
  local copies, waits for them, and re-layouts  7.43 us (3%)
  other arithmetic  5.63 us (3%)
    pallas_call x14, Pallas kernels, call(): pl.pallas_call(placed, out_shape=outs, in_specs=in_specs, out_specs=[spec...  62.4 us
    ppermute x28, waiting for transfers between devices, swap(): return lax.ppermute(x, axis, [(i, i ^ k) for i in range(count)])  48.9 us
    ppermute x28, starting transfers between devices, swap(): return lax.ppermute(x, axis, [(i, i ^ k) for i in range(count)])  25.7 us
    ppermute x9, waiting for transfers between devices, step(): lax.ppermute(x, 'fsdp', [(2 * a + c, 2 * b + c) for a, b in pairs for c i...  22.4 us
    all_to_all x2, waiting for transfers between devices, deal(): return lax.all_to_all(x, 'seq', split_axis=0, concat_axis=0, tiled=True)  16.3 us
    all_to_all x2, starting transfers between devices, deal(): return lax.all_to_all(x, 'seq', split_axis=0, concat_axis=0, tiled=True)  8.72 us
    ppermute x9, starting transfers between devices, step(): lax.ppermute(x, 'fsdp', [(2 * a + c, 2 * b + c) for a, b in pairs for c i...  7.83 us
    unnamed x54, local copies, waits for them, and re-layouts  7.29 us
  transfers between devices with their start and end apart: 40, of which 21 were waited for; matrix products, arithmetic and copies ran while one was open for 2% of the time, Pallas kernels for 23%

profile of v6, /device:TPU:0, one launch (start us, length us, event | category | flops | bytes accessed | tf_op | source)
XLA Modules:
  0.0 215.7 jit_solution(2832972920920097470)
XLA Ops:
  0.7 3.0 %prepare_first.1 = (bf16[4,144,1024]{2,1,0:T(8,128)(2,1)}, bf16[256,1024]{1,0:T(8,128)(2,1)}) custom-call(bf16[128,3072]{1,0:T(8,128)(2,1)} %refs_0_.2, bf16[128,1024]{1,0:T(8,128)(2,1)} %refs_1_.2, bf16[128,1024]{1,0:T(8,128)(2,1)} %refs_2_.1, bf16[128,1024]{1,0:T(8,128)(2,1)} %refs_3_.1, bf16[128]{0:T(256)(128)(2,1)} %refs_4_.1, bf16[128]{0:T(256)(128)(2,1)} %refs_5_.1, ...), custom_call_target="tpu_custom_call" | custom-call | tf_op jit(solution)/shard_map/prepare_first/pallas_call | solution.py:411
  3.7 6.5 %all-to-all-start = ((bf16[4,144,1024]{2,1,0:T(8,128)(2,1)}), bf16[4,144,1024]{2,1,0:T(8,128)(2,1)}, u32[]{:S(2)}, u32[]{:S(2)}) async-start(bf16[4,144,1024]{2,1,0:T(8,128)(2,1)} %get-tuple-element.100), calls=%async_computation | async-start | bytes 2359296 | tf_op jit(solution)/shard_map/all_to_all | solution.py:724
  10.2 2.6 %collective-permute-start.2 = (bf16[256,1024]{1,0:T(8,128)(2,1)S(1)}, bf16[256,1024]{1,0:T(8,128)(2,1)}, u32[]{:S(2)}, u32[]{:S(2)}) collective-permute-start(bf16[256,1024]{1,0:T(8,128)(2,1)S(1)} %copy-done), channel_id=1, source_target_pairs={{0,3},{1,2},{2,1},{3,0},{4,7},{5,6},{6,5},{7,4},{8,11},{9,10},{10,... | collective-permute-start | bytes 1572872 | tf_op jit(solution)/shard_map/ppermute | solution.py:52
  13.7 2.1 prepare_second.1.refs_1_
  15.8 10.3 %collective-permute-done.2.refs_3_.refs_8_.refs_12_ = bf16[256,1024]{1,0:T(8,128)(2,1)} collective-permute-done((bf16[256,1024]{1,0:T(8,128)(2,1)S(1)}, bf16[256,1024]{1,0:T(8,128)(2,1)}, u32[]{:S(2)}, u32[]{:S(2)}) %collective-permute-start.2) | collective-permute-done | bytes 524320 | tf_op jit(solution)/shard_map/ppermute | solution.py:52
  26.1 9.7 %collective-permute-done.1.refs_2_.refs_7_.refs_11_ = bf16[256,1024]{1,0:T(8,128)(2,1)} collective-permute-done((bf16[256,1024]{1,0:T(8,128)(2,1)S(1)}, bf16[256,1024]{1,0:T(8,128)(2,1)}, u32[]{:S(2)}, u32[]{:S(2)}) %collective-permute-start.1) | collective-permute-done | bytes 524320 | tf_op jit(solution)/shard_map/ppermute | solution.py:52
  35.9 2.9 %all-to-all-done.refs_0_ = bf16[4,144,1024]{2,1,0:T(8,128)(2,1)} async-done(((bf16[4,144,1024]{2,1,0:T(8,128)(2,1)}), bf16[4,144,1024]{2,1,0:T(8,128)(2,1)}, u32[]{:S(2)}, u32[]{:S(2)}) %all-to-all-start) | async-done | bytes 1179680 | tf_op jit(solution)/shard_map/all_to_all | solution.py:724
  39.0 3.0 %collective-permute-done.3.refs_1_ = bf16[4,144,1024]{2,1,0:T(8,128)(2,1)} collective-permute-done((bf16[4,144,1024]{2,1,0:T(8,128)(2,1)}, bf16[4,144,1024]{2,1,0:T(8,128)(2,1)}, u32[]{:S(2)}, u32[]{:S(2)}) %collective-permute-start.3) | collective-permute-done | bytes 1179680 | tf_op jit(solution)/shard_map/ppermute | solution.py:52
  42.0 3.1 %place_first.1 = (bf16[1024,768]{1,0:T(8,128)(2,1)}, bf16[1024,256]{1,0:T(8,128)(2,1)}, f32[16,1024]{1,0:T(8,128)}) custom-call(bf16[4,144,1024]{2,1,0:T(8,128)(2,1)} %all-to-all-done.refs_0_, bf16[4,144,1024]{2,1,0:T(8,128)(2,1)} %collective-permute-done.3.refs_1_), custom_call_target="tpu_custom_call" | custom-call | tf_op jit(solution)/shard_map/place_first/pallas_call | solution.py:411
  45.1 2.6 %collective-permute-start.6 = (bf16[1024,256]{1,0:T(8,128)(2,1)}, bf16[1024,256]{1,0:T(8,128)(2,1)}, u32[]{:S(2)}, u32[]{:S(2)}) collective-permute-start(bf16[1024,256]{1,0:T(8,128)(2,1)} %get-tuple-element.107.refs_1_.refs_9_), channel_id=1, source_target_pairs={{0,3},{1,2},{2,1},{3,0},{4,7},{5,6},{6,5},{7,4},{8,11},{9,10},{10,... | collective-permute-start | bytes 1572872 | tf_op jit(solution)/shard_map/ppermute | solution.py:52
  49.4 6.9 %attention.1 = (bf16[512,768]{1,0:T(8,128)(2,1)S(1)}, bf16[4,512,256]{2,1,0:T(8,128)(2,1)}, f32[512,128]{1,0:T(8,128)S(1)}, bf16[512,1024]{1,0:T(8,128)(2,1)}) custom-call(bf16[256,1024]{1,0:T(8,128)(2,1)S(1)} %copy-done, bf16[256,1024]{1,0:T(8,128)(2,1)} %collective-permute-done.refs_1_.refs_6_.refs_10_, ...), custom_call_target="tpu_custom_call" | custom-call | tf_op jit(solution)/shard_map/attention/pallas_call | solution.py:411
  57.9 4.3 %all-to-all-start.1 = ((bf16[4,512,256]{2,1,0:T(8,128)(2,1)}), bf16[4,512,256]{2,1,0:T(8,128)(2,1)}, u32[]{:S(2)}, u32[]{:S(2)}) async-start(bf16[4,512,256]{2,1,0:T(8,128)(2,1)} %get-tuple-element.106), calls=%async_computation.1 | async-start | bytes 2097152 | tf_op jit(solution)/shard_map/all_to_all | solution.py:742
  62.2 10.2 %collective-permute-done.5.refs_3_.refs_11_ = bf16[1024,256]{1,0:T(8,128)(2,1)} collective-permute-done((bf16[1024,256]{1,0:T(8,128)(2,1)}, bf16[1024,256]{1,0:T(8,128)(2,1)}, u32[]{:S(2)}, u32[]{:S(2)}) %collective-permute-start.5) | collective-permute-done | bytes 524320 | tf_op jit(solution)/shard_map/ppermute | solution.py:52
  72.7 10.2 %all-to-all-done.1.refs_0_ = bf16[4,512,256]{2,1,0:T(8,128)(2,1)} async-done(((bf16[4,512,256]{2,1,0:T(8,128)(2,1)}), bf16[4,512,256]{2,1,0:T(8,128)(2,1)}, u32[]{:S(2)}, u32[]{:S(2)}) %all-to-all-start.1) | async-done | bytes 1048608 | tf_op jit(solution)/shard_map/all_to_all | solution.py:742
  83.4 5.8 %project.1 = (bf16[512,1024]{1,0:T(8,128)(2,1)}, bf16[512,1024]{1,0:T(8,128)(2,1)}, f32[128,1024]{1,0:T(8,128)}, f32[128,1024]{1,0:T(8,128)}) custom-call(bf16[4,512,256]{2,1,0:T(8,128)(2,1)} %all-to-all-done.1.refs_0_, bf16[1024,256]{1,0:T(8,128)(2,1)} %get-tuple-element.107.refs_1_.refs_9_, bf16[1024,256]{1,0:T(8,128)(2,1)} %collective-permute-done.4.refs_2_.refs_10_, ...), custom_call_target="tpu_custom_call" | custom-call | tf_op jit(solution)/shard_map/project/pallas_call | solution.py:411
  89.9 1.7 collective-permute-done.13.refs_8_
  92.4 8.7 %feed.1 = (bf16[1024,1024]{1,0:T(8,128)(2,1)}, bf16[512,1024]{1,0:T(8,128)(2,1)}, bf16[512,1024]{1,0:T(8,128)(2,1)}, bf16[512,1024]{1,0:T(8,128)(2,1)}, f32[1,10...) custom-call(bf16[512,1024]{1,0:T(8,128)(2,1)} %get-tuple-element.108, ...), custom_call_target="tpu_custom_call" | custom-call | tf_op jit(solution)/shard_map/feed/pallas_call | solution.py:411
  101.2 1.5 collective-permute-start.14
  102.7 1.6 collective-permute-start.15
  104.7 8.0 %feed_weights.1 = (bf16[4,256,1024]{2,1,0:T(8,128)(2,1)}, bf16[4,256,1024]{2,1,0:T(8,128)(2,1)}, f32[2,1024]{1,0:T(2,128)S(1)}, bf16[128,1024]{1,0:T(8,128)(2,1)...) custom-call(bf16[512,1024]{1,0:T(8,128)(2,1)} %get-tuple-element.108.refs_0_, ...), custom_call_target="tpu_custom_call" | custom-call | tf_op jit(solution)/shard_map/feed_weights/pallas_call | solution.py:411
  113.5 3.1 %collective-permute-done.15.refs_2_ = bf16[128,1024]{1,0:T(8,128)(2,1)S(1)} collective-permute-done((bf16[128,1024]{1,0:T(8,128)(2,1)S(1)}, bf16[128,1024]{1,0:T(8,128)(2,1)S(1)}, u32[]{:S(2)}, u32[]{:S(2)}) %collective-permute-start.15) | collective-permute-done | bytes 262176 | tf_op jit(solution)/shard_map/ppermute | solution.py:52
  116.6 3.5 %middle_back.1 = (f32[128,1024]{1,0:T(8,128)S(1)}, f32[4,1024]{1,0:T(4,128)S(1)}, bf16[256,256]{1,0:T(8,128)(2,1)S(1)}, bf16[256,256]{1,0:T(8,128)(2,1)S(1)}, bf...) custom-call(f32[128,1024]{1,0:T(8,128)S(1)} %get-tuple-element.116.refs_0_, ...), custom_call_target="tpu_custom_call" | custom-call | tf_op jit(solution)/shard_map/middle_back/pallas_call | solution.py:411
  122.3 1.6 collective-permute-start.20
  125.8 4.3 %collective-permute-done.20.refs_4_.refs_5_ = bf16[256,256]{1,0:T(8,128)(2,1)S(1)} collective-permute-done((bf16[256,256]{1,0:T(8,128)(2,1)S(1)}, bf16[256,256]{1,0:T(8,128)(2,1)S(1)}, u32[]{:S(2)}, u32[]{:S(2)}) %collective-permute-start.20) | collective-permute-done | bytes 131104 | tf_op jit(solution)/shard_map/ppermute | solution.py:52
  131.9 4.4 %collective-permute-done.18 = bf16[256,1024]{1,0:T(8,128)(2,1)S(1)} collective-permute-done((bf16[256,1024]{1,0:T(8,128)(2,1)S(1)}, bf16[256,1024]{1,0:T(8,128)(2,1)S(1)}, u32[]{:S(2)}, u32[]{:S(2)}) %collective-permute-start.18) | collective-permute-done | bytes 524320 | tf_op jit(solution)/shard_map/ppermute | solution.py:718
  136.5 1.2 collective-permute-start.28
  137.7 1.3 collective-permute-start.22
  139.7 1.5 collective-permute-start.24
  141.2 8.2 %attention_back.1 = (bf16[512,768]{1,0:T(8,128)(2,1)}, f32[4,1024]{1,0:T(4,128)S(1)}, bf16[128,1024]{1,0:T(8,128)(2,1)S(1)}, bf16[128,1024]{1,0:T(8,128)(2,1)S(1...) custom-call(bf16[512,768]{1,0:T(8,128)(2,1)} %copy-done.8, f32[512,128]{1,0:T(8,128)S(1)} %copy-done.15, ...), custom_call_target="tpu_custom_call" | custom-call | tf_op jit(solution)/shard_map/attention_back/pallas_call | solution.py:411
  151.3 2.7 %attention_weights.1 = (bf16[4,144,1024]{2,1,0:T(8,128)(2,1)}, bf16[4,144,1024]{2,1,0:T(8,128)(2,1)}) custom-call(bf16[512,1024]{1,0:T(8,128)(2,1)S(1)} %copy-done.6, bf16[512,768]{1,0:T(8,128)(2,1)S(1)} %copy-done.9, bf16[512,1024]{1,0:T(8,128)(2,1)S(1)} %copy-done.7, bf16[256,256]{1,0:T(8,128)(2,1)S(1)} %get-tuple-element.136.refs_2_.refs_3_, ...), custom_call_target="tpu_custom_call" | custom-call | tf_op jit(solution)/shard_map/attention_weights/pallas_call | solution.py:411
  154.8 1.2 fusion
  158.9 1.4 collective-permute-start.27
  160.3 1.4 collective-permute-start.26
  162.3 8.5 %collective-permute-done.31.refs_0_ = bf16[256,1024]{1,0:T(8,128)(2,1)S(1)} collective-permute-done((bf16[256,1024]{1,0:T(8,128)(2,1)S(1)}, bf16[256,1024]{1,0:T(8,128)(2,1)S(1)}, u32[]{:S(2)}, u32[]{:S(2)}) %collective-permute-start.31) | collective-permute-done | bytes 524320 | tf_op jit(solution)/shard_map/ppermute | solution.py:718
  170.8 1.5 share_feed.1
  172.3 4.4 %all-to-all-start.2 = ((bf16[4,256,1024]{2,1,0:T(8,128)(2,1)}), bf16[4,256,1024]{2,1,0:T(8,128)(2,1)}, u32[]{:S(2)}, u32[]{:S(2)}) async-start(bf16[4,256,1024]{2,1,0:T(8,128)(2,1)} %share_feed.1), calls=%async_computation.2 | async-start | bytes 4194304 | tf_op jit(solution)/shard_map/all_to_all | solution.py:742
  177.9 1.8 collective-permute-start.32
  179.7 3.5 %finish_rows.1 = (bf16[128,1024]{1,0:T(8,128)(2,1)}, bf16[128,1024]{1,0:T(8,128)(2,1)}) custom-call(bf16[128,1024]{1,0:T(8,128)(2,1)} %copy-done.13, bf16[128,1024]{1,0:T(8,128)(2,1)} %collective-permute-done.25.refs_1_, bf16[128,1024]{1,0:T(8,128)(2,1)} %collective-permute-done.26.refs_2_, bf16[128,1024]{1,0:T(8,128)(2,1)} %copy-done.26, ...), custom_call_target="tpu_custom_call" | custom-call | tf_op jit(solution)/shard_map/finish_rows/pallas_call | solution.py:411
  183.2 3.4 %collective-permute-done.32 = bf16[144,1024]{1,0:T(8,128)(2,1)S(1)} collective-permute-done((bf16[144,1024]{1,0:T(8,128)(2,1)S(1)}, bf16[144,1024]{1,0:T(8,128)(2,1)S(1)}, u32[]{:S(2)}, u32[]{:S(2)}) %collective-permute-start.32) | collective-permute-done | bytes 294944 | tf_op jit(solution)/shard_map/ppermute | solution.py:718
  186.6 1.2 fusion.2
  187.8 2.7 %collective-permute-start.33 = (bf16[144,1024]{1,0:T(8,128)(2,1)S(1)}, bf16[144,1024]{1,0:T(8,128)(2,1)S(1)}, u32[]{:S(2)}, u32[]{:S(2)}) collective-permute-start(bf16[144,1024]{1,0:T(8,128)(2,1)S(1)} %fusion.2), channel_id=1, source_target_pairs={{0,16},{4,20},{16,24},{20,28},{24,8},{28,12},{8,0},{12,4},{1,17},{... | collective-permute-start | bytes 884744 | tf_op jit(solution)/shard_map/ppermute | solution.py:718
  190.5 6.1 %collective-permute-done.33 = bf16[144,1024]{1,0:T(8,128)(2,1)S(1)} collective-permute-done((bf16[144,1024]{1,0:T(8,128)(2,1)S(1)}, bf16[144,1024]{1,0:T(8,128)(2,1)S(1)}, u32[]{:S(2)}, u32[]{:S(2)}) %collective-permute-start.33) | collective-permute-done | bytes 294944 | tf_op jit(solution)/shard_map/ppermute | solution.py:718
  197.8 1.5 collective-permute-start.36
  199.9 1.5 collective-permute-start.34
  201.3 6.1 %all-to-all-done.2.refs_0_ = bf16[4,256,1024]{2,1,0:T(8,128)(2,1)} async-done(((bf16[4,256,1024]{2,1,0:T(8,128)(2,1)}), bf16[4,256,1024]{2,1,0:T(8,128)(2,1)}, u32[]{:S(2)}, u32[]{:S(2)}) %all-to-all-start.2) | async-done | bytes 2097184 | tf_op jit(solution)/shard_map/all_to_all | solution.py:742
  207.4 3.9 %finish_feed.1 = (f32[128,4096]{1,0:T(8,128)}, f32[512,1024]{1,0:T(8,128)}) custom-call(bf16[4,256,1024]{2,1,0:T(8,128)(2,1)} %all-to-all-done.2.refs_0_), custom_call_target="tpu_custom_call" | custom-call | tf_op jit(solution)/shard_map/finish_feed/pallas_call | solution.py:411
  211.4 2.7 %collective-permute-done.35.refs_2_ = bf16[144,1024]{1,0:T(8,128)(2,1)S(1)} collective-permute-done((bf16[144,1024]{1,0:T(8,128)(2,1)S(1)}, bf16[144,1024]{1,0:T(8,128)(2,1)S(1)}, u32[]{:S(2)}, u32[]{:S(2)}) %collective-permute-start.35) | collective-permute-done | bytes 294944 | tf_op jit(solution)/shard_map/ppermute | solution.py:52
  214.1 1.4 finish_attention.1
  (108 shorter events, 23.6 us)
Async XLA Ops:
  3.7 35.1 %all-to-all-start = ((bf16[4,144,1024]{2,1,0:T(8,128)(2,1)}), bf16[4,144,1024]{2,1,0:T(8,128)(2,1)}, u32[]{:S(2)}, u32[]{:S(2)}) async-start(bf16[4,144,1024]{2,1,0:T(8,128)(2,1)} %get-tuple-element.100), calls=%async_computation | async-start | bytes 2359296 | tf_op jit(solution)/shard_map/all_to_all | solution.py:724
  10.2 28.6 %copy-start.16 = (s32[512]{0:T(512)S(1)}, s32[512]{0:T(512)}, u32[]{:S(2)}) copy-start(s32[512]{0:T(512)} %param.19) | copy-start | bytes 6148
  10.2 15.9 %collective-permute-start.2 = (bf16[256,1024]{1,0:T(8,128)(2,1)S(1)}, bf16[256,1024]{1,0:T(8,128)(2,1)}, u32[]{:S(2)}, u32[]{:S(2)}) collective-permute-start(bf16[256,1024]{1,0:T(8,128)(2,1)S(1)} %copy-done), channel_id=1, source_target_pairs={{0,3},{1,2},{2,1},{3,0},{4,7},{5,6},{6,5},{7,4},{8,11},{9,10},{10,... | collective-permute-start | bytes 1572872 | tf_op jit(solution)/shard_map/ppermute | solution.py:52
  12.8 23.0 %collective-permute-start.1 = (bf16[256,1024]{1,0:T(8,128)(2,1)S(1)}, bf16[256,1024]{1,0:T(8,128)(2,1)}, u32[]{:S(2)}, u32[]{:S(2)}) collective-permute-start(bf16[256,1024]{1,0:T(8,128)(2,1)S(1)} %copy-done), channel_id=1, source_target_pairs={{0,2},{1,3},{2,0},{3,1},{4,6},{5,7},{6,4},{7,5},{8,10},{9,11},{10,... | collective-permute-start | bytes 1572872 | tf_op jit(solution)/shard_map/ppermute | solution.py:52
  13.2 22.7 %collective-permute-start = (bf16[256,1024]{1,0:T(8,128)(2,1)S(1)}, bf16[256,1024]{1,0:T(8,128)(2,1)}, u32[]{:S(2)}, u32[]{:S(2)}) collective-permute-start(bf16[256,1024]{1,0:T(8,128)(2,1)S(1)} %copy-done), channel_id=1, source_target_pairs={{0,1},{1,0},{2,3},{3,2},{4,5},{5,4},{6,7},{7,6},{8,9},{9,8},{10,11... | collective-permute-start | bytes 1572872 | tf_op jit(solution)/shard_map/ppermute | solution.py:52
  38.8 3.2 %collective-permute-start.3 = (bf16[4,144,1024]{2,1,0:T(8,128)(2,1)}, bf16[4,144,1024]{2,1,0:T(8,128)(2,1)}, u32[]{:S(2)}, u32[]{:S(2)}) collective-permute-start(bf16[4,144,1024]{2,1,0:T(8,128)(2,1)} %all-to-all-done.refs_0_), channel_id=1, source_target_pairs={{0,4},{4,0},{8,12},{12,8},{16,20},{20,16},{24,28},{28,24},{1,5},{5... | collective-permute-start | bytes 3538952 | tf_op jit(solution)/shard_map/ppermute | solution.py:52
  38.8 19.1 %collective-permute-start.8 = (bf16[256,1024]{1,0:T(8,128)(2,1)}, bf16[256,1024]{1,0:T(8,128)(2,1)}, u32[]{:S(2)}, u32[]{:S(2)}) collective-permute-start(bf16[256,1024]{1,0:T(8,128)(2,1)} %prepare_second.1.refs_1_), channel_id=1, source_target_pairs={{0,16},{4,20},{16,24},{20,28},{24,8},{28,12},{8,0},{12,4},{1,17},{... | collective-permute-start | bytes 1572872 | tf_op jit(solution)/shard_map/ppermute | solution.py:718
  45.1 17.1 %collective-permute-start.6 = (bf16[1024,256]{1,0:T(8,128)(2,1)}, bf16[1024,256]{1,0:T(8,128)(2,1)}, u32[]{:S(2)}, u32[]{:S(2)}) collective-permute-start(bf16[1024,256]{1,0:T(8,128)(2,1)} %get-tuple-element.107.refs_1_.refs_9_), channel_id=1, source_target_pairs={{0,3},{1,2},{2,1},{3,0},{4,7},{5,6},{6,5},{7,4},{8,11},{9,10},{10,... | collective-permute-start | bytes 1572872 | tf_op jit(solution)/shard_map/ppermute | solution.py:52
  47.7 24.7 %collective-permute-start.5 = (bf16[1024,256]{1,0:T(8,128)(2,1)}, bf16[1024,256]{1,0:T(8,128)(2,1)}, u32[]{:S(2)}, u32[]{:S(2)}) collective-permute-start(bf16[1024,256]{1,0:T(8,128)(2,1)} %get-tuple-element.107.refs_1_.refs_9_), channel_id=1, source_target_pairs={{0,2},{1,3},{2,0},{3,1},{4,6},{5,7},{6,4},{7,5},{8,10},{9,11},{10,... | collective-permute-start | bytes 1572872 | tf_op jit(solution)/shard_map/ppermute | solution.py:52
  48.1 24.3 %collective-permute-start.4 = (bf16[1024,256]{1,0:T(8,128)(2,1)}, bf16[1024,256]{1,0:T(8,128)(2,1)}, u32[]{:S(2)}, u32[]{:S(2)}) collective-permute-start(bf16[1024,256]{1,0:T(8,128)(2,1)} %get-tuple-element.107.refs_1_.refs_9_), channel_id=1, source_target_pairs={{0,1},{1,0},{2,3},{3,2},{4,5},{5,4},{6,7},{7,6},{8,9},{9,8},{10,11... | collective-permute-start | bytes 1572872 | tf_op jit(solution)/shard_map/ppermute | solution.py:52
  57.9 14.6 %collective-permute-start.10 = (bf16[256,1024]{1,0:T(8,128)(2,1)}, bf16[256,1024]{1,0:T(8,128)(2,1)S(1)}, u32[]{:S(2)}, u32[]{:S(2)}) collective-permute-start(bf16[256,1024]{1,0:T(8,128)(2,1)} %collective-permute-done.8.refs_3_), channel_id=1, source_target_pairs={{0,16},{4,20},{16,24},{20,28},{24,8},{28,12},{8,0},{12,4},{1,17},{... | collective-permute-start | bytes 1572872 | tf_op jit(solution)/shard_map/ppermute | solution.py:718
  57.9 25.0 %all-to-all-start.1 = ((bf16[4,512,256]{2,1,0:T(8,128)(2,1)}), bf16[4,512,256]{2,1,0:T(8,128)(2,1)}, u32[]{:S(2)}, u32[]{:S(2)}) async-start(bf16[4,512,256]{2,1,0:T(8,128)(2,1)} %get-tuple-element.106), calls=%async_computation.1 | async-start | bytes 2097152 | tf_op jit(solution)/shard_map/all_to_all | solution.py:742
  62.2 30.3 %copy-start.4 = (f32[16,1024]{1,0:T(8,128)S(1)}, f32[16,1024]{1,0:T(8,128)}, u32[]{:S(2)}) copy-start(f32[16,1024]{1,0:T(8,128)} %get-tuple-element.103.refs_5_.refs_9_.refs_13_.refs_8_.refs_11_) | copy-start | bytes 196612
  72.4 16.8 %copy-start.21 = (bf16[256,1024]{1,0:T(8,128)(2,1)}, bf16[256,1024]{1,0:T(8,128)(2,1)S(1)}, u32[]{:S(2)}) copy-start(bf16[256,1024]{1,0:T(8,128)(2,1)S(1)} %collective-permute-done.10.refs_5_) | copy-start | bytes 1572868
  72.5 16.8 %collective-permute-start.12 = (bf16[256,1024]{1,0:T(8,128)(2,1)S(1)}, bf16[256,1024]{1,0:T(8,128)(2,1)}, u32[]{:S(2)}, u32[]{:S(2)}) collective-permute-start(bf16[256,1024]{1,0:T(8,128)(2,1)S(1)} %collective-permute-done.10.refs_5_), channel_id=1, source_target_pairs={{0,16},{4,20},{16,24},{20,28},{24,8},{28,12},{8,0},{12,4},{1,17},{... | collective-permute-start | bytes 1572872 | tf_op jit(solution)/shard_map/ppermute | solution.py:718
  82.9 7.0 %collective-permute-start.7 = (bf16[256,1024]{1,0:T(8,128)(2,1)}, bf16[256,1024]{1,0:T(8,128)(2,1)}, u32[]{:S(2)}, u32[]{:S(2)}) collective-permute-start(bf16[256,1024]{1,0:T(8,128)(2,1)} %prepare_second.1.refs_1_), channel_id=1, source_target_pairs={{0,4},{4,0},{8,12},{12,8},{16,20},{20,16},{24,28},{28,24},{1,5},{5... | collective-permute-start | bytes 1572872 | tf_op jit(solution)/shard_map/ppermute | solution.py:52
  82.9 7.0 %collective-permute-start.9 = (bf16[256,1024]{1,0:T(8,128)(2,1)}, bf16[256,1024]{1,0:T(8,128)(2,1)}, u32[]{:S(2)}, u32[]{:S(2)}) collective-permute-start(bf16[256,1024]{1,0:T(8,128)(2,1)} %collective-permute-done.8.refs_3_), channel_id=1, source_target_pairs={{0,4},{4,0},{8,12},{12,8},{16,20},{20,16},{24,28},{28,24},{1,5},{5... | collective-permute-start | bytes 1572872 | tf_op jit(solution)/shard_map/ppermute | solution.py:52
  83.4 6.5 %collective-permute-start.11 = (bf16[256,1024]{1,0:T(8,128)(2,1)S(1)}, bf16[256,1024]{1,0:T(8,128)(2,1)}, u32[]{:S(2)}, u32[]{:S(2)}) collective-permute-start(bf16[256,1024]{1,0:T(8,128)(2,1)S(1)} %collective-permute-done.10.refs_5_), channel_id=1, source_target_pairs={{0,4},{4,0},{8,12},{12,8},{16,20},{20,16},{24,28},{28,24},{1,5},{5... | collective-permute-start | bytes 1572872 | tf_op jit(solution)/shard_map/ppermute | solution.py:52
  89.3 15.5 %copy-start.1 = (bf16[256,1024]{1,0:T(8,128)(2,1)S(1)}, bf16[256,1024]{1,0:T(8,128)(2,1)}, u32[]{:S(2)}) copy-start(bf16[256,1024]{1,0:T(8,128)(2,1)} %get-tuple-element.99.refs_0_.refs_5_.refs_9_.refs_6_.refs_10_) | copy-start | bytes 1572868
  89.3 2.3 %collective-permute-start.13 = (bf16[256,1024]{1,0:T(8,128)(2,1)}, bf16[256,1024]{1,0:T(8,128)(2,1)S(1)}, u32[]{:S(2)}, u32[]{:S(2)}) collective-permute-start(bf16[256,1024]{1,0:T(8,128)(2,1)} %collective-permute-done.12.refs_7_), channel_id=1, source_target_pairs={{0,4},{4,0},{8,12},{12,8},{16,20},{20,16},{24,28},{28,24},{1,5},{5... | collective-permute-start | bytes 1572872 | tf_op jit(solution)/shard_map/ppermute | solution.py:52
  101.2 12.3 %collective-permute-start.14 = (bf16[128,1024]{1,0:T(8,128)(2,1)S(1)}, bf16[128,1024]{1,0:T(8,128)(2,1)S(1)}, u32[]{:S(2)}, u32[]{:S(2)}) collective-permute-start(bf16[128,1024]{1,0:T(8,128)(2,1)S(1)} %get-tuple-element.117), channel_id=1, source_target_pairs={{0,1},{1,0},{2,3},{3,2},{4,5},{5,4},{6,7},{7,6},{8,9},{9,8},{10,11... | collective-permute-start | bytes 786440 | tf_op jit(solution)/shard_map/ppermute | solution.py:52
  102.7 13.9 %collective-permute-start.15 = (bf16[128,1024]{1,0:T(8,128)(2,1)S(1)}, bf16[128,1024]{1,0:T(8,128)(2,1)S(1)}, u32[]{:S(2)}, u32[]{:S(2)}) collective-permute-start(bf16[128,1024]{1,0:T(8,128)(2,1)S(1)} %get-tuple-element.118), channel_id=1, source_target_pairs={{0,2},{1,3},{2,0},{3,1},{4,6},{5,7},{6,4},{7,5},{8,10},{9,11},{10,... | collective-permute-start | bytes 786440 | tf_op jit(solution)/shard_map/ppermute | solution.py:52
  104.3 12.3 %collective-permute-start.16 = (bf16[128,1024]{1,0:T(8,128)(2,1)S(1)}, bf16[128,1024]{1,0:T(8,128)(2,1)S(1)}, u32[]{:S(2)}, u32[]{:S(2)}) collective-permute-start(bf16[128,1024]{1,0:T(8,128)(2,1)S(1)} %get-tuple-element.119), channel_id=1, source_target_pairs={{0,3},{1,2},{2,1},{3,0},{4,7},{5,6},{6,5},{7,4},{8,11},{9,10},{10,... | collective-permute-start | bytes 786440 | tf_op jit(solution)/shard_map/ppermute | solution.py:52
  116.6 4.4 %collective-permute-start.17 = (bf16[4,256,1024]{2,1,0:T(8,128)(2,1)}, bf16[4,256,1024]{2,1,0:T(8,128)(2,1)S(1)}, u32[]{:S(2)}, u32[]{:S(2)}) collective-permute-start(bf16[4,256,1024]{2,1,0:T(8,128)(2,1)} %get-tuple-element.132), channel_id=1, source_target_pairs={{0,4},{4,0},{8,12},{12,8},{16,20},{20,16},{24,28},{28,24},{1,5},{5... | collective-permute-start | bytes 6291464 | tf_op jit(solution)/shard_map/ppermute | solution.py:52
  122.3 18.9 %copy-start.2 = (bf16[256,1024]{1,0:T(8,128)(2,1)S(1)}, bf16[256,1024]{1,0:T(8,128)(2,1)}, u32[]{:S(2)}) copy-start(bf16[256,1024]{1,0:T(8,128)(2,1)} %get-tuple-element.99.refs_0_.refs_5_.refs_9_.refs_6_.refs_10_) | copy-start | bytes 1572868
  122.3 18.9 %copy-start.15 = (f32[512,128]{1,0:T(8,128)S(1)}, f32[512,128]{1,0:T(8,128)}, u32[]{:S(2)}) copy-start(f32[512,128]{1,0:T(8,128)} %copy-done.14) | copy-start | bytes 786436
  122.3 14.0 %collective-permute-start.18 = (bf16[256,1024]{1,0:T(8,128)(2,1)S(1)}, bf16[256,1024]{1,0:T(8,128)(2,1)S(1)}, u32[]{:S(2)}, u32[]{:S(2)}) collective-permute-start(bf16[256,1024]{1,0:T(8,128)(2,1)S(1)} %get-tuple-element.183), channel_id=1, source_target_pairs={{0,16},{4,20},{16,24},{20,28},{24,8},{28,12},{8,0},{12,4},{1,17},{... | collective-permute-start | bytes 1572872 | tf_op jit(solution)/shard_map/ppermute | solution.py:718
  122.3 7.8 %collective-permute-start.20 = (bf16[256,256]{1,0:T(8,128)(2,1)S(1)}, bf16[256,256]{1,0:T(8,128)(2,1)S(1)}, u32[]{:S(2)}, u32[]{:S(2)}) collective-permute-start(bf16[256,256]{1,0:T(8,128)(2,1)S(1)} %get-tuple-element.133), channel_id=1, source_target_pairs={{0,2},{1,3},{2,0},{3,1},{4,6},{5,7},{6,4},{7,5},{8,10},{9,11},{10,... | collective-permute-start | bytes 393224 | tf_op jit(solution)/shard_map/ppermute | solution.py:52
  123.9 7.3 %collective-permute-start.21 = (bf16[256,256]{1,0:T(8,128)(2,1)S(1)}, bf16[256,256]{1,0:T(8,128)(2,1)S(1)}, u32[]{:S(2)}, u32[]{:S(2)}) collective-permute-start(bf16[256,256]{1,0:T(8,128)(2,1)S(1)} %get-tuple-element.134), channel_id=1, source_target_pairs={{0,3},{1,2},{2,1},{3,0},{4,7},{5,6},{6,5},{7,4},{8,11},{9,10},{10,... | collective-permute-start | bytes 393224 | tf_op jit(solution)/shard_map/ppermute | solution.py:52
  125.1 6.8 %collective-permute-start.19 = (bf16[256,256]{1,0:T(8,128)(2,1)S(1)}, bf16[256,256]{1,0:T(8,128)(2,1)S(1)}, u32[]{:S(2)}, u32[]{:S(2)}) collective-permute-start(bf16[256,256]{1,0:T(8,128)(2,1)S(1)} %get-tuple-element.128), channel_id=1, source_target_pairs={{0,1},{1,0},{2,3},{3,2},{4,5},{5,4},{6,7},{7,6},{8,9},{9,8},{10,11... | collective-permute-start | bytes 393224 | tf_op jit(solution)/shard_map/ppermute | solution.py:52
  136.5 17.6 %collective-permute-start.28 = (bf16[256,1024]{1,0:T(8,128)(2,1)S(1)}, bf16[256,1024]{1,0:T(8,128)(2,1)S(1)}, u32[]{:S(2)}, u32[]{:S(2)}) collective-permute-start(bf16[256,1024]{1,0:T(8,128)(2,1)S(1)} %add_convert_fusion.2), channel_id=1, source_target_pairs={{0,16},{4,20},{16,24},{20,28},{24,8},{28,12},{8,0},{12,4},{1,17},{... | collective-permute-start | bytes 1572872 | tf_op jit(solution)/shard_map/ppermute | solution.py:718
  137.7 16.3 %collective-permute-start.22 = (bf16[128,1024]{1,0:T(8,128)(2,1)S(1)}, bf16[128,1024]{1,0:T(8,128)(2,1)S(1)}, u32[]{:S(2)}, u32[]{:S(2)}) collective-permute-start(bf16[128,1024]{1,0:T(8,128)(2,1)S(1)} %get-tuple-element.140), channel_id=1, source_target_pairs={{0,1},{1,0},{2,3},{3,2},{4,5},{5,4},{6,7},{7,6},{8,9},{9,8},{10,11... | collective-permute-start | bytes 786440 | tf_op jit(solution)/shard_map/ppermute | solution.py:52
  139.0 15.0 %collective-permute-start.23 = (bf16[128,1024]{1,0:T(8,128)(2,1)S(1)}, bf16[128,1024]{1,0:T(8,128)(2,1)S(1)}, u32[]{:S(2)}, u32[]{:S(2)}) collective-permute-start(bf16[128,1024]{1,0:T(8,128)(2,1)S(1)} %get-tuple-element.142), channel_id=1, source_target_pairs={{0,2},{1,3},{2,0},{3,1},{4,6},{5,7},{6,4},{7,5},{8,10},{9,11},{10,... | collective-permute-start | bytes 786440 | tf_op jit(solution)/shard_map/ppermute | solution.py:52
  139.7 14.3 %collective-permute-start.24 = (bf16[128,1024]{1,0:T(8,128)(2,1)S(1)}, bf16[128,1024]{1,0:T(8,128)(2,1)S(1)}, u32[]{:S(2)}, u32[]{:S(2)}) collective-permute-start(bf16[128,1024]{1,0:T(8,128)(2,1)S(1)} %get-tuple-element.144), channel_id=1, source_target_pairs={{0,3},{1,2},{2,1},{3,0},{4,7},{5,6},{6,5},{7,4},{8,11},{9,10},{10,... | collective-permute-start | bytes 786440 | tf_op jit(solution)/shard_map/ppermute | solution.py:52
  154.0 16.8 %copy-start.25 = (bf16[128,1024]{1,0:T(8,128)(2,1)}, bf16[128,1024]{1,0:T(8,128)(2,1)S(1)}, u32[]{:S(2)}) copy-start(bf16[128,1024]{1,0:T(8,128)(2,1)S(1)} %collective-permute-done.24.refs_7_) | copy-start | bytes 786436
  154.8 3.1 %collective-permute-start.29 = (bf16[4,144,1024]{2,1,0:T(8,128)(2,1)}, bf16[4,144,1024]{2,1,0:T(8,128)(2,1)S(1)}, u32[]{:S(2)}, u32[]{:S(2)}) collective-permute-start(bf16[4,144,1024]{2,1,0:T(8,128)(2,1)} %get-tuple-element.162), channel_id=1, source_target_pairs={{0,4},{4,0},{8,12},{12,8},{16,20},{20,16},{24,28},{28,24},{1,5},{5... | collective-permute-start | bytes 3538952 | tf_op jit(solution)/shard_map/ppermute | solution.py:52
  156.0 14.8 %collective-permute-start.31 = (bf16[256,1024]{1,0:T(8,128)(2,1)S(1)}, bf16[256,1024]{1,0:T(8,128)(2,1)S(1)}, u32[]{:S(2)}, u32[]{:S(2)}) collective-permute-start(bf16[256,1024]{1,0:T(8,128)(2,1)S(1)} %fusion), channel_id=1, source_target_pairs={{0,16},{4,20},{16,24},{20,28},{24,8},{28,12},{8,0},{12,4},{1,17},{... | collective-permute-start | bytes 1572872 | tf_op jit(solution)/shard_map/ppermute | solution.py:718
  157.8 13.0 %copy-start.20 = (bf16[4,144,1024]{2,1,0:T(8,128)(2,1)}, bf16[4,144,1024]{2,1,0:T(8,128)(2,1)S(1)}, u32[]{:S(2)}) copy-start(bf16[4,144,1024]{2,1,0:T(8,128)(2,1)S(1)} %collective-permute-done.29) | copy-start | bytes 3538948
  157.9 18.8 %collective-permute-start.30 = (bf16[144,1024]{1,0:T(8,128)(2,1)S(1)}, bf16[144,1024]{1,0:T(8,128)(2,1)S(1)}, u32[]{:S(2)}, u32[]{:S(2)}) collective-permute-start(bf16[144,1024]{1,0:T(8,128)(2,1)S(1)} %fusion.8), channel_id=1, source_target_pairs={{0,16},{4,20},{16,24},{20,28},{24,8},{28,12},{8,0},{12,4},{1,17},{... | collective-permute-start | bytes 884744 | tf_op jit(solution)/shard_map/ppermute | solution.py:718
  158.9 19.0 %collective-permute-start.27 = (bf16[128,1024]{1,0:T(8,128)(2,1)S(1)}, bf16[128,1024]{1,0:T(8,128)(2,1)S(1)}, u32[]{:S(2)}, u32[]{:S(2)}) collective-permute-start(bf16[128,1024]{1,0:T(8,128)(2,1)S(1)} %get-tuple-element.149), channel_id=1, source_target_pairs={{0,3},{1,2},{2,1},{3,0},{4,7},{5,6},{6,5},{7,4},{8,11},{9,10},{10,... | collective-permute-start | bytes 786440 | tf_op jit(solution)/shard_map/ppermute | solution.py:52
  160.3 17.6 %collective-permute-start.26 = (bf16[128,1024]{1,0:T(8,128)(2,1)S(1)}, bf16[128,1024]{1,0:T(8,128)(2,1)}, u32[]{:S(2)}, u32[]{:S(2)}) collective-permute-start(bf16[128,1024]{1,0:T(8,128)(2,1)S(1)} %get-tuple-element.147), channel_id=1, source_target_pairs={{0,2},{1,3},{2,0},{3,1},{4,6},{5,7},{6,4},{7,5},{8,10},{9,11},{10,... | collective-permute-start | bytes 786440 | tf_op jit(solution)/shard_map/ppermute | solution.py:52
  161.6 16.3 %collective-permute-start.25 = (bf16[128,1024]{1,0:T(8,128)(2,1)S(1)}, bf16[128,1024]{1,0:T(8,128)(2,1)}, u32[]{:S(2)}, u32[]{:S(2)}) collective-permute-start(bf16[128,1024]{1,0:T(8,128)(2,1)S(1)} %get-tuple-element.145), channel_id=1, source_target_pairs={{0,1},{1,0},{2,3},{3,2},{4,5},{5,4},{6,7},{7,6},{8,9},{9,8},{10,11... | collective-permute-start | bytes 786440 | tf_op jit(solution)/shard_map/ppermute | solution.py:52
  172.3 35.1 %all-to-all-start.2 = ((bf16[4,256,1024]{2,1,0:T(8,128)(2,1)}), bf16[4,256,1024]{2,1,0:T(8,128)(2,1)}, u32[]{:S(2)}, u32[]{:S(2)}) async-start(bf16[4,256,1024]{2,1,0:T(8,128)(2,1)} %share_feed.1), calls=%async_computation.2 | async-start | bytes 4194304 | tf_op jit(solution)/shard_map/all_to_all | solution.py:742
  177.9 8.7 %collective-permute-start.32 = (bf16[144,1024]{1,0:T(8,128)(2,1)S(1)}, bf16[144,1024]{1,0:T(8,128)(2,1)S(1)}, u32[]{:S(2)}, u32[]{:S(2)}) collective-permute-start(bf16[144,1024]{1,0:T(8,128)(2,1)S(1)} %fusion.3), channel_id=1, source_target_pairs={{0,16},{4,20},{16,24},{20,28},{24,8},{28,12},{8,0},{12,4},{1,17},{... | collective-permute-start | bytes 884744 | tf_op jit(solution)/shard_map/ppermute | solution.py:718
  187.8 8.8 %collective-permute-start.33 = (bf16[144,1024]{1,0:T(8,128)(2,1)S(1)}, bf16[144,1024]{1,0:T(8,128)(2,1)S(1)}, u32[]{:S(2)}, u32[]{:S(2)}) collective-permute-start(bf16[144,1024]{1,0:T(8,128)(2,1)S(1)} %fusion.2), channel_id=1, source_target_pairs={{0,16},{4,20},{16,24},{20,28},{24,8},{28,12},{8,0},{12,4},{1,17},{... | collective-permute-start | bytes 884744 | tf_op jit(solution)/shard_map/ppermute | solution.py:718
  197.8 13.6 %collective-permute-start.36 = (bf16[144,1024]{1,0:T(8,128)(2,1)S(1)}, bf16[144,1024]{1,0:T(8,128)(2,1)S(1)}, u32[]{:S(2)}, u32[]{:S(2)}) collective-permute-start(bf16[144,1024]{1,0:T(8,128)(2,1)S(1)} %fusion.1.refs_0_), channel_id=1, source_target_pairs={{0,3},{1,2},{2,1},{3,0},{4,7},{5,6},{6,5},{7,4},{8,11},{9,10},{10,... | collective-permute-start | bytes 884744 | tf_op jit(solution)/shard_map/ppermute | solution.py:52
  199.2 14.8 %collective-permute-start.35 = (bf16[144,1024]{1,0:T(8,128)(2,1)S(1)}, bf16[144,1024]{1,0:T(8,128)(2,1)S(1)}, u32[]{:S(2)}, u32[]{:S(2)}) collective-permute-start(bf16[144,1024]{1,0:T(8,128)(2,1)S(1)} %fusion.1.refs_0_), channel_id=1, source_target_pairs={{0,2},{1,3},{2,0},{3,1},{4,6},{5,7},{6,4},{7,5},{8,10},{9,11},{10,... | collective-permute-start | bytes 884744 | tf_op jit(solution)/shard_map/ppermute | solution.py:52
  199.9 14.3 %collective-permute-start.34 = (bf16[144,1024]{1,0:T(8,128)(2,1)S(1)}, bf16[144,1024]{1,0:T(8,128)(2,1)S(1)}, u32[]{:S(2)}, u32[]{:S(2)}) collective-permute-start(bf16[144,1024]{1,0:T(8,128)(2,1)S(1)} %fusion.1.refs_0_), channel_id=1, source_target_pairs={{0,1},{1,0},{2,3},{3,2},{4,5},{5,4},{6,7},{7,6},{8,9},{9,8},{10,11... | collective-permute-start | bytes 884744 | tf_op jit(solution)/shard_map/ppermute | solution.py:52
  (19 other events, 68.3 us)
